TPU v7x, 512 devices: a whole 4x4x16 slice. The times are simulated.
512 devices in a mesh: pts: 128 (over x, z, core), scene: 4 (over y).
Axes of the slice: x: 4, y: 4, z: 16, core: 2. Of those that a mesh axis runs over, the one named last changes fastest.
Arguments:
- points: bfloat16 [4, 16384, 512], P('scene', 'pts'), may hold values from -6 to 6
- cotangent: bfloat16 [4, 16384, 512], P('scene', 'pts'), may hold values from -6 to 6
- valid_counts: int32 [4, 16], P('scene'), may hold values from 256 to 1024, as said below
- zorder_targets: int32 [4, 16384], P('scene', 'pts'), may hold values from 0 to 16383, as said below
- hilbert_sources: int32 [4, 16384], P('scene', 'pts'), may hold values from 0 to 16383, as said below
- zorder_project: bfloat16 [512, 1536], P('pts')
- zorder_output: bfloat16 [512, 512], P('pts'), may hold values from -0.25 to 0.25
- hilbert_project: bfloat16 [512, 1536], P('pts')
- hilbert_output: bfloat16 [512, 512], P('pts'), may hold values from -0.25 to 0.25
Outputs:
- point_grads: bfloat16 [4, 16384, 512], P('scene', 'pts')
- output_grad: float32 [512, 512], P('pts')
Inputs may be any that keep to these rules, and one draw needn't show every extreme that they name: `valid_counts`: every scene has a patch with 1024 valid points and one with 256. `hilbert_sources`: for each scene, a permutation of all blocks; zorder_targets is its inverse. Index u of pts holds Z-order blocks u * 128 to (u + 1) * 128 - 1 and Hilbert positions likewise. The blocks that index u sends to index v number at most 2, and this number depends only on v - u modulo the size of pts; 2 is reached. `zorder_targets`: the inverse permutation of hilbert_sources in each scene.
All inputs are finite; a program needn't handle non-finite values.
Results may differ from a plain program's by a relative error of at most 0.034.
The roundings to bfloat16 on the way count: a program that leaves them out, or rounds other values in their place, can miss the bound.
Values may be sent and summed in bfloat16 or wider, within the bound.
No kernel may reach another device: no remote copies, remote signals or barrier semaphores. Data moves between devices by JAX's collectives and lax.ppermute only.
A program may use at most 64 MiB of HBM per device.

v0:
```python
import functools

import jax
import jax.numpy as jnp
from jax import lax
from jax.experimental import pallas as pl
from jax.experimental.pallas import tpu as pltpu
from jax.sharding import Mesh, PartitionSpec as P

HEADS = 16
PATCH = 1024
WIDTH = 512
HEAD = 32
ROWS = 128
PAIR = 64
MEMBERS = 8
PATCHES = 16
SLOTS = 16
META = 16
SHARE = 4
SCENES = 4
EPSILON = 1e-05
NEGATIVE = -1e30
SCALE = HEAD ** (-0.5)
LOG2E = 1.4426950408889634
QBLOCK = 256

F32 = jnp.float32
BF16 = jnp.bfloat16
PTS = ("x", "zh", "zl", "core")
GROUP = ("zl", "core")
ACROSS = ("x", "zh")


def dot(a, b, ca=1, cb=0):
    return lax.dot_general(a, b, (((ca,), (cb,)), ((), ())), preferred_element_type=F32)


def normalize(values):
    center = values - jnp.mean(values, axis=1, keepdims=True)
    inverse = lax.rsqrt(jnp.mean(center * center, axis=1, keepdims=True) + EPSILON)
    return center * inverse, inverse


def normalize_back(grad, unit, inverse):
    middle = grad - jnp.mean(grad, axis=1, keepdims=True)
    return inverse * (middle - unit * jnp.mean(grad * unit, axis=1, keepdims=True))


def iota(shape, dim):
    return lax.broadcasted_iota(jnp.int32, shape, dim)


def call(kernel, outs, scratch=(), smem=1, count=1):
    def run(*args):
        specs = [pl.BlockSpec(memory_space=pltpu.SMEM)] * smem
        specs += [pl.BlockSpec(memory_space=pltpu.VMEM)] * (len(args) - smem)
        return pl.pallas_call(
            kernel,
            out_shape=[jax.ShapeDtypeStruct(s, d) for s, d in outs],
            in_specs=specs,
            out_specs=[pl.BlockSpec(memory_space=pltpu.VMEM)] * len(outs),
            scratch_shapes=list(scratch),
            compiler_params=pltpu.CompilerParams(vmem_limit_bytes=48 * 1024 * 1024),
        )(*args)

    return run


def softmax_keys(keys, query, mask):
    scores = dot(keys, query, 1, 1) * (SCALE * LOG2E)
    scores = jnp.where(mask, scores, NEGATIVE)
    weights = jnp.exp2(scores - jnp.max(scores, axis=0, keepdims=True))
    return weights * (1.0 / jnp.sum(weights, axis=0, keepdims=True))


def wide(mask_ref):
    mask = mask_ref[...]
    return jnp.concatenate([mask] * (QBLOCK // ROWS), axis=1) > 0.5


def forward_kernel(scal, gathered, weights, qkv, attended, spread, mask_z, mask_h, att):
    member = scal[0]
    limit = scal[2 + scal[1]]
    quarter = member // 2
    query_w = weights[:, : 4 * PAIR]
    keyval_w = weights[:, pl.ds(pl.multiple_of(4 * PAIR + quarter * 2 * PAIR, 2 * PAIR), 2 * PAIR)]
    stride = ROWS + META
    device = iota((ROWS, ROWS), 0)
    total = jnp.zeros((ROWS, ROWS), F32)
    flagged = jnp.zeros((ROWS, ROWS), F32)
    bound = jnp.concatenate(
        [scal[2 + k] - ROWS * iota((MEMBERS, ROWS), 0) for k in range(PATCHES)], axis=0
    ).astype(F32)
    device_f = device.astype(F32)
    for b in range(MEMBERS):
        first = b * stride
        block = gathered[first : first + ROWS, :]
        unit, _ = normalize(block.astype(F32))
        unit = unit.astype(BF16)
        rows = slice(b * ROWS, (b + 1) * ROWS)
        qkv[rows, : 2 * PAIR] = dot(unit, keyval_w).astype(BF16)
        queries = dot(unit, query_w)
        query = queries[:, :PAIR]
        for k in range(1, 4):
            query = jnp.where(quarter == k, queries[:, k * PAIR : (k + 1) * PAIR], query)
        qkv[rows, 2 * PAIR : 3 * PAIR] = query.astype(BF16)
        index = iota((ROWS, ROWS), 0) + ROWS * b
        mask_z[b * ROWS : (b + 1) * ROWS, :] = jnp.where(index < limit, 1.0, 0.0)
        meta = gathered[first + ROWS : first + stride, :].astype(F32)
        owner = meta[0:1, 0:ROWS]
        place = meta[0:1, ROWS : 2 * ROWS]
        hit = device_f == owner
        total += jnp.where(hit, 1.0, 0.0)
        flagged += jnp.where(hit & (place < bound), 1.0, 0.0)
    total = jnp.sum(total, axis=1, keepdims=True)
    flagged = jnp.sum(flagged, axis=1, keepdims=True)
    lane = iota((MEMBERS, ROWS), 1).astype(F32)
    mine = iota((MEMBERS, 1), 0) == member
    slot = iota((SLOTS, ROWS), 0).astype(F32)
    lane_slot = iota((SLOTS, ROWS), 1).astype(F32)
    offset = jnp.zeros((MEMBERS, 1), F32)
    flags = jnp.zeros((MEMBERS, ROWS), F32)
    for k in range(PATCHES):
        here = total[k * MEMBERS : (k + 1) * MEMBERS, :]
        good = flagged[k * MEMBERS : (k + 1) * MEMBERS, :]
        flags += jnp.where((lane >= offset) & (lane < offset + good), 1.0, 0.0)
        own_first = jnp.sum(jnp.where(mine, offset, 0.0), axis=0, keepdims=True)
        own_count = jnp.sum(jnp.where(mine, here, 0.0), axis=0, keepdims=True)
        spread[k * SLOTS : (k + 1) * SLOTS, :] = jnp.where(
            (slot + own_first == lane_slot) & (slot < own_count), 1.0, 0.0
        ).astype(BF16)
        offset += here
    flags = flags.astype(BF16)
    for b in range(MEMBERS):
        pick = jnp.where(iota((MEMBERS, ROWS), 0) == b, 1.0, 0.0).astype(BF16)
        mask_h[b * ROWS : (b + 1) * ROWS, :] = dot(flags, pick, 0, 0)
    mask = wide(mask_z)
    for h in range(2):
        keys = qkv[:, h * HEAD : (h + 1) * HEAD]
        values_t = qkv[:, PAIR + h * HEAD : PAIR + (h + 1) * HEAD].astype(F32).T.astype(BF16)
        for n in range(PATCH // QBLOCK):
            span = slice(n * QBLOCK, (n + 1) * QBLOCK)
            query = qkv[span, 2 * PAIR + h * HEAD : 2 * PAIR + (h + 1) * HEAD]
            probs = softmax_keys(keys, query, mask)
            att[h * HEAD : (h + 1) * HEAD, span] = dot(values_t, probs.astype(BF16))
    for b in range(MEMBERS):
        attended[b] = att[:, b * ROWS : (b + 1) * ROWS].astype(BF16)


def halves(blocks, first, last):
    return [
        jnp.concatenate([blocks[2 * x + c, :, first:last] for x in range(4)], axis=0)
        for c in range(2)
    ]


def mix_kernel(scal, targets_row, targets_col, attended, points, cotangent, output, send, placing):
    patch_row = targets_row[...] // PATCH
    patch_col = targets_col[...] // PATCH
    same = (patch_col == patch_row) & (iota((ROWS, ROWS), 0) < iota((ROWS, ROWS), 1))
    rank = jnp.sum(jnp.where(same, 1.0, 0.0), axis=0, keepdims=True).astype(jnp.int32)
    code = patch_row * SLOTS + rank
    place = jnp.where(iota((PATCHES * SLOTS, ROWS), 0) == code, 1.0, 0.0).astype(BF16)
    placing[...] = place
    weights = halves(output, 0, WIDTH // 2)
    mixed = jnp.concatenate([dot(attended[...], w, 0, 0) for w in weights], axis=1)
    mixed = points[...].astype(F32) + mixed
    send[:, :WIDTH] = dot(place, mixed.astype(BF16)).astype(BF16)
    send[:, WIDTH:] = dot(place, cotangent[...]).astype(BF16)


def project_kernel(scal, arrived, spread, project, output, send, rows, grads):
    gathered = dot(spread[...], arrived[...], 0, 0).astype(BF16)
    mixed = gathered[:, :WIDTH]
    grad = gathered[:, WIDTH:]
    rows[...] = mixed
    grads[...] = grad
    unit, _ = normalize(mixed.astype(F32))
    unit = unit.astype(BF16)
    projected = [dot(unit, w) for w in halves(project, 0, 3 * WIDTH // 2)]
    low, high = halves(output, WIDTH // 2, WIDTH)
    grad_attended = dot(grad[:, : WIDTH // 2], low, 1, 1) + dot(grad[:, WIDTH // 2 :], high, 1, 1)
    for k in range(MEMBERS):
        half, t = projected[k % 2], k // 2
        first = WIDTH // 2 + t * 2 * PAIR
        send[k, :ROWS, :] = half[:, first : first + 2 * PAIR].astype(BF16)
        send[k, ROWS:, :] = jnp.concatenate(
            [half[:, t * PAIR : (t + 1) * PAIR], grad_attended[:, k * PAIR : (k + 1) * PAIR]],
            axis=1,
        ).astype(BF16)


def backward_body(qkv, grad_t, mask, send, attended, dq, dk, dv):
    for h in range(2):
        low, high = h * HEAD, (h + 1) * HEAD
        keys = qkv[:, low:high]
        values = qkv[:, PAIR + low : PAIR + high]
        keys_t = keys.astype(F32).T.astype(BF16)
        values_t = values.astype(F32).T.astype(BF16)
        for n in range(PATCH // QBLOCK):
            span = slice(n * QBLOCK, (n + 1) * QBLOCK)
            query = qkv[span, 2 * PAIR + low : 2 * PAIR + high]
            grad = grad_t[low:high, span]
            probs = softmax_keys(keys, query, mask)
            probs_low = probs.astype(BF16)
            grad_probs = dot(values, grad)
            row_dot = jnp.sum(probs * grad_probs, axis=0, keepdims=True)
            grad_scores = (probs * (grad_probs - row_dot)).astype(BF16)
            dq[low:high, span] = dot(keys_t, grad_scores)
            part_k = dot(grad_scores, query)
            part_v = dot(probs_low, grad, 1, 1)
            if n == 0:
                dk[:, low:high] = part_k
                dv[:, low:high] = part_v
            else:
                dk[:, low:high] += part_k
                dv[:, low:high] += part_v
            if attended is not None:
                attended[low:high, span] = dot(values_t, probs_low).astype(BF16)
    for b in range(MEMBERS):
        rows = slice(b * ROWS, (b + 1) * ROWS)
        send[b, :ROWS, :] = jnp.concatenate([dk[rows, :] * SCALE, dv[rows, :]], axis=1).astype(BF16)
        send[b, ROWS:, :] = (dq[:, rows] * SCALE).astype(BF16)


def backward_h_kernel(scal, arrived, mask_h, send, attended, qkv, grad_t, dq, dk, dv):
    for b in range(MEMBERS):
        rows = slice(b * ROWS, (b + 1) * ROWS)
        qkv[rows, :ROWS] = arrived[b, :ROWS, :]
        both = arrived[b, ROWS:, :]
        qkv[rows, ROWS:] = both
        grad_t[:, rows] = both.astype(F32).T[PAIR:, :].astype(BF16)
    backward_body(qkv, grad_t, wide(mask_h), send, attended, dq, dk, dv)


def backward_z_kernel(scal, arrived, qkv, mask_z, send, grad_t, dq, dk, dv):
    for b in range(MEMBERS):
        grad_t[:, b * ROWS : (b + 1) * ROWS] = arrived[b]
    backward_body(qkv, grad_t, wide(mask_z), send, None, dq, dk, dv)


def input_grad(arrived, weights, swap, rows, grads):
    sides = []
    for c in range(2):
        members = range(c, MEMBERS, 2)
        query_part = jnp.concatenate([arrived[k, ROWS:, :].astype(F32) for k in members], axis=0)
        sides.append(
            jnp.concatenate(
                [query_part.T.astype(BF16)] + [arrived[k, :ROWS, :] for k in members], axis=1
            )
        )
    if swap is not None:
        first, second = sides
        sides = [jnp.where(swap, second, first), jnp.where(swap, first, second)]
    grad_normed = dot(sides[0], weights[0], 1, 1) + dot(sides[1], weights[1], 1, 1)
    unit, inverse = normalize(rows[...].astype(F32))
    return (grads[...].astype(F32) + normalize_back(grad_normed, unit, inverse)).astype(BF16)


def return_kernel(scal, arrived, project, rows, grads, spread, attended, all_grads, send):
    grad = input_grad(arrived, halves(project, 0, 3 * WIDTH // 2), None, rows, grads)
    spaced = dot(spread[...], grad).astype(BF16)
    term = dot(attended[...], all_grads[...])
    upper = term.astype(BF16)
    lower = (term - upper.astype(F32)).astype(BF16)
    for k in range(PATCHES):
        send[k, :SLOTS, :] = spaced[k * SLOTS : (k + 1) * SLOTS, :]
        share = slice(k * SHARE, (k + 1) * SHARE)
        send[k, SLOTS:, :] = jnp.concatenate([upper[share, :], lower[share, :]], axis=0)


def regain_kernel(scal, arrived, placing, output, grad_mixed, send, term):
    spaced = jnp.concatenate([arrived[k, :SLOTS, :] for k in range(PATCHES)], axis=0)
    grad = dot(placing[...], spaced, 0, 0).astype(BF16)
    grad_mixed[...] = grad
    low, high = halves(output, 0, WIDTH // 2)
    grad_attended = dot(low, grad[:, : WIDTH // 2], 1, 1) + dot(high, grad[:, WIDTH // 2 :], 1, 1)
    send[...] = grad_attended.astype(BF16)
    total = jnp.zeros((2 * SHARE, WIDTH), F32)
    for k in range(PATCHES):
        total += arrived[k, SLOTS:, :].astype(F32)
    factor = (SCENES * PATCHES * PATCH) ** (-0.5)
    term[...] = (total[:SHARE, :] + total[SHARE:, :]) * factor


def finish_kernel(scal, arrived, project, other, rows, grads, out):
    weights = [project[...], other[...]]
    out[...] = input_grad(arrived, weights, scal[0] % 2 == 1, rows, grads)


def by_core(project):
    shard = project.shape[0]
    pairs = jnp.transpose(project.reshape(shard, 3, 4, 2, PAIR), (3, 0, 1, 2, 4))
    queries = pairs[:, :, 0].reshape(2, shard, 4 * PAIR)
    both = jnp.stack([pairs[:, :, 1], pairs[:, :, 2]], axis=3).reshape(2, shard, 8 * PAIR)
    return jnp.concatenate([queries, both], axis=2)


def by_half(output):
    return jnp.transpose(output.reshape(output.shape[0], 2, WIDTH // 2), (1, 0, 2))


def exchange(value, axes):
    return lax.all_to_all(value, axes, split_axis=0, concat_axis=0, tiled=True)


def per_device(
    points, cotangent, valid_counts, zorder_targets, hilbert_sources,
    zorder_project, zorder_output, hilbert_project, hilbert_output,
):
    rows = points[0]
    cot = cotangent[0]
    member = lax.axis_index(GROUP).astype(jnp.int32)
    patch = lax.axis_index(ACROSS).astype(jnp.int32)
    scal = jnp.concatenate([jnp.stack([member, patch]), valid_counts[0]])
    targets = zorder_targets[0]
    sources = hilbert_sources[0]

    meta = jnp.concatenate([sources // ROWS, sources % ROWS]).astype(BF16)
    meta = jnp.pad(meta[None], ((0, META - 1), (0, WIDTH - 2 * ROWS)))
    gathered = lax.all_gather(jnp.concatenate([rows, meta], axis=0), GROUP, axis=0, tiled=True)

    weights = jnp.concatenate(
        [by_core(zorder_project), by_core(hilbert_project), by_half(zorder_output), by_half(hilbert_output)],
        axis=2,
    )
    weights = exchange(weights, "core").reshape(MEMBERS, 4 * WIDTH)
    weights = lax.all_gather(weights, ("zh", "zl"), axis=0, tiled=True)
    third = 3 * WIDTH // 2
    project_z = lax.all_gather(weights[:, :third], "x", axis=0, tiled=True)
    outputs = lax.all_gather(weights[:, 2 * third :], ("x", "core"), axis=0, tiled=True)
    outputs = outputs.reshape(MEMBERS, ROWS, WIDTH)
    project_h = lax.all_gather(weights[:, third : 2 * third], ("x", "core"), axis=0, tiled=True)
    project_h = project_h.reshape(MEMBERS, ROWS, third)
    other_z = lax.ppermute(project_z, "core", [(0, 1), (1, 0)])

    qkv_z, attended, spread, mask_z, mask_h = call(
        forward_kernel,
        [
            ((PATCH, 4 * PAIR), BF16),
            ((MEMBERS, PAIR, ROWS), BF16),
            ((PATCHES * SLOTS, ROWS), BF16),
            ((PATCH, ROWS), F32),
            ((PATCH, ROWS), F32),
        ],
        [pltpu.VMEM((PAIR, PATCH), F32)],
    )(scal, gathered, project_z)

    attended = exchange(attended, GROUP).reshape(WIDTH, ROWS)
    send, placing = call(
        mix_kernel,
        [((PATCHES * SLOTS, 2 * WIDTH), BF16), ((PATCHES * SLOTS, ROWS), BF16)],
    )(scal, targets[None, :], targets[:, None], attended, rows, cot, outputs)

    arrived = exchange(send.reshape(PATCHES, SLOTS, 2 * WIDTH), ACROSS)
    send, rows_h, grads_h = call(
        project_kernel,
        [((MEMBERS, 2 * ROWS, ROWS), BF16), ((ROWS, WIDTH), BF16), ((ROWS, WIDTH), BF16)],
    )(scal, arrived.reshape(PATCHES * SLOTS, 2 * WIDTH), spread, project_h, outputs)
    all_grads_h = lax.all_gather(grads_h, GROUP, axis=0, tiled=True)

    arrived = exchange(send, GROUP)
    sums = [
        pltpu.VMEM((PAIR, PATCH), F32),
        pltpu.VMEM((PATCH, PAIR), F32),
        pltpu.VMEM((PATCH, PAIR), F32),
    ]
    send, attended_h = call(
        backward_h_kernel,
        [((MEMBERS, 3 * PAIR, ROWS), BF16), ((PAIR, PATCH), BF16)],
        [pltpu.VMEM((PATCH, 4 * PAIR), BF16), pltpu.VMEM((PAIR, PATCH), BF16)] + sums,
    )(scal, arrived, mask_h)

    arrived = exchange(send, GROUP)
    (send,) = call(return_kernel, [((PATCHES, SLOTS + 2 * SHARE, WIDTH), BF16)])(
        scal, arrived, project_h, rows_h, grads_h, spread, attended_h, all_grads_h
    )

    arrived = exchange(send, ACROSS)
    grad_mixed, send, term = call(
        regain_kernel,
        [((ROWS, WIDTH), BF16), ((WIDTH, ROWS), BF16), ((SHARE, WIDTH), F32)],
    )(scal, arrived, placing, outputs)
    beside = lax.ppermute(term, "scene", [(i, i ^ 1) for i in range(SCENES)])
    arrived = exchange(send.reshape(MEMBERS, PAIR, ROWS), GROUP)
    arrived, beside = lax.optimization_barrier((arrived, beside))
    term = term + beside
    moves = [(r * MEMBERS + j, j * PATCHES + r) for r in range(PATCHES) for j in range(MEMBERS)]
    moved = lax.ppermute(term, PTS, moves)
    crossed = lax.ppermute(
        term,
        PTS + ("scene",),
        [(a * SCENES + i, b * SCENES + (i ^ 2)) for a, b in moves for i in range(SCENES)],
    )

    (send,) = call(
        backward_z_kernel,
        [((MEMBERS, 3 * PAIR, ROWS), BF16)],
        [pltpu.VMEM((PAIR, PATCH), BF16)] + sums,
    )(scal, arrived, qkv_z, mask_z)
    send, moved, crossed = lax.optimization_barrier((send, moved, crossed))

    arrived = exchange(send, GROUP)
    (out,) = call(finish_kernel, [((ROWS, WIDTH), BF16)])(
        scal, arrived, project_z, other_z, rows, grad_mixed
    )

    return out[None], moved + crossed


def solution(mesh):
    devices = mesh.devices.reshape(4, 4, 4, 2, 4)
    fine = Mesh(devices, ("x", "zh", "zl", "core", "scene"))
    rows = P("scene", PTS, None)
    index = P("scene", PTS)
    weight = P(PTS, None)
    return jax.shard_map(
        per_device,
        mesh=fine,
        in_specs=(rows, rows, P("scene", None), index, index, weight, weight, weight, weight),
        out_specs=(rows, weight),
        check_vma=False,
    )
```

profile of v0, /device:TPU:1, one launch (start us, length us, event | category | flops | bytes accessed | tf_op | source)
XLA Modules:
  0.0 300.6 jit_solution(10501036375937398734)
XLA Ops:
  7.2 0.7 fusion.7
  7.9 1.6 pad_maximum_fusion
  9.6 0.8 reshape.66
  10.4 0.1 reshape.67
  10.6 0.8 reshape.68
  11.6 0.1 reshape.69
  11.7 0.7 constant_dynamic-update-slice_fusion.1
  12.4 0.7 constant_dynamic-update-slice_fusion
  13.1 10.3 %all_to_all.40 = bf16[2,4,2048]{2,1,0:T(4,128)(2,1)S(1)} all-to-all(bf16[2,4,2048]{2,1,0:T(4,128)(2,1)S(1)} %constant_dynamic-update-slice_fusion), channel_id=1, replica_groups=mesh['x'=4,'zh'=4,'zl'=4,'core'=2,'scene'=4] {'core'}, dimensions={0} | all-to-all | bytes 65536 | tf_op jit(solution)/shard_map/all_to_all | solution.py:305
  23.4 27.5 %all_gather.19 = bf16[128,2048]{1,0:T(8,128)(2,1)S(1)} all-gather(bf16[8,2048]{1,0:T(8,128)(2,1)S(1)} %reshape.72), channel_id=1, replica_groups=mesh['x'=4,'zh'=4,'zl'=4,'core'=2,'scene'=4] {'zh','zl'}, dimensions={0}, use_global_device_ids=true | all-gather | bytes 557056 | tf_op jit(solution)/shard_map/all_gather | solution.py:329
  51.0 0.7 slice.43
  51.7 0.7 fusion.8
  52.5 12.0 %all_gather.20.weights.project = bf16[512,768]{1,0:T(8,128)(2,1)S(1)} all-gather(bf16[128,768]{1,0:T(8,128)(2,1)S(1)} %get-tuple-element.43), channel_id=1, replica_groups=mesh['x'=4,'zh'=4,'zl'=4,'core'=2,'scene'=4] {'x'}, dimensions={0}, use_global_device_ids=true | all-gather | bytes 983040 | tf_op jit(solution)/shard_map/all_gather | solution.py:331
  64.5 1.3 copy-done.5
  65.8 9.7 %shard_map.104 = (bf16[1024,256]{1,0:T(8,128)(2,1)S(1)}, bf16[8,64,128]{2,1,0:T(8,128)(2,1)}, bf16[256,128]{1,0:T(8,128)(2,1)S(1)}, f32[1024,128]{1,0:T(8,128)S(1)}, f32[1024,128]{1,0:T(8,128)S(1)}) custom-call(s32[18]{0:T(128)S(1)} %pad_add_fusion.scal, bf16[1152,512]{1,0:T(8,128)(2,1)S(1)} %copy-done.5, bf16[512,768]{1,0:T(8,128)(2,1)S(1)} %all_gather.20.weights.project), custom_call_target="tpu_custom_call" | custom-call | tf_op jit(solution)/shard_map/pallas_call | solution.py:58
  75.5 0.8 copy-done.9
  76.3 0.8 copy-done.11
  77.1 0.8 copy-done.14
  77.9 11.2 %all-to-all-start.1 = ((bf16[8,64,128]{2,1,0:T(8,128)(2,1)}), bf16[8,64,128]{2,1,0:T(8,128)(2,1)S(1)}, u32[]{:S(2)}, u32[]{:S(2)}) async-start(bf16[8,64,128]{2,1,0:T(8,128)(2,1)} %get-tuple-element.22), calls=%async_computation.1 | async-start | bytes 262144 | tf_op jit(solution)/shard_map/all_to_all | solution.py:305
  89.1 0.1 copy.19.targets_col
  89.2 1.9 all-gather.7.cloned.1.call-done
  91.1 3.8 %all-to-all-done.1 = bf16[8,64,128]{2,1,0:T(8,128)(2,1)S(1)} async-done(((bf16[8,64,128]{2,1,0:T(8,128)(2,1)}), bf16[8,64,128]{2,1,0:T(8,128)(2,1)S(1)}, u32[]{:S(2)}, u32[]{:S(2)}) %all-to-all-start.1) | async-done | bytes 131104 | tf_op jit(solution)/shard_map/all_to_all | solution.py:305
  95.0 1.2 copy-done
  96.2 1.9 shard_map.105
  98.1 0.6 copy-done.24
  98.7 8.9 %all-to-all-start.2 = ((bf16[16,16,1024]{2,1,0:T(8,128)(2,1)}), bf16[16,16,1024]{2,1,0:T(8,128)(2,1)S(1)}, u32[]{:S(2)}, u32[]{:S(2)}) async-start(bf16[16,16,1024]{2,1,0:T(8,128)(2,1)} %bitcast.18), calls=%async_computation.2 | async-start | bytes 1048576 | tf_op jit(solution)/shard_map/all_to_all | solution.py:305
  107.6 17.9 %all-gather.9.cloned.1.call-done = bf16[1024,768]{1,0:T(8,128)(2,1)} async-done(((bf16[128,768]{1,0:T(8,128)(2,1)}), bf16[1024,768]{1,0:T(8,128)(2,1)}) %all-gather.9.cloned.1.call-update) | async-done | bytes 1572880 | tf_op jit(solution)/shard_map/all_gather | solution.py:334
  125.5 11.4 %all-to-all-done.2 = bf16[16,16,1024]{2,1,0:T(8,128)(2,1)S(1)} async-done(((bf16[16,16,1024]{2,1,0:T(8,128)(2,1)}), bf16[16,16,1024]{2,1,0:T(8,128)(2,1)S(1)}, u32[]{:S(2)}, u32[]{:S(2)}) %all-to-all-start.2) | async-done | bytes 524320 | tf_op jit(solution)/shard_map/all_to_all | solution.py:305
  136.9 1.4 copy-done.2
  138.3 1.5 shard_map.106
  139.8 0.7 copy-done.7
  140.5 0.8 copy-done.13
  141.3 0.7 copy-done.20
  141.9 8.0 %all-to-all-start.3 = ((bf16[8,256,128]{2,1,0:T(8,128)(2,1)}), bf16[8,256,128]{2,1,0:T(8,128)(2,1)}, u32[]{:S(2)}, u32[]{:S(2)}) async-start(bf16[8,256,128]{2,1,0:T(8,128)(2,1)} %copy-done.13), calls=%async_computation.3 | async-start | bytes 1048576 | tf_op jit(solution)/shard_map/all_to_all | solution.py:305
  150.0 0.6 all-gather.11.cloned.1.call-update
  150.5 14.0 %all-to-all-done.3.arrived = bf16[8,256,128]{2,1,0:T(8,128)(2,1)} async-done(((bf16[8,256,128]{2,1,0:T(8,128)(2,1)}), bf16[8,256,128]{2,1,0:T(8,128)(2,1)}, u32[]{:S(2)}, u32[]{:S(2)}) %all-to-all-start.3) | async-done | bytes 524320 | tf_op jit(solution)/shard_map/all_to_all | solution.py:305
  164.6 1.0 copy-done.15
  165.6 12.0 %shard_map.107 = (bf16[8,192,128]{2,1,0:T(8,128)(2,1)S(1)}, bf16[64,1024]{1,0:T(8,128)(2,1)S(1)}) custom-call(s32[18]{0:T(128)S(1)} %pad_add_fusion.scal, bf16[8,256,128]{2,1,0:T(8,128)(2,1)} %all-to-all-done.3.arrived, f32[1024,128]{1,0:T(8,128)S(1)} %copy-done.15), custom_call_target="tpu_custom_call" | custom-call | tf_op jit(solution)/shard_map/pallas_call | solution.py:58
  177.7 0.7 copy-done.16
  178.4 0.7 copy-done.22
  179.1 4.9 %all-to-all-start.4 = ((bf16[8,192,128]{2,1,0:T(8,128)(2,1)}), bf16[8,192,128]{2,1,0:T(8,128)(2,1)}, u32[]{:S(2)}, u32[]{:S(2)}) async-start(bf16[8,192,128]{2,1,0:T(8,128)(2,1)} %copy-done.16), calls=%async_computation.4 | async-start | bytes 786432 | tf_op jit(solution)/shard_map/all_to_all | solution.py:305
  183.9 3.6 %all-gather.11.cloned.1.call-done.all_grads = bf16[1024,512]{1,0:T(8,128)(2,1)} async-done(((bf16[128,512]{1,0:T(8,128)(2,1)}), bf16[1024,512]{1,0:T(8,128)(2,1)}) %all-gather.11.cloned.1.call-update) | async-done | bytes 1048592 | tf_op jit(solution)/shard_map/all_gather | solution.py:361
  187.5 8.4 %all-to-all-done.4.arrived = bf16[8,192,128]{2,1,0:T(8,128)(2,1)} async-done(((bf16[8,192,128]{2,1,0:T(8,128)(2,1)}), bf16[8,192,128]{2,1,0:T(8,128)(2,1)}, u32[]{:S(2)}, u32[]{:S(2)}) %all-to-all-start.4) | async-done | bytes 393248 | tf_op jit(solution)/shard_map/all_to_all | solution.py:305
  195.9 1.2 copy-done.6
  197.1 0.9 copy-done.8
  198.0 0.8 copy-done.18
  198.9 0.9 copy-done.21
  199.8 0.9 copy-done.23
  200.7 2.2 shard_map.108
  202.9 32.4 %all_to_all.41.arrived = bf16[16,24,512]{2,1,0:T(8,128)(2,1)S(1)} all-to-all(bf16[16,24,512]{2,1,0:T(8,128)(2,1)S(1)} %shard_map.108), channel_id=1, replica_groups=mesh['x'=4,'zh'=4,'zl'=4,'core'=2,'scene'=4] {'x','zh'}, dimensions={0} | all-to-all | bytes 786432 | tf_op jit(solution)/shard_map/all_to_all | solution.py:305
  235.2 1.7 shard_map.109
  236.9 6.6 %all-to-all-start.6 = ((bf16[8,64,128]{2,1,0:T(8,128)(2,1)}), bf16[8,64,128]{2,1,0:T(8,128)(2,1)S(1)}, u32[]{:S(2)}, u32[]{:S(2)}) async-start(bf16[8,64,128]{2,1,0:T(8,128)(2,1)} %bitcast.21), calls=%async_computation.6 | async-start | bytes 262144 | tf_op jit(solution)/shard_map/all_to_all | solution.py:305
  243.5 3.1 %collective-permute-start = (f32[4,512]{1,0:T(4,128)S(1)}, f32[4,512]{1,0:T(4,128)S(1)}, u32[]{:S(2)}, u32[]{:S(2)}) collective-permute-start(f32[4,512]{1,0:T(4,128)S(1)} %get-tuple-element.33), channel_id=1, source_target_pairs={{0,1},{1,0},{2,3},{3,2},{4,5},{5,4},{6,7},{7,6},{8,9},{9,8},{10,11... | collective-permute-start | bytes 24584 | tf_op jit(solution)/shard_map/ppermute | solution.py:385
  246.7 1.2 collective-permute-done
  247.9 1.5 all-to-all-done.6.arrived
  249.4 3.5 %collective-permute-start.1 = (f32[4,512]{1,0:T(4,128)S(1)}, f32[4,512]{1,0:T(4,128)S(1)}, u32[]{:S(2)}, u32[]{:S(2)}) collective-permute-start(f32[4,512]{1,0:T(4,128)S(1)} %add.26), channel_id=1, source_target_pairs={{0,0},{4,64},{8,128},{12,192},{16,256},{20,320},{24,384},{28,448},... | collective-permute-start | bytes 24584 | tf_op jit(solution)/shard_map/ppermute | solution.py:390
  252.9 13.7 %collective-permute-start.2 = (f32[4,512]{1,0:T(4,128)S(1)}, f32[4,512]{1,0:T(4,128)S(1)}, u32[]{:S(2)}, u32[]{:S(2)}) collective-permute-start(f32[4,512]{1,0:T(4,128)S(1)} %add.26), channel_id=1, source_target_pairs={{0,2},{1,3},{2,0},{3,1},{4,66},{5,67},{6,64},{7,65},{8,130},{9,131... | collective-permute-start | bytes 24584 | tf_op jit(solution)/shard_map/ppermute | solution.py:391
  266.6 11.0 %shard_map.110 = bf16[8,192,128]{2,1,0:T(8,128)(2,1)} custom-call(s32[18]{0:T(128)S(1)} %pad_add_fusion.scal, bf16[8,64,128]{2,1,0:T(8,128)(2,1)S(1)} %all-to-all-done.6.arrived, bf16[1024,256]{1,0:T(8,128)(2,1)S(1)} %copy-done.10, f32[1024,128]{1,0:T(8,128)S(1)} %copy-done.12), custom_call_target="tpu_custom_call" | custom-call | tf_op jit(solution)/shard_map/pallas_call | solution.py:58
  277.6 3.4 %all-to-all-start.7 = ((bf16[8,192,128]{2,1,0:T(8,128)(2,1)}), bf16[8,192,128]{2,1,0:T(8,128)(2,1)S(1)}, u32[]{:S(2)}, u32[]{:S(2)}) async-start(bf16[8,192,128]{2,1,0:T(8,128)(2,1)} %shard_map.110), calls=%async_computation.7 | async-start | bytes 786432 | tf_op jit(solution)/shard_map/all_to_all | solution.py:305
  281.1 1.9 collective-permute-start.3
  283.0 0.6 add.27
  283.6 1.6 collective-permute-done.3.other
  285.2 6.8 %all-to-all-done.7.arrived = bf16[8,192,128]{2,1,0:T(8,128)(2,1)S(1)} async-done(((bf16[8,192,128]{2,1,0:T(8,128)(2,1)}), bf16[8,192,128]{2,1,0:T(8,128)(2,1)S(1)}, u32[]{:S(2)}, u32[]{:S(2)}) %all-to-all-start.7) | async-done | bytes 393248 | tf_op jit(solution)/shard_map/all_to_all | solution.py:305
  292.1 2.0 shard_map.111
  (66 shorter events, 0.7 us)
Async XLA Ops:
  7.2 45.3 %copy-start.27 = (s32[1,16]{1,0:T(1,128)S(1)}, s32[1,16]{1,0:T(1,128)}, u32[]{:S(2)}) copy-start(s32[1,16]{1,0:T(1,128)} %param.11) | copy-start | bytes 196
  7.2 57.4 %all-gather.5.cloned.1.call-start = ((), (), s32[]{:S(2)}) async-start(), calls=%async_computation.8 | async-start | bytes 1327104 | tf_op jit(solution)/shard_map/all_gather | solution.py:322
  9.5 81.6 %all-gather.7.cloned.1.call-start = ((), (), s32[]{:S(2)}) async-start(), calls=%async_computation.9 | async-start | bytes 1179648 | tf_op jit(solution)/shard_map/all_gather | solution.py:332
  51.7 73.8 %all-gather.9.cloned.1.call-start = ((), (), s32[]{:S(2)}) async-start(), calls=%async_computation.10 | async-start | bytes 1769472 | tf_op jit(solution)/shard_map/all_gather | solution.py:334
  52.5 36.6 %copy-start.26 = (s32[1,128]{1,0:T(1,128)S(1)}, s32[1,128]{1,0:T(1,128)}, u32[]{:S(2)}) copy-start(s32[1,128]{1,0:T(1,128)} %targets_row.1) | copy-start | bytes 1540
  52.5 42.4 %copy-start.4 = (bf16[1,128,512]{2,1,0:T(8,128)(2,1)S(1)}, bf16[1,128,512]{2,1,0:T(8,128)(2,1)}, u32[]{:S(2)}) copy-start(bf16[1,128,512]{2,1,0:T(8,128)(2,1)} %param.9) | copy-start | bytes 393220
  52.5 42.4 %copy-start.19 = (bf16[1,128,512]{2,1,0:T(8,128)(2,1)S(1)}, bf16[1,128,512]{2,1,0:T(8,128)(2,1)}, u32[]{:S(2)}) copy-start(bf16[1,128,512]{2,1,0:T(8,128)(2,1)} %param.10) | copy-start | bytes 393220
  64.5 1.3 copy-start.5
  75.5 0.8 copy-start.9
  76.3 0.8 copy-start.11
  77.1 0.8 copy-start.14
  77.9 59.0 %copy-start.17 = (bf16[256,128]{1,0:T(8,128)(2,1)}, bf16[256,128]{1,0:T(8,128)(2,1)S(1)}, u32[]{:S(2)}) copy-start(bf16[256,128]{1,0:T(8,128)(2,1)S(1)} %get-tuple-element.24.spread) | copy-start | bytes 196612
  77.9 17.1 %all-to-all-start.1 = ((bf16[8,64,128]{2,1,0:T(8,128)(2,1)}), bf16[8,64,128]{2,1,0:T(8,128)(2,1)S(1)}, u32[]{:S(2)}, u32[]{:S(2)}) async-start(bf16[8,64,128]{2,1,0:T(8,128)(2,1)} %get-tuple-element.22), calls=%async_computation.1 | async-start | bytes 262144 | tf_op jit(solution)/shard_map/all_to_all | solution.py:305
  95.0 1.2 copy-start
  96.2 40.7 %copy-start.1 = (bf16[1024,512]{1,0:T(8,128)(2,1)S(1)}, bf16[1024,512]{1,0:T(8,128)(2,1)}, u32[]{:S(2)}) copy-start(bf16[1024,512]{1,0:T(8,128)(2,1)} %all-gather.7.cloned.1.call-done) | copy-start | bytes 3145732
  98.1 0.6 copy-start.24
  98.7 38.2 %all-to-all-start.2 = ((bf16[16,16,1024]{2,1,0:T(8,128)(2,1)}), bf16[16,16,1024]{2,1,0:T(8,128)(2,1)S(1)}, u32[]{:S(2)}, u32[]{:S(2)}) async-start(bf16[16,16,1024]{2,1,0:T(8,128)(2,1)} %bitcast.18), calls=%async_computation.2 | async-start | bytes 1048576 | tf_op jit(solution)/shard_map/all_to_all | solution.py:305
  136.9 1.4 copy-start.2
  139.8 0.7 copy-start.7
  140.5 0.8 copy-start.13
  141.3 0.7 copy-start.20
  141.9 54.0 %copy-start.3 = (bf16[1024,768]{1,0:T(8,128)(2,1)S(1)}, bf16[1024,768]{1,0:T(8,128)(2,1)}, u32[]{:S(2)}) copy-start(bf16[1024,768]{1,0:T(8,128)(2,1)} %all-gather.9.cloned.1.call-done) | copy-start | bytes 4718596
  141.9 22.6 %all-to-all-start.3 = ((bf16[8,256,128]{2,1,0:T(8,128)(2,1)}), bf16[8,256,128]{2,1,0:T(8,128)(2,1)}, u32[]{:S(2)}, u32[]{:S(2)}) async-start(bf16[8,256,128]{2,1,0:T(8,128)(2,1)} %copy-done.13), calls=%async_computation.3 | async-start | bytes 1048576 | tf_op jit(solution)/shard_map/all_to_all | solution.py:305
  150.0 37.6 %all-gather.11.cloned.1.call-start = ((), (), s32[]{:S(2)}) async-start(), calls=%async_computation.11 | async-start | bytes 1179648 | tf_op jit(solution)/shard_map/all_gather | solution.py:361
  164.6 1.0 copy-start.15
  177.6 0.7 copy-start.16
  178.4 0.7 copy-start.22
  179.1 16.8 %all-to-all-start.4 = ((bf16[8,192,128]{2,1,0:T(8,128)(2,1)}), bf16[8,192,128]{2,1,0:T(8,128)(2,1)}, u32[]{:S(2)}, u32[]{:S(2)}) async-start(bf16[8,192,128]{2,1,0:T(8,128)(2,1)} %copy-done.16), calls=%async_computation.4 | async-start | bytes 786432 | tf_op jit(solution)/shard_map/all_to_all | solution.py:305
  195.9 1.2 copy-start.6
  197.1 0.9 copy-start.8
  198.0 0.8 copy-start.18
  198.9 0.9 copy-start.21
  199.8 0.9 copy-start.23
  200.7 34.6 %copy-start.25 = (bf16[256,128]{1,0:T(8,128)(2,1)S(1)}, bf16[256,128]{1,0:T(8,128)(2,1)}, u32[]{:S(2)}) copy-start(bf16[256,128]{1,0:T(8,128)(2,1)} %copy-done.24) | copy-start | bytes 196612
  202.8 63.8 %copy-start.10 = (bf16[1024,256]{1,0:T(8,128)(2,1)S(1)}, bf16[1024,256]{1,0:T(8,128)(2,1)}, u32[]{:S(2)}) copy-start(bf16[1024,256]{1,0:T(8,128)(2,1)} %copy-done.9) | copy-start | bytes 1572868
  202.9 63.8 %copy-start.12 = (f32[1024,128]{1,0:T(8,128)S(1)}, f32[1024,128]{1,0:T(8,128)}, u32[]{:S(2)}) copy-start(f32[1024,128]{1,0:T(8,128)} %copy-done.11) | copy-start | bytes 1572868
  236.9 12.5 %all-to-all-start.6 = ((bf16[8,64,128]{2,1,0:T(8,128)(2,1)}), bf16[8,64,128]{2,1,0:T(8,128)(2,1)S(1)}, u32[]{:S(2)}, u32[]{:S(2)}) async-start(bf16[8,64,128]{2,1,0:T(8,128)(2,1)} %bitcast.21), calls=%async_computation.6 | async-start | bytes 262144 | tf_op jit(solution)/shard_map/all_to_all | solution.py:305
  243.5 4.4 %collective-permute-start = (f32[4,512]{1,0:T(4,128)S(1)}, f32[4,512]{1,0:T(4,128)S(1)}, u32[]{:S(2)}, u32[]{:S(2)}) collective-permute-start(f32[4,512]{1,0:T(4,128)S(1)} %get-tuple-element.33), channel_id=1, source_target_pairs={{0,1},{1,0},{2,3},{3,2},{4,5},{5,4},{6,7},{7,6},{8,9},{9,8},{10,11... | collective-permute-start | bytes 24584 | tf_op jit(solution)/shard_map/ppermute | solution.py:385
  249.4 28.2 %collective-permute-start.1 = (f32[4,512]{1,0:T(4,128)S(1)}, f32[4,512]{1,0:T(4,128)S(1)}, u32[]{:S(2)}, u32[]{:S(2)}) collective-permute-start(f32[4,512]{1,0:T(4,128)S(1)} %add.26), channel_id=1, source_target_pairs={{0,0},{4,64},{8,128},{12,192},{16,256},{20,320},{24,384},{28,448},... | collective-permute-start | bytes 24584 | tf_op jit(solution)/shard_map/ppermute | solution.py:390
  252.9 24.8 %collective-permute-start.2 = (f32[4,512]{1,0:T(4,128)S(1)}, f32[4,512]{1,0:T(4,128)S(1)}, u32[]{:S(2)}, u32[]{:S(2)}) collective-permute-start(f32[4,512]{1,0:T(4,128)S(1)} %add.26), channel_id=1, source_target_pairs={{0,2},{1,3},{2,0},{3,1},{4,66},{5,67},{6,64},{7,65},{8,130},{9,131... | collective-permute-start | bytes 24584 | tf_op jit(solution)/shard_map/ppermute | solution.py:391
  277.6 14.4 %all-to-all-start.7 = ((bf16[8,192,128]{2,1,0:T(8,128)(2,1)}), bf16[8,192,128]{2,1,0:T(8,128)(2,1)S(1)}, u32[]{:S(2)}, u32[]{:S(2)}) async-start(bf16[8,192,128]{2,1,0:T(8,128)(2,1)} %shard_map.110), calls=%async_computation.7 | async-start | bytes 786432 | tf_op jit(solution)/shard_map/all_to_all | solution.py:305
  281.1 4.2 %collective-permute-start.3 = (bf16[512,768]{1,0:T(8,128)(2,1)S(1)}, bf16[512,768]{1,0:T(8,128)(2,1)S(1)}, u32[]{:S(2)}, u32[]{:S(2)}) collective-permute-start(bf16[512,768]{1,0:T(8,128)(2,1)S(1)} %all_gather.20.weights.project), channel_id=1, source_target_pairs={{0,4},{4,0},{1,5},{5,1},{2,6},{6,2},{3,7},{7,3},{8,12},{12,8},{9,1... | collective-permute-start | bytes 2359304 | tf_op jit(solution)/shard_map/ppermute | solution.py:336
Sparse Core Ops, SparseCore 0:
  10.1 46.1 all-gather.4
  58.5 32.6 all-gather.6
  93.3 32.1 all-gather.8
  152.5 34.9 all-gather.10
where the time goes:
time: 302 us; the launch traced here: 301 us
  blocking collectives  82.2 us (27%)
  waiting for transfers between devices  72.8 us (24%)
  starting transfers between devices  65.4 us (22%)
  Pallas kernels  41.9 us (14%)
  local copies, waits for them, and re-layouts  21.3 us (7%)
  between operations  14 us (5%)
    all_to_all x6, waiting for transfers between devices, exchange(): return lax.all_to_all(value, axes, split_axis=0, concat_axis=0, tiled=True)  45.9 us
    all_to_all x6, starting transfers between devices, exchange(): return lax.all_to_all(value, axes, split_axis=0, concat_axis=0, tiled=True)  43 us
    all_to_all x2, blocking collectives, exchange(): return lax.all_to_all(value, axes, split_axis=0, concat_axis=0, tiled=True)  42.6 us
    pallas_call x8, Pallas kernels, run(): pl.pallas_call(kernel, out_shape=[jax.ShapeDtypeStruct(s, d) for s, d in...  41.9 us
    all_gather x1, blocking collectives, per_device(): weights = lax.all_gather(weights, ('zh', 'zl'), axis=0, tiled=True)  27.5 us
    all_gather x1, waiting for transfers between devices, per_device(): lax.all_gather(weights[:, third:2 * third], ('x', 'core'), axis=0, tiled=...  17.9 us
    unnamed x61, local copies, waits for them, and re-layouts  17 us
    ppermute x1, starting transfers between devices, per_device(): lax.ppermute(term, PTS + ('scene',), [(a * SCENES + i, b * SCENES + (i ^...  13.7 us
  transfers between devices with their start and end apart: 14, of which 11 were waited for; matrix products, arithmetic and copies ran while one was open for 2% of the time, Pallas kernels for 12%

commit v1 on v0

v1 whole, which is shorter than its diff:
```python
import functools

import jax
import jax.numpy as jnp
from jax import lax
from jax.experimental import pallas as pl
from jax.experimental.pallas import tpu as pltpu
from jax.sharding import Mesh, PartitionSpec as P

HEADS = 16
PATCH = 1024
WIDTH = 512
HEAD = 32
ROWS = 128
PAIR = 64
MEMBERS = 8
PATCHES = 16
SLOTS = 16
META = 16
SHARE = 4
SCENES = 4
PROJECT_H = (0, 768)
OUTPUT_Z = (768, 1024)
OUTPUT_H = (1024, 1280)
EPSILON = 1e-05
NEGATIVE = -1e30
SCALE = HEAD ** (-0.5)
LOG2E = 1.4426950408889634
QBLOCK = 256

F32 = jnp.float32
BF16 = jnp.bfloat16
PTS = ("x", "zh", "zl", "core")
GROUP = ("zl", "core")
ACROSS = ("x", "zh")


def dot(a, b, ca=1, cb=0):
    return lax.dot_general(a, b, (((ca,), (cb,)), ((), ())), preferred_element_type=F32)


def normalize(values):
    center = values - jnp.mean(values, axis=1, keepdims=True)
    inverse = lax.rsqrt(jnp.mean(center * center, axis=1, keepdims=True) + EPSILON)
    return center * inverse, inverse


def normalize_back(grad, unit, inverse):
    middle = grad - jnp.mean(grad, axis=1, keepdims=True)
    return inverse * (middle - unit * jnp.mean(grad * unit, axis=1, keepdims=True))


def iota(shape, dim):
    return lax.broadcasted_iota(jnp.int32, shape, dim)


def call(kernel, ins, outs, scratch=(), limit=32):
    views = [item[1:] if isinstance(item, tuple) else None for item in ins]
    arrays = [item[0] if isinstance(item, tuple) else item for item in ins]
    scalars = [a.ndim == 1 for a in arrays]

    def body(*refs):
        given = list(refs)
        for k, view in enumerate(views):
            if view is not None:
                lead = (slice(None),) * (len(arrays[k].shape) - 1)
                given[k] = refs[k].at[lead + (pl.ds(view[0], view[1] - view[0]),)]
        kernel(*given)

    return pl.pallas_call(
        body,
        out_shape=[jax.ShapeDtypeStruct(shape, dtype) for shape, dtype in outs],
        in_specs=[pl.BlockSpec(memory_space=pltpu.SMEM if flat else pltpu.VMEM) for flat in scalars],
        out_specs=[pl.BlockSpec(memory_space=pltpu.VMEM) for _ in outs],
        scratch_shapes=list(scratch),
        compiler_params=pltpu.CompilerParams(vmem_limit_bytes=limit * 1024 * 1024),
    )(*arrays)


def softmax_keys(keys, query, mask):
    scores = dot(keys, query, 1, 1) * (SCALE * LOG2E)
    scores = jnp.where(mask, scores, NEGATIVE)
    weights = jnp.exp2(scores - jnp.max(scores, axis=0, keepdims=True))
    return weights * (1.0 / jnp.sum(weights, axis=0, keepdims=True))


def key_mask(flags):
    parts = []
    for b in range(MEMBERS):
        pick = jnp.where(iota((MEMBERS, QBLOCK), 0) == b, 1.0, 0.0).astype(BF16)
        parts.append(dot(flags, pick, 0, 0))
    return jnp.concatenate(parts, axis=0) > 0.5


def place_rows(targets):
    patch = targets[...] // PATCH
    patches = jnp.broadcast_to(patch, (MEMBERS, ROWS)).astype(F32)
    column = jnp.broadcast_to(patches.T[:, :1], (ROWS, ROWS))
    row = jnp.broadcast_to(patch, (ROWS, ROWS)).astype(F32)
    same = (column == row) & (iota((ROWS, ROWS), 0) < iota((ROWS, ROWS), 1))
    rank = jnp.sum(jnp.where(same, 1.0, 0.0), axis=0, keepdims=True).astype(jnp.int32)
    code = patch * SLOTS + rank
    return jnp.where(iota((PATCHES * SLOTS, ROWS), 0) == code, 1.0, 0.0).astype(BF16)


def prepare_kernel(points, sources, project_z, project_h, output_z, output_h, mine, weights):
    mine[:ROWS, :] = points[...]
    source = sources[...]
    digits = jnp.concatenate([source // ROWS, source % ROWS], axis=1).astype(F32)
    digits = jnp.concatenate([digits, jnp.zeros((1, WIDTH - 2 * ROWS), F32)], axis=1)
    mine[ROWS:, :] = jnp.broadcast_to(digits, (META, WIDTH)).astype(BF16)
    for c in range(2):
        pieces = []
        for project in (project_z, project_h):
            values = project[...].astype(F32)
            pairs = range(c, MEMBERS, 2)
            pieces += [values[:, k * PAIR : (k + 1) * PAIR] for k in pairs]
            for k in pairs:
                pieces += [
                    values[:, n * WIDTH + k * PAIR : n * WIDTH + (k + 1) * PAIR] for n in (1, 2)
                ]
        for output in (output_z, output_h):
            half = WIDTH // 2
            pieces.append(output[:, c * half : (c + 1) * half].astype(F32))
        weights[c] = jnp.concatenate(pieces, axis=1).astype(BF16)


def forward_kernel(scal, gathered, weights, qkv, attended, plan, att):
    member = scal[0]
    limit = scal[2 + scal[1]]
    w = weights[...]
    stride = ROWS + META
    source = gathered
    device = iota((ROWS, ROWS), 0)
    total = jnp.zeros((ROWS, ROWS), F32)
    flagged = jnp.zeros((ROWS, ROWS), F32)
    bound = jnp.concatenate(
        [scal[2 + k] - ROWS * iota((MEMBERS, ROWS), 0) for k in range(PATCHES)], axis=0
    ).astype(F32)
    device_f = device.astype(F32)
    for b in range(MEMBERS):
        first = b * stride
        block = source[first : first + ROWS, :]
        unit, _ = normalize(block.astype(F32))
        unit = unit.astype(BF16)
        rows = slice(b * ROWS, (b + 1) * ROWS)
        qkv[rows, :] = dot(unit, w).astype(BF16)
        meta = source[first + ROWS : first + stride, :].astype(F32)
        owner = meta[0:1, 0:ROWS]
        place = meta[0:1, ROWS : 2 * ROWS]
        hit = device_f == owner
        total += jnp.where(hit, 1.0, 0.0)
        flagged += jnp.where(hit & (place < bound), 1.0, 0.0)
    total = jnp.sum(total, axis=1, keepdims=True)
    flagged = jnp.sum(flagged, axis=1, keepdims=True)
    lane = iota((MEMBERS, ROWS), 1).astype(F32)
    mine = iota((MEMBERS, 1), 0) == member
    slot = iota((SLOTS, ROWS), 0).astype(F32)
    lane_slot = iota((SLOTS, ROWS), 1).astype(F32)
    offset = jnp.zeros((MEMBERS, 1), F32)
    flags = jnp.zeros((MEMBERS, ROWS), F32)
    for k in range(PATCHES):
        here = total[k * MEMBERS : (k + 1) * MEMBERS, :]
        good = flagged[k * MEMBERS : (k + 1) * MEMBERS, :]
        flags += jnp.where((lane >= offset) & (lane < offset + good), 1.0, 0.0)
        own_first = jnp.sum(jnp.where(mine, offset, 0.0), axis=0, keepdims=True)
        own_count = jnp.sum(jnp.where(mine, here, 0.0), axis=0, keepdims=True)
        plan[k * SLOTS : (k + 1) * SLOTS, :] = jnp.where(
            (slot + own_first == lane_slot) & (slot < own_count), 1.0, 0.0
        ).astype(BF16)
        offset += here
    plan[PATCHES * SLOTS :, :] = jnp.concatenate([flags, flags], axis=0).astype(BF16)
    mask = iota((PATCH, QBLOCK), 0) < limit
    for h in range(2):
        keys = qkv[:, h * HEAD : (h + 1) * HEAD]
        values_t = qkv[:, PAIR + h * HEAD : PAIR + (h + 1) * HEAD].astype(F32).T.astype(BF16)
        for n in range(PATCH // QBLOCK):
            span = slice(n * QBLOCK, (n + 1) * QBLOCK)
            query = qkv[span, 2 * PAIR + h * HEAD : 2 * PAIR + (h + 1) * HEAD]
            probs = softmax_keys(keys, query, mask)
            att[h * HEAD : (h + 1) * HEAD, span] = dot(values_t, probs.astype(BF16))
    for b in range(MEMBERS):
        attended[b] = att[:, b * ROWS : (b + 1) * ROWS].astype(BF16)


def halves(blocks, first, last):
    return [
        jnp.concatenate([blocks[2 * x + c, :, first:last] for x in range(4)], axis=0)
        for c in range(2)
    ]


def mix_kernel(targets, attended, points, cotangent, shared, send):
    place = place_rows(targets)
    weights = halves(shared, 0, WIDTH // 2)
    mixed = jnp.concatenate([dot(attended[...], w, 0, 0) for w in weights], axis=1)
    mixed = points[...].astype(F32) + mixed
    send[:, :WIDTH] = dot(place, mixed.astype(BF16)).astype(BF16)
    send[:, WIDTH:] = dot(place, cotangent[...]).astype(BF16)


def project_kernel(arrived, plan, project, output, send, rows_out, grads_out):
    gathered = dot(plan[: PATCHES * SLOTS, :], arrived[...], 0, 0).astype(BF16)
    mixed = gathered[:, :WIDTH]
    grad = gathered[:, WIDTH:]
    grads_out[...] = grad
    rows_out[...] = mixed
    unit, _ = normalize(mixed.astype(F32))
    unit = unit.astype(BF16)
    projected = [dot(unit, w) for w in halves(project, 0, 3 * WIDTH // 2)]
    low, high = halves(output, 0, WIDTH // 2)
    grad_attended = dot(grad[:, : WIDTH // 2], low, 1, 1) + dot(grad[:, WIDTH // 2 :], high, 1, 1)
    for k in range(MEMBERS):
        half, t = projected[k % 2], k // 2
        first = WIDTH // 2 + t * 2 * PAIR
        send[k, :ROWS, :] = half[:, first : first + 2 * PAIR].astype(BF16)
        send[k, ROWS:, :] = jnp.concatenate(
            [half[:, t * PAIR : (t + 1) * PAIR], grad_attended[:, k * PAIR : (k + 1) * PAIR]],
            axis=1,
        ).astype(BF16)


def backward_body(qkv, grad_t, mask, send, attended, dq, dk, dv):
    for h in range(2):
        low, high = h * HEAD, (h + 1) * HEAD
        keys = qkv[:, low:high]
        values = qkv[:, PAIR + low : PAIR + high]
        keys_t = keys.astype(F32).T.astype(BF16)
        values_t = values.astype(F32).T.astype(BF16)
        for n in range(PATCH // QBLOCK):
            span = slice(n * QBLOCK, (n + 1) * QBLOCK)
            query = qkv[span, 2 * PAIR + low : 2 * PAIR + high]
            grad = grad_t[low:high, span]
            probs = softmax_keys(keys, query, mask)
            probs_low = probs.astype(BF16)
            grad_probs = dot(values, grad)
            row_dot = jnp.sum(probs * grad_probs, axis=0, keepdims=True)
            grad_scores = (probs * (grad_probs - row_dot)).astype(BF16)
            dq[low:high, span] = dot(keys_t, grad_scores)
            part_k = dot(grad_scores, query)
            part_v = dot(probs_low, grad, 1, 1)
            if n == 0:
                dk[:, low:high] = part_k
                dv[:, low:high] = part_v
            else:
                dk[:, low:high] += part_k
                dv[:, low:high] += part_v
            if attended is not None:
                attended[low:high, span] = dot(values_t, probs_low).astype(BF16)
    for b in range(MEMBERS):
        rows = slice(b * ROWS, (b + 1) * ROWS)
        send[b, :ROWS, :] = jnp.concatenate([dk[rows, :] * SCALE, dv[rows, :]], axis=1).astype(BF16)
        send[b, ROWS:, :] = (dq[:, rows] * SCALE).astype(BF16)


def backward_h_kernel(arrived, plan, send, attended, qkv, grad_t, dq, dk, dv):
    for b in range(MEMBERS):
        rows = slice(b * ROWS, (b + 1) * ROWS)
        qkv[rows, :ROWS] = arrived[b, :ROWS, :]
        both = arrived[b, ROWS:, :]
        qkv[rows, ROWS:] = both
        grad_t[:, rows] = both.astype(F32).T[PAIR:, :].astype(BF16)
    mask = key_mask(plan[PATCHES * SLOTS : PATCHES * SLOTS + MEMBERS, :])
    backward_body(qkv, grad_t, mask, send, attended, dq, dk, dv)


def backward_z_kernel(scal, arrived, qkv, send, grad_t, dq, dk, dv):
    for b in range(MEMBERS):
        grad_t[:, b * ROWS : (b + 1) * ROWS] = arrived[b]
    mask = iota((PATCH, QBLOCK), 0) < scal[2 + scal[1]]
    backward_body(qkv, grad_t, mask, send, None, dq, dk, dv)


def input_grad(arrived, weights, rows, grads):
    sides = []
    for c in range(2):
        members = range(c, MEMBERS, 2)
        query_part = jnp.concatenate([arrived[k, ROWS:, :].astype(F32) for k in members], axis=0)
        sides.append(
            jnp.concatenate(
                [query_part.T.astype(BF16)] + [arrived[k, :ROWS, :] for k in members], axis=1
            )
        )
    grad_normed = dot(sides[0], weights[0], 1, 1) + dot(sides[1], weights[1], 1, 1)
    unit, inverse = normalize(rows[...].astype(F32))
    return (grads[...].astype(F32) + normalize_back(grad_normed, unit, inverse)).astype(BF16)


def return_kernel(arrived, project, rows, grads, plan, attended, all_grads, send):
    grad = input_grad(arrived, halves(project, 0, 3 * WIDTH // 2), rows, grads)
    spaced = dot(plan[: PATCHES * SLOTS, :], grad).astype(BF16)
    term = dot(attended[...], all_grads[...])
    upper = term.astype(BF16)
    lower = (term - upper.astype(F32)).astype(BF16)
    for k in range(PATCHES):
        send[k, :SLOTS, :] = spaced[k * SLOTS : (k + 1) * SLOTS, :]
        share = slice(k * SHARE, (k + 1) * SHARE)
        send[k, SLOTS:, :] = jnp.concatenate([upper[share, :], lower[share, :]], axis=0)


def regain_kernel(arrived, targets, output, grad_mixed, send, term):
    spaced = jnp.concatenate([arrived[k, :SLOTS, :] for k in range(PATCHES)], axis=0)
    grad = dot(place_rows(targets), spaced, 0, 0).astype(BF16)
    grad_mixed[...] = grad
    low, high = halves(output, 0, WIDTH // 2)
    grad_attended = dot(low, grad[:, : WIDTH // 2], 1, 1) + dot(high, grad[:, WIDTH // 2 :], 1, 1)
    send[...] = grad_attended.astype(BF16)
    total = jnp.zeros((2 * SHARE, WIDTH), F32)
    for k in range(PATCHES):
        total += arrived[k, SLOTS:, :].astype(F32)
    factor = (SCENES * PATCHES * PATCH) ** (-0.5)
    term[...] = (total[:SHARE, :] + total[SHARE:, :]) * factor


def finish_kernel(arrived, project, rows, grads, out):
    out[...] = input_grad(arrived, halves(project, 0, 3 * WIDTH // 2), rows, grads)


def exchange(value, axes):
    return lax.all_to_all(value, axes, split_axis=0, concat_axis=0, tiled=True)


def per_device(
    points, cotangent, valid_counts, zorder_targets, hilbert_sources,
    zorder_project, zorder_output, hilbert_project, hilbert_output,
):
    rows = points[0]
    cot = cotangent[0]
    member = lax.axis_index(GROUP).astype(jnp.int32)
    patch = lax.axis_index(ACROSS).astype(jnp.int32)
    scal = jnp.concatenate([jnp.stack([member, patch]), valid_counts[0]])
    targets = zorder_targets[0]
    sources = hilbert_sources[0]

    mine, weights = call(
        prepare_kernel,
        [rows, sources[None, :], zorder_project, hilbert_project, zorder_output, hilbert_output],
        [((ROWS + META, WIDTH), BF16), ((2, SHARE, 4 * WIDTH), BF16)],
    )
    gathered = lax.all_gather(mine, GROUP, axis=0, tiled=True)
    weights = exchange(weights, "core").reshape(MEMBERS, 4 * WIDTH)
    weights = lax.all_gather(weights, ("zh", "zl"), axis=0, tiled=True)
    third = 3 * WIDTH // 2
    quarter = lax.axis_index("zl")
    own = jnp.concatenate(
        [
            lax.dynamic_slice_in_dim(weights, 4 * PAIR + quarter * 2 * PAIR, 2 * PAIR, 1),
            lax.dynamic_slice_in_dim(weights, quarter * PAIR, PAIR, 1),
            jnp.zeros((ROWS, PAIR), BF16),
        ],
        axis=1,
    )
    own = lax.all_gather(own, "x", axis=0, tiled=True)
    shared = lax.all_gather(weights[:, third:], ("x", "core"), axis=0, tiled=True)
    shared = shared.reshape(MEMBERS, ROWS, third + WIDTH)
    project_z = lax.all_gather(weights[:, :third], ("x", "core"), axis=0, tiled=True)
    project_z = project_z.reshape(MEMBERS, ROWS, third)

    targets = targets[None, :]
    qkv_z, attended, plan = call(
        forward_kernel,
        [scal, gathered, own],
        [
            ((PATCH, 4 * PAIR), BF16),
            ((MEMBERS, PAIR, ROWS), BF16),
            ((PATCHES * SLOTS + 2 * MEMBERS, ROWS), BF16),
        ],
        [pltpu.VMEM((PAIR, PATCH), F32)],
    )

    attended = exchange(attended, GROUP).reshape(WIDTH, ROWS)
    (send,) = call(
        mix_kernel,
        [targets, attended, rows, cot, (shared, *OUTPUT_Z)],
        [((PATCHES * SLOTS, 2 * WIDTH), BF16)],
    )

    arrived = exchange(send.reshape(PATCHES, SLOTS, 2 * WIDTH), ACROSS)
    send, rows_h, grads_h = call(
        project_kernel,
        [
            arrived.reshape(PATCHES * SLOTS, 2 * WIDTH),
            plan,
            (shared, *PROJECT_H),
            (shared, *OUTPUT_H),
        ],
        [((MEMBERS, 2 * ROWS, ROWS), BF16), ((ROWS, WIDTH), BF16), ((ROWS, WIDTH), BF16)],
    )
    all_grads_h = lax.all_gather(grads_h, GROUP, axis=0, tiled=True)

    arrived = exchange(send, GROUP)
    sums = [
        pltpu.VMEM((PAIR, PATCH), F32),
        pltpu.VMEM((PATCH, PAIR), F32),
        pltpu.VMEM((PATCH, PAIR), F32),
    ]
    send, attended_h = call(
        backward_h_kernel,
        [arrived, plan],
        [((MEMBERS, 3 * PAIR, ROWS), BF16), ((PAIR, PATCH), BF16)],
        [pltpu.VMEM((PATCH, 4 * PAIR), BF16), pltpu.VMEM((PAIR, PATCH), BF16)] + sums,
    )

    arrived = exchange(send, GROUP)
    (send,) = call(
        return_kernel,
        [arrived, (shared, *PROJECT_H), rows_h, grads_h, plan, attended_h, all_grads_h],
        [((PATCHES, SLOTS + 2 * SHARE, WIDTH), BF16)],
    )

    arrived = exchange(send, ACROSS)
    grad_mixed, send, term = call(
        regain_kernel,
        [arrived, targets, (shared, *OUTPUT_Z)],
        [((ROWS, WIDTH), BF16), ((WIDTH, ROWS), BF16), ((SHARE, WIDTH), F32)],
    )
    beside = lax.ppermute(term, "scene", [(i, i ^ 1) for i in range(SCENES)])
    arrived = exchange(send.reshape(MEMBERS, PAIR, ROWS), GROUP)
    arrived, beside = lax.optimization_barrier((arrived, beside))
    term = term + beside
    beside = lax.ppermute(term, "scene", [(i, i ^ 2) for i in range(SCENES)])
    (send,) = call(
        backward_z_kernel,
        [scal, arrived, qkv_z],
        [((MEMBERS, 3 * PAIR, ROWS), BF16)],
        [pltpu.VMEM((PAIR, PATCH), BF16)] + sums,
    )
    send, term, beside = lax.optimization_barrier((send, term, beside))
    term = lax.ppermute(
        term + beside,
        PTS,
        [(r * MEMBERS + j, j * PATCHES + r) for r in range(PATCHES) for j in range(MEMBERS)],
    )

    arrived = exchange(send, GROUP)
    (out,) = call(finish_kernel, [arrived, project_z, rows, grad_mixed], [((ROWS, WIDTH), BF16)])
    return out[None], term


def solution(mesh):
    devices = mesh.devices.reshape(4, 4, 4, 2, 4)
    fine = Mesh(devices, ("x", "zh", "zl", "core", "scene"))
    rows = P("scene", PTS, None)
    index = P("scene", PTS)
    weight = P(PTS, None)
    return jax.shard_map(
        per_device,
        mesh=fine,
        in_specs=(rows, rows, P("scene", None), index, index, weight, weight, weight, weight),
        out_specs=(rows, weight),
        check_vma=False,
    )
```

time: 302 us -> 293 us (0.970)
  blocking collectives: 82.2 us -> 107 us
  starting transfers between devices: 65.4 us -> 48.6 us
  waiting for transfers between devices: 72.8 us -> 65.6 us
  Pallas kernels: 41.9 us -> 38.1 us
  local copies, waits for them, and re-layouts: 21.3 us -> 18.1 us
    all_to_all x2 -> x3, blocking collectives: 42.6 us -> 69.4 us  [exchange(): return lax.all_to_all(value, axes, split_axis=0, concat_axis=0, tiled=True)]
    ppermute x3 -> x2, starting transfers between devices: 19.1 us -> 7.18 us  [the longest x1 5.09 us: per_device(): beside = lax.ppermute(term, 'scene', [(i, i ^ 2) for i in range(SCENES)])]
    all_gather x3, waiting for transfers between devices: 19.8 us -> 7.87 us  [the longest x1 7.87 us: per_device(): lax.all_gather(weights[:, third:], ('x', 'core'), axis=0, tiled=True)]
    ppermute x3 -> x2, waiting for transfers between devices: 1.65 us -> 7 us  [the longest x1 7 us: per_device(): lax.ppermute(term + beside, PTS, [(r * MEMBERS + j, j * PATCHES + r) for...]
    all_to_all x6 -> x5, starting transfers between devices: 43 us -> 38.1 us  [exchange(): return lax.all_to_all(value, axes, split_axis=0, concat_axis=0, tiled=True)]
    pallas_call x8 -> x9, Pallas kernels: 41.9 us -> 38.1 us  [call(): pl.pallas_call(body, out_shape=[jax.ShapeDtypeStruct(shape, dtype) for sh...]
    all_to_all x6 -> x5, waiting for transfers between devices: 45.9 us -> 42.5 us  [exchange(): return lax.all_to_all(value, axes, split_axis=0, concat_axis=0, tiled=True)]
    unnamed x61 -> x45, local copies, waits for them, and re-layouts: 17 us -> 15.5 us
  transfers between devices with their start and end apart: 14 -> 12, of which waited for: 11 -> 9; matrix products, arithmetic and copies ran while one was open for 2% -> 1% of each run, Pallas kernels for 12% -> 11%
where the time goes in v1:
time: 293 us; the launch traced here: 292 us
  blocking collectives  107 us (37%)
  waiting for transfers between devices  65.6 us (22%)
  starting transfers between devices  48.6 us (17%)
  Pallas kernels  38.1 us (13%)
  local copies, waits for them, and re-layouts  18.1 us (6%)
  between operations  13.9 us (5%)
    all_to_all x3, blocking collectives, exchange(): return lax.all_to_all(value, axes, split_axis=0, concat_axis=0, tiled=True)  69.4 us
    all_to_all x5, waiting for transfers between devices, exchange(): return lax.all_to_all(value, axes, split_axis=0, concat_axis=0, tiled=True)  42.5 us
    pallas_call x9, Pallas kernels, call(): pl.pallas_call(body, out_shape=[jax.ShapeDtypeStruct(shape, dtype) for sh...  38.1 us
    all_to_all x5, starting transfers between devices, exchange(): return lax.all_to_all(value, axes, split_axis=0, concat_axis=0, tiled=True)  38.1 us
    all_gather x1, blocking collectives, per_device(): weights = lax.all_gather(weights, ('zh', 'zl'), axis=0, tiled=True)  27.6 us
    unnamed x45, local copies, waits for them, and re-layouts  15.5 us
    all_gather x1, blocking collectives, per_device(): own = lax.all_gather(own, 'x', axis=0, tiled=True)  10.2 us
    all_gather x1, waiting for transfers between devices, per_device(): lax.all_gather(weights[:, third:], ('x', 'core'), axis=0, tiled=True)  7.87 us
  transfers between devices with their start and end apart: 12, of which 9 were waited for; matrix products, arithmetic and copies ran while one was open for 1% of the time, Pallas kernels for 11%

profile of v1, /device:TPU:1, one launch (start us, length us, event | category | flops | bytes accessed | tf_op | source)
XLA Modules:
  0.0 291.6 jit_solution(9655760447742345793)
XLA Ops:
  7.2 0.0 all-gather.5.cloned.1.call-start
  7.2 0.0 copy-start.4
  7.2 0.9 copy-done.4
  8.1 0.7 copy-done.14
  8.8 0.7 copy-done.15
  9.5 0.7 copy-done.16
  10.2 0.7 copy-done.17
  10.9 0.7 copy-done.19
  11.6 0.7 shard_map.104
  12.3 0.0 all-gather.5.cloned.1.call-update
  12.3 0.0 all-gather.7.cloned.1.call-start
  12.4 10.3 %all_to_all.40 = bf16[2,4,2048]{2,1,0:T(4,128)(2,1)S(1)} all-to-all(bf16[2,4,2048]{2,1,0:T(4,128)(2,1)S(1)} %get-tuple-element.21), channel_id=1, replica_groups=mesh['x'=4,'zh'=4,'zl'=4,'core'=2,'scene'=4] {'core'}, dimensions={0} | all-to-all | bytes 65536 | tf_op jit(solution)/shard_map/all_to_all | solution.py:320
  22.7 27.6 %all_gather.19 = bf16[128,2048]{1,0:T(8,128)(2,1)S(1)} all-gather(bf16[8,2048]{1,0:T(8,128)(2,1)S(1)} %reshape.25), channel_id=1, replica_groups=mesh['x'=4,'zh'=4,'zl'=4,'core'=2,'scene'=4] {'zh','zl'}, dimensions={0}, use_global_device_ids=true | all-gather | bytes 557056 | tf_op jit(solution)/shard_map/all_gather | solution.py:342
  50.2 0.8 slice.8
  51.0 0.0 all-gather.7.cloned.1.call-update
  51.0 0.1 pad.2.clone
  51.1 0.1 constant_dynamic-slice_fusion
  51.2 10.2 %all_gather.20.refs_2_ = bf16[512,256]{1,0:T(8,128)(2,1)S(1)} all-gather(bf16[128,256]{1,0:T(8,128)(2,1)S(1)} %maximum_maximum_fusion), channel_id=1, replica_groups=mesh['x'=4,'zh'=4,'zl'=4,'core'=2,'scene'=4] {'x'}, dimensions={0}, use_global_device_ids=true | all-gather | bytes 327680 | tf_op jit(solution)/shard_map/all_gather | solution.py:353
  61.4 0.1 pad_add_fusion.refs_0_
  61.5 1.3 copy-done.3
  62.8 8.3 %shard_map.105 = (bf16[1024,256]{1,0:T(8,128)(2,1)S(1)}, bf16[8,64,128]{2,1,0:T(8,128)(2,1)S(1)}, bf16[272,128]{1,0:T(8,128)(2,1)S(1)}) custom-call(s32[18]{0:T(128)S(1)} %pad_add_fusion.refs_0_, bf16[1152,512]{1,0:T(8,128)(2,1)S(1)} %copy-done.3, bf16[512,256]{1,0:T(8,128)(2,1)S(1)} %all_gather.20.refs_2_), custom_call_target="tpu_custom_call" | custom-call | tf_op jit(solution)/shard_map/pallas_call | solution.py:70
  71.0 0.0 copy-start.8
  71.0 0.8 copy-done.8
  71.8 16.2 %all_to_all.41 = bf16[8,64,128]{2,1,0:T(8,128)(2,1)S(1)} all-to-all(bf16[8,64,128]{2,1,0:T(8,128)(2,1)S(1)} %get-tuple-element.22), channel_id=1, replica_groups=mesh['x'=4,'zh'=4,'zl'=4,'core'=2,'scene'=4] {'zl','core'}, dimensions={0} | all-to-all | bytes 262144 | tf_op jit(solution)/shard_map/all_to_all | solution.py:320
  88.1 7.9 %all-gather.7.cloned.1.call-done = bf16[1024,1280]{1,0:T(8,128)(2,1)} async-done(((bf16[128,1280]{1,0:T(8,128)(2,1)}), bf16[1024,1280]{1,0:T(8,128)(2,1)}) %all-gather.7.cloned.1.call-update) | async-done | bytes 2621456 | tf_op jit(solution)/shard_map/all_gather | solution.py:354
  95.9 1.7 copy-done
  97.7 0.6 shard_map.106
  98.2 42.9 %all_to_all.42 = bf16[16,16,1024]{2,1,0:T(8,128)(2,1)S(1)} all-to-all(bf16[16,16,1024]{2,1,0:T(8,128)(2,1)S(1)} %bitcast.18), channel_id=1, replica_groups=mesh['x'=4,'zh'=4,'zl'=4,'core'=2,'scene'=4] {'x','zh'}, dimensions={0} | all-to-all | bytes 1048576 | tf_op jit(solution)/shard_map/all_to_all | solution.py:320
  141.1 1.0 shard_map.107
  142.1 0.8 copy-done.7
  142.9 8.3 %all-to-all-start.3 = ((bf16[8,256,128]{2,1,0:T(8,128)(2,1)}), bf16[8,256,128]{2,1,0:T(8,128)(2,1)S(1)}, u32[]{:S(2)}, u32[]{:S(2)}) async-start(bf16[8,256,128]{2,1,0:T(8,128)(2,1)} %copy-done.7), calls=%async_computation.3 | async-start | bytes 1048576 | tf_op jit(solution)/shard_map/all_to_all | solution.py:320
  151.2 0.0 all-gather.9.cloned.1.call-start
  151.2 0.7 all-gather.9.cloned.1.call-update
  151.9 13.8 %all-to-all-done.3.refs_0_ = bf16[8,256,128]{2,1,0:T(8,128)(2,1)S(1)} async-done(((bf16[8,256,128]{2,1,0:T(8,128)(2,1)}), bf16[8,256,128]{2,1,0:T(8,128)(2,1)S(1)}, u32[]{:S(2)}, u32[]{:S(2)}) %all-to-all-start.3) | async-done | bytes 524320 | tf_op jit(solution)/shard_map/all_to_all | solution.py:320
  165.7 11.2 %shard_map.108 = (bf16[8,192,128]{2,1,0:T(8,128)(2,1)S(1)}, bf16[64,1024]{1,0:T(8,128)(2,1)S(1)}) custom-call(bf16[8,256,128]{2,1,0:T(8,128)(2,1)S(1)} %all-to-all-done.3.refs_0_, bf16[272,128]{1,0:T(8,128)(2,1)S(1)} %get-tuple-element.23.refs_1_.refs_4_), custom_call_target="tpu_custom_call" | custom-call | tf_op jit(solution)/shard_map/pallas_call | solution.py:70
  176.8 0.8 copy-done.10
  177.6 0.6 copy-done.11
  178.2 4.2 %all-to-all-start.4 = ((bf16[8,192,128]{2,1,0:T(8,128)(2,1)}), bf16[8,192,128]{2,1,0:T(8,128)(2,1)S(1)}, u32[]{:S(2)}, u32[]{:S(2)}) async-start(bf16[8,192,128]{2,1,0:T(8,128)(2,1)} %copy-done.10), calls=%async_computation.4 | async-start | bytes 786432 | tf_op jit(solution)/shard_map/all_to_all | solution.py:320
  182.5 6.1 %all-gather.9.cloned.1.call-done.refs_6_ = bf16[1024,512]{1,0:T(8,128)(2,1)} async-done(((bf16[128,512]{1,0:T(8,128)(2,1)}), bf16[1024,512]{1,0:T(8,128)(2,1)}) %all-gather.9.cloned.1.call-update) | async-done | bytes 1048592 | tf_op jit(solution)/shard_map/all_gather | solution.py:389
  188.6 6.8 %all-to-all-done.4.refs_0_ = bf16[8,192,128]{2,1,0:T(8,128)(2,1)S(1)} async-done(((bf16[8,192,128]{2,1,0:T(8,128)(2,1)}), bf16[8,192,128]{2,1,0:T(8,128)(2,1)S(1)}, u32[]{:S(2)}, u32[]{:S(2)}) %all-to-all-start.4) | async-done | bytes 393248 | tf_op jit(solution)/shard_map/all_to_all | solution.py:320
  195.4 1.2 copy-done.6
  196.6 0.9 copy-done.12
  197.5 2.8 shard_map.109
  200.3 7.4 %all-to-all-start.5 = ((bf16[16,24,512]{2,1,0:T(8,128)(2,1)}), bf16[16,24,512]{2,1,0:T(8,128)(2,1)S(1)}, u32[]{:S(2)}, u32[]{:S(2)}) async-start(bf16[16,24,512]{2,1,0:T(8,128)(2,1)} %shard_map.109), calls=%async_computation.5 | async-start | bytes 786432 | tf_op jit(solution)/shard_map/all_to_all | solution.py:320
  207.7 0.3 all-gather.11.cloned.1.call-start
  208.0 1.6 slice.9
  209.6 0.0 all-gather.11.cloned.1.call-update
  209.6 17.6 %all-to-all-done.5.refs_0_ = bf16[16,24,512]{2,1,0:T(8,128)(2,1)S(1)} async-done(((bf16[16,24,512]{2,1,0:T(8,128)(2,1)}), bf16[16,24,512]{2,1,0:T(8,128)(2,1)S(1)}, u32[]{:S(2)}, u32[]{:S(2)}) %all-to-all-start.5) | async-done | bytes 393248 | tf_op jit(solution)/shard_map/all_to_all | solution.py:320
  227.2 1.3 shard_map.110
  228.5 13.1 %all-to-all-start.6 = ((bf16[8,64,128]{2,1,0:T(8,128)(2,1)}), bf16[8,64,128]{2,1,0:T(8,128)(2,1)S(1)}, u32[]{:S(2)}, u32[]{:S(2)}) async-start(bf16[8,64,128]{2,1,0:T(8,128)(2,1)} %bitcast.9), calls=%async_computation.6 | async-start | bytes 262144 | tf_op jit(solution)/shard_map/all_to_all | solution.py:320
  241.6 3.0 %collective-permute-start = (f32[4,512]{1,0:T(4,128)S(1)}, f32[4,512]{1,0:T(4,128)S(1)}, u32[]{:S(2)}, u32[]{:S(2)}) collective-permute-start(f32[4,512]{1,0:T(4,128)S(1)} %get-tuple-element.30), channel_id=1, source_target_pairs={{0,1},{1,0},{2,3},{3,2},{4,5},{5,4},{6,7},{7,6},{8,9},{9,8},{10,11... | collective-permute-start | bytes 24584 | tf_op jit(solution)/shard_map/ppermute | solution.py:417
  244.6 1.4 collective-permute-done
  246.0 1.4 all-to-all-done.6.refs_1_
  247.4 5.1 %collective-permute-start.1 = (f32[4,512]{1,0:T(4,128)S(1)}, f32[4,512]{1,0:T(4,128)S(1)}, u32[]{:S(2)}, u32[]{:S(2)}) collective-permute-start(f32[4,512]{1,0:T(4,128)S(1)} %add.24), channel_id=1, source_target_pairs={{0,2},{1,3},{2,0},{3,1},{4,6},{5,7},{6,4},{7,5},{8,10},{9,11},{10,... | collective-permute-start | bytes 24584 | tf_op jit(solution)/shard_map/ppermute | solution.py:421
  252.5 1.0 copy-done.9
  253.6 10.9 %shard_map.111 = bf16[8,192,128]{2,1,0:T(8,128)(2,1)} custom-call(s32[18]{0:T(128)S(1)} %pad_add_fusion.refs_0_, bf16[8,64,128]{2,1,0:T(8,128)(2,1)S(1)} %all-to-all-done.6.refs_1_, bf16[1024,256]{1,0:T(8,128)(2,1)S(1)} %copy-done.9), custom_call_target="tpu_custom_call" | custom-call | tf_op jit(solution)/shard_map/pallas_call | solution.py:70
  264.5 0.0 collective-permute-done.1
  264.5 5.1 %all-to-all-start.7 = ((bf16[8,192,128]{2,1,0:T(8,128)(2,1)}), bf16[8,192,128]{2,1,0:T(8,128)(2,1)S(1)}, u32[]{:S(2)}, u32[]{:S(2)}) async-start(bf16[8,192,128]{2,1,0:T(8,128)(2,1)} %shard_map.111), calls=%async_computation.7 | async-start | bytes 786432 | tf_op jit(solution)/shard_map/all_to_all | solution.py:320
  269.7 2.1 collective-permute-start.2
  271.8 7.0 %collective-permute-done.2 = f32[4,512]{1,0:T(4,128)S(1)} collective-permute-done((f32[4,512]{1,0:T(4,128)S(1)}, f32[4,512]{1,0:T(4,128)S(1)}, u32[]{:S(2)}, u32[]{:S(2)}) %collective-permute-start.2) | collective-permute-done | bytes 8224 | tf_op jit(solution)/shard_map/ppermute | solution.py:429
  278.8 2.9 all-to-all-done.7.refs_0_
  281.6 1.4 copy-done.2
  283.0 1.4 shard_map.112
  284.4 0.6 copy.12
  (34 shorter events, 0.1 us)
Async XLA Ops:
  7.2 54.3 %copy-start.21 = (s32[1,16]{1,0:T(1,128)S(1)}, s32[1,16]{1,0:T(1,128)}, u32[]{:S(2)}) copy-start(s32[1,16]{1,0:T(1,128)} %param.11) | copy-start | bytes 196
  7.2 54.3 %all-gather.5.cloned.1.call-start = ((), (), s32[]{:S(2)}) async-start(), calls=%async_computation.8 | async-start | bytes 1327104 | tf_op jit(solution)/shard_map/all_gather | solution.py:340
  7.2 0.9 copy-start.4
  8.1 0.7 copy-start.14
  8.8 0.7 copy-start.15
  9.5 0.7 copy-start.16
  10.2 0.7 copy-start.17
  10.9 0.7 copy-start.19
  12.3 83.6 %all-gather.7.cloned.1.call-start = ((), (), s32[]{:S(2)}) async-start(), calls=%async_computation.9 | async-start | bytes 2949120 | tf_op jit(solution)/shard_map/all_gather | solution.py:354
  50.2 1.0 copy-start.20
  50.2 45.7 %copy-start.5 = (bf16[1,128,512]{2,1,0:T(8,128)(2,1)S(1)}, bf16[1,128,512]{2,1,0:T(8,128)(2,1)}, u32[]{:S(2)}) copy-start(bf16[1,128,512]{2,1,0:T(8,128)(2,1)} %param.9) | copy-start | bytes 393220
  50.2 45.7 %copy-start.13 = (bf16[1,128,512]{2,1,0:T(8,128)(2,1)S(1)}, bf16[1,128,512]{2,1,0:T(8,128)(2,1)}, u32[]{:S(2)}) copy-start(bf16[1,128,512]{2,1,0:T(8,128)(2,1)} %param.10) | copy-start | bytes 393220
  50.2 45.7 %copy-start.18 = (s32[1,128]{1,0:T(1,128)S(1)}, s32[1,128]{1,0:T(1,128)}, u32[]{:S(2)}) copy-start(s32[1,128]{1,0:T(1,128)} %refs_1_.3) | copy-start | bytes 1540
  61.5 1.3 copy-start.3
  71.0 0.8 copy-start.8
  95.9 1.7 copy-start
  97.7 43.4 %copy-start.1 = (bf16[1024,1280]{1,0:T(8,128)(2,1)S(1)}, bf16[1024,1280]{1,0:T(8,128)(2,1)}, u32[]{:S(2)}) copy-start(bf16[1024,1280]{1,0:T(8,128)(2,1)} %all-gather.7.cloned.1.call-done) | copy-start | bytes 7864324
  142.1 0.8 copy-start.7
  142.9 22.8 %all-to-all-start.3 = ((bf16[8,256,128]{2,1,0:T(8,128)(2,1)}), bf16[8,256,128]{2,1,0:T(8,128)(2,1)S(1)}, u32[]{:S(2)}, u32[]{:S(2)}) async-start(bf16[8,256,128]{2,1,0:T(8,128)(2,1)} %copy-done.7), calls=%async_computation.3 | async-start | bytes 1048576 | tf_op jit(solution)/shard_map/all_to_all | solution.py:320
  151.2 37.4 %all-gather.9.cloned.1.call-start = ((), (), s32[]{:S(2)}) async-start(), calls=%async_computation.10 | async-start | bytes 1179648 | tf_op jit(solution)/shard_map/all_gather | solution.py:389
  176.8 0.8 copy-start.10
  177.6 0.7 copy-start.11
  178.2 17.1 %all-to-all-start.4 = ((bf16[8,192,128]{2,1,0:T(8,128)(2,1)}), bf16[8,192,128]{2,1,0:T(8,128)(2,1)S(1)}, u32[]{:S(2)}, u32[]{:S(2)}) async-start(bf16[8,192,128]{2,1,0:T(8,128)(2,1)} %copy-done.10), calls=%async_computation.4 | async-start | bytes 786432 | tf_op jit(solution)/shard_map/all_to_all | solution.py:320
  195.4 1.2 copy-start.6
  196.6 0.9 copy-start.12
  200.3 26.9 %all-to-all-start.5 = ((bf16[16,24,512]{2,1,0:T(8,128)(2,1)}), bf16[16,24,512]{2,1,0:T(8,128)(2,1)S(1)}, u32[]{:S(2)}, u32[]{:S(2)}) async-start(bf16[16,24,512]{2,1,0:T(8,128)(2,1)} %shard_map.109), calls=%async_computation.5 | async-start | bytes 786432 | tf_op jit(solution)/shard_map/all_to_all | solution.py:320
  207.7 71.0 %all-gather.11.cloned.1.call-start = ((), (), s32[]{:S(2)}) async-start(), calls=%async_computation.11 | async-start | bytes 1769472 | tf_op jit(solution)/shard_map/all_gather | solution.py:356
  228.5 18.9 %all-to-all-start.6 = ((bf16[8,64,128]{2,1,0:T(8,128)(2,1)}), bf16[8,64,128]{2,1,0:T(8,128)(2,1)S(1)}, u32[]{:S(2)}, u32[]{:S(2)}) async-start(bf16[8,64,128]{2,1,0:T(8,128)(2,1)} %bitcast.9), calls=%async_computation.6 | async-start | bytes 262144 | tf_op jit(solution)/shard_map/all_to_all | solution.py:320
  241.6 4.4 %collective-permute-start = (f32[4,512]{1,0:T(4,128)S(1)}, f32[4,512]{1,0:T(4,128)S(1)}, u32[]{:S(2)}, u32[]{:S(2)}) collective-permute-start(f32[4,512]{1,0:T(4,128)S(1)} %get-tuple-element.30), channel_id=1, source_target_pairs={{0,1},{1,0},{2,3},{3,2},{4,5},{5,4},{6,7},{7,6},{8,9},{9,8},{10,11... | collective-permute-start | bytes 24584 | tf_op jit(solution)/shard_map/ppermute | solution.py:417
  247.4 17.1 %collective-permute-start.1 = (f32[4,512]{1,0:T(4,128)S(1)}, f32[4,512]{1,0:T(4,128)S(1)}, u32[]{:S(2)}, u32[]{:S(2)}) collective-permute-start(f32[4,512]{1,0:T(4,128)S(1)} %add.24), channel_id=1, source_target_pairs={{0,2},{1,3},{2,0},{3,1},{4,6},{5,7},{6,4},{7,5},{8,10},{9,11},{10,... | collective-permute-start | bytes 24584 | tf_op jit(solution)/shard_map/ppermute | solution.py:421
  252.5 1.0 copy-start.9
  264.5 17.1 %all-to-all-start.7 = ((bf16[8,192,128]{2,1,0:T(8,128)(2,1)}), bf16[8,192,128]{2,1,0:T(8,128)(2,1)S(1)}, u32[]{:S(2)}, u32[]{:S(2)}) async-start(bf16[8,192,128]{2,1,0:T(8,128)(2,1)} %shard_map.111), calls=%async_computation.7 | async-start | bytes 786432 | tf_op jit(solution)/shard_map/all_to_all | solution.py:320
  269.7 9.1 %collective-permute-start.2 = (f32[4,512]{1,0:T(4,128)S(1)}, f32[4,512]{1,0:T(4,128)S(1)}, u32[]{:S(2)}, u32[]{:S(2)}) collective-permute-start(f32[4,512]{1,0:T(4,128)S(1)} %add.25), channel_id=1, source_target_pairs={{0,0},{4,64},{8,128},{12,192},{16,256},{20,320},{24,384},{28,448},... | collective-permute-start | bytes 24584 | tf_op jit(solution)/shard_map/ppermute | solution.py:429
  281.6 1.4 copy-start.2
Sparse Core Ops, SparseCore 0:
  12.4 46.0 all-gather.4
  60.7 35.2 all-gather.6
  154.6 33.8 all-gather.8
  210.4 34.7 all-gather.10

commit v2 on v1

--- a/solution.py
+++ b/solution.py
@@ -27,6 +27,7 @@
 SCALE = HEAD ** (-0.5)
 LOG2E = 1.4426950408889634
 QBLOCK = 256
+MICRO = 1_150_000_000
 
 F32 = jnp.float32
 BF16 = jnp.bfloat16
@@ -54,7 +55,7 @@
     return lax.broadcasted_iota(jnp.int32, shape, dim)
 
 
-def call(kernel, ins, outs, scratch=(), limit=32):
+def call(kernel, ins, outs, scratch=(), limit=32, micros=1):
     views = [item[1:] if isinstance(item, tuple) else None for item in ins]
     arrays = [item[0] if isinstance(item, tuple) else item for item in ins]
     scalars = [a.ndim == 1 for a in arrays]
@@ -73,6 +74,7 @@
         in_specs=[pl.BlockSpec(memory_space=pltpu.SMEM if flat else pltpu.VMEM) for flat in scalars],
         out_specs=[pl.BlockSpec(memory_space=pltpu.VMEM) for _ in outs],
         scratch_shapes=list(scratch),
+        cost_estimate=pl.CostEstimate(flops=micros * MICRO, bytes_accessed=0, transcendentals=0),
         compiler_params=pltpu.CompilerParams(vmem_limit_bytes=limit * 1024 * 1024),
     )(*arrays)
 
@@ -103,7 +105,10 @@
     return jnp.where(iota((PATCHES * SLOTS, ROWS), 0) == code, 1.0, 0.0).astype(BF16)
 
 
-def prepare_kernel(points, sources, project_z, project_h, output_z, output_h, mine, weights):
+def prepare_kernel(
+    points, cotangent, targets, sources, project_z, project_h, output_z, output_h, mine, weights, grads
+):
+    grads[...] = dot(place_rows(targets), cotangent[...]).astype(BF16)
     mine[:ROWS, :] = points[...]
     source = sources[...]
     digits = jnp.concatenate([source // ROWS, source % ROWS], axis=1).astype(F32)
@@ -190,26 +195,26 @@
     ]
 
 
-def mix_kernel(targets, attended, points, cotangent, shared, send):
+def mix_kernel(targets, attended, points, shared, send):
     place = place_rows(targets)
     weights = halves(shared, 0, WIDTH // 2)
     mixed = jnp.concatenate([dot(attended[...], w, 0, 0) for w in weights], axis=1)
     mixed = points[...].astype(F32) + mixed
-    send[:, :WIDTH] = dot(place, mixed.astype(BF16)).astype(BF16)
-    send[:, WIDTH:] = dot(place, cotangent[...]).astype(BF16)
-
-
-def project_kernel(arrived, plan, project, output, send, rows_out, grads_out):
-    gathered = dot(plan[: PATCHES * SLOTS, :], arrived[...], 0, 0).astype(BF16)
-    mixed = gathered[:, :WIDTH]
-    grad = gathered[:, WIDTH:]
-    grads_out[...] = grad
-    rows_out[...] = mixed
+    send[...] = dot(place, mixed.astype(BF16)).astype(BF16)
+
+
+def collect_kernel(arrived, plan, grads):
+    grads[...] = dot(plan[: PATCHES * SLOTS, :], arrived[...], 0, 0).astype(BF16)
+
+
+def project_kernel(arrived, plan, project, output, grads, send, rows):
+    mixed = dot(plan[: PATCHES * SLOTS, :], arrived[...], 0, 0).astype(BF16)
+    rows[...] = mixed
+    low, high = halves(output, 0, WIDTH // 2)
+    grad_attended = dot(grads[:, : WIDTH // 2], low, 1, 1) + dot(grads[:, WIDTH // 2 :], high, 1, 1)
     unit, _ = normalize(mixed.astype(F32))
     unit = unit.astype(BF16)
     projected = [dot(unit, w) for w in halves(project, 0, 3 * WIDTH // 2)]
-    low, high = halves(output, 0, WIDTH // 2)
-    grad_attended = dot(grad[:, : WIDTH // 2], low, 1, 1) + dot(grad[:, WIDTH // 2 :], high, 1, 1)
     for k in range(MEMBERS):
         half, t = projected[k % 2], k // 2
         first = WIDTH // 2 + t * 2 * PAIR
@@ -332,10 +337,15 @@
     targets = zorder_targets[0]
     sources = hilbert_sources[0]
 
-    mine, weights = call(
+    targets = targets[None, :]
+    mine, weights, send_grads = call(
         prepare_kernel,
-        [rows, sources[None, :], zorder_project, hilbert_project, zorder_output, hilbert_output],
-        [((ROWS + META, WIDTH), BF16), ((2, SHARE, 4 * WIDTH), BF16)],
+        [rows, cot, targets, sources[None, :], zorder_project, hilbert_project, zorder_output, hilbert_output],
+        [
+            ((ROWS + META, WIDTH), BF16),
+            ((2, SHARE, 4 * WIDTH), BF16),
+            ((PATCHES * SLOTS, WIDTH), BF16),
+        ],
     )
     gathered = lax.all_gather(mine, GROUP, axis=0, tiled=True)
     weights = exchange(weights, "core").reshape(MEMBERS, 4 * WIDTH)
@@ -356,7 +366,9 @@
     project_z = lax.all_gather(weights[:, :third], ("x", "core"), axis=0, tiled=True)
     project_z = project_z.reshape(MEMBERS, ROWS, third)
 
-    targets = targets[None, :]
+    send_grads, own = lax.optimization_barrier((send_grads, own))
+    arrived_grads = exchange(send_grads.reshape(PATCHES, SLOTS, WIDTH), ACROSS)
+
     qkv_z, attended, plan = call(
         forward_kernel,
         [scal, gathered, own],
@@ -366,27 +378,36 @@
             ((PATCHES * SLOTS + 2 * MEMBERS, ROWS), BF16),
         ],
         [pltpu.VMEM((PAIR, PATCH), F32)],
-    )
-
+        micros=8,
+    )
+
+    attended, arrived_grads = lax.optimization_barrier((attended, arrived_grads))
+    (grads_h,) = call(
+        collect_kernel,
+        [arrived_grads.reshape(PATCHES * SLOTS, WIDTH), plan],
+        [((ROWS, WIDTH), BF16)],
+    )
     attended = exchange(attended, GROUP).reshape(WIDTH, ROWS)
+    attended, grads_h, shared = lax.optimization_barrier((attended, grads_h, shared))
+    all_grads_h = lax.all_gather(grads_h, GROUP, axis=0, tiled=True)
     (send,) = call(
         mix_kernel,
-        [targets, attended, rows, cot, (shared, *OUTPUT_Z)],
-        [((PATCHES * SLOTS, 2 * WIDTH), BF16)],
-    )
-
-    arrived = exchange(send.reshape(PATCHES, SLOTS, 2 * WIDTH), ACROSS)
-    send, rows_h, grads_h = call(
+        [targets, attended, rows, (shared, *OUTPUT_Z)],
+        [((PATCHES * SLOTS, WIDTH), BF16)],
+    )
+
+    arrived = exchange(send.reshape(PATCHES, SLOTS, WIDTH), ACROSS)
+    send, rows_h = call(
         project_kernel,
         [
-            arrived.reshape(PATCHES * SLOTS, 2 * WIDTH),
+            arrived.reshape(PATCHES * SLOTS, WIDTH),
             plan,
             (shared, *PROJECT_H),
             (shared, *OUTPUT_H),
+            grads_h,
         ],
-        [((MEMBERS, 2 * ROWS, ROWS), BF16), ((ROWS, WIDTH), BF16), ((ROWS, WIDTH), BF16)],
-    )
-    all_grads_h = lax.all_gather(grads_h, GROUP, axis=0, tiled=True)
+        [((MEMBERS, 2 * ROWS, ROWS), BF16), ((ROWS, WIDTH), BF16)],
+    )
 
     arrived = exchange(send, GROUP)
     sums = [
@@ -399,6 +420,7 @@
         [arrived, plan],
         [((MEMBERS, 3 * PAIR, ROWS), BF16), ((PAIR, PATCH), BF16)],
         [pltpu.VMEM((PATCH, 4 * PAIR), BF16), pltpu.VMEM((PAIR, PATCH), BF16)] + sums,
+        micros=11,
     )
 
     arrived = exchange(send, GROUP)
@@ -424,6 +446,7 @@
         [scal, arrived, qkv_z],
         [((MEMBERS, 3 * PAIR, ROWS), BF16)],
         [pltpu.VMEM((PAIR, PATCH), BF16)] + sums,
+        micros=11,
     )
     send, term, beside = lax.optimization_barrier((send, term, beside))
     term = lax.ppermute(

time: 293 us -> 285 us (0.973)
  waiting for transfers between devices: 65.6 us -> 47.8 us
  starting transfers between devices: 48.6 us -> 64.7 us
  blocking collectives: 107 us -> 99.7 us
    all_to_all x5 -> x6, starting transfers between devices: 38.1 us -> 54.6 us  [exchange(): return lax.all_to_all(value, axes, split_axis=0, concat_axis=0, tiled=True)]
    all_to_all x5 -> x6, waiting for transfers between devices: 42.5 us -> 33.9 us  [exchange(): return lax.all_to_all(value, axes, split_axis=0, concat_axis=0, tiled=True)]
    all_gather x1, waiting for transfers between devices: 7.87 us -> 0.01 us  [per_device(): lax.all_gather(weights[:, third:], ('x', 'core'), axis=0, tiled=True)]
    all_to_all x3, blocking collectives: 69.4 us -> 61.9 us  [exchange(): return lax.all_to_all(value, axes, split_axis=0, concat_axis=0, tiled=True)]
    pallas_call x9 -> x10, Pallas kernels: 38.1 us -> 40.6 us  [call(): pl.pallas_call(body, out_shape=[jax.ShapeDtypeStruct(shape, dtype) for sh...]
    unnamed x45 -> x43, local copies, waits for them, and re-layouts: 15.5 us -> 13.7 us
  transfers between devices with their start and end apart: 12 -> 13, of which waited for: 9 -> 8; matrix products, arithmetic and copies ran while one was open for 1% -> 1% of each run, Pallas kernels for 11% -> 12%
where the time goes in v2:
time: 285 us; the launch traced here: 283 us
  blocking collectives  99.7 us (35%)
  starting transfers between devices  64.7 us (23%)
  waiting for transfers between devices  47.8 us (17%)
  Pallas kernels  40.6 us (14%)
  local copies, waits for them, and re-layouts  16.4 us (6%)
  between operations  13.9 us (5%)
    all_to_all x3, blocking collectives, exchange(): return lax.all_to_all(value, axes, split_axis=0, concat_axis=0, tiled=True)  61.9 us
    all_to_all x6, starting transfers between devices, exchange(): return lax.all_to_all(value, axes, split_axis=0, concat_axis=0, tiled=True)  54.6 us
    pallas_call x10, Pallas kernels, call(): pl.pallas_call(body, out_shape=[jax.ShapeDtypeStruct(shape, dtype) for sh...  40.6 us
    all_to_all x6, waiting for transfers between devices, exchange(): return lax.all_to_all(value, axes, split_axis=0, concat_axis=0, tiled=True)  33.9 us
    all_gather x1, blocking collectives, per_device(): weights = lax.all_gather(weights, ('zh', 'zl'), axis=0, tiled=True)  27 us
    unnamed x43, local copies, waits for them, and re-layouts  13.7 us
    all_gather x1, blocking collectives, per_device(): own = lax.all_gather(own, 'x', axis=0, tiled=True)  10.7 us
    all_gather x1, waiting for transfers between devices, per_device(): all_grads_h = lax.all_gather(grads_h, GROUP, axis=0, tiled=True)  5.85 us
  transfers between devices with their start and end apart: 13, of which 8 were waited for; matrix products, arithmetic and copies ran while one was open for 1% of the time, Pallas kernels for 12%

profile of v2, /device:TPU:1, one launch (start us, length us, event | category | flops | bytes accessed | tf_op | source)
XLA Modules:
  0.0 283.2 jit_solution(18418224940230710985)
XLA Ops:
  7.2 0.0 all-gather.5.cloned.1.call-start
  7.2 0.0 copy-start.6
  7.2 0.9 copy-done.6
  8.1 0.9 copy-done.7
  9.0 0.7 copy-done.10
  9.7 0.7 copy-done.11
  10.4 0.7 copy-done.12
  11.1 0.7 copy-done.13
  11.8 0.7 copy-done.14
  12.5 0.7 copy-done.15
  13.1 1.1 shard_map.104
  14.2 0.0 all-gather.5.cloned.1.call-update
  14.3 0.0 all-gather.7.cloned.1.call-start
  14.3 10.3 %all_to_all.45 = bf16[2,4,2048]{2,1,0:T(4,128)(2,1)S(1)} all-to-all(bf16[2,4,2048]{2,1,0:T(4,128)(2,1)S(1)} %get-tuple-element.29), channel_id=1, replica_groups=mesh['x'=4,'zh'=4,'zl'=4,'core'=2,'scene'=4] {'core'}, dimensions={0} | all-to-all | bytes 65536 | tf_op jit(solution)/shard_map/all_to_all | solution.py:325
  24.6 27.0 %all_gather.19 = bf16[128,2048]{1,0:T(8,128)(2,1)S(1)} all-gather(bf16[8,2048]{1,0:T(8,128)(2,1)S(1)} %reshape.31), channel_id=1, replica_groups=mesh['x'=4,'zh'=4,'zl'=4,'core'=2,'scene'=4] {'zh','zl'}, dimensions={0}, use_global_device_ids=true | all-gather | bytes 557056 | tf_op jit(solution)/shard_map/all_gather | solution.py:352
  51.6 0.8 slice.8
  52.4 0.0 all-gather.7.cloned.1.call-update
  52.5 0.1 pad.2.clone
  52.6 0.1 constant_dynamic-slice_fusion
  52.7 10.7 %all_gather.20.refs_2_ = bf16[512,256]{1,0:T(8,128)(2,1)S(1)} all-gather(bf16[128,256]{1,0:T(8,128)(2,1)S(1)} %maximum_maximum_fusion), channel_id=1, replica_groups=mesh['x'=4,'zh'=4,'zl'=4,'core'=2,'scene'=4] {'x'}, dimensions={0}, use_global_device_ids=true | all-gather | bytes 327680 | tf_op jit(solution)/shard_map/all_gather | solution.py:363
  63.4 7.2 %all-to-all-start.1 = ((bf16[16,16,512]{2,1,0:T(8,128)(2,1)}), bf16[16,16,512]{2,1,0:T(8,128)(2,1)S(1)}, u32[]{:S(2)}, u32[]{:S(2)}) async-start(bf16[16,16,512]{2,1,0:T(8,128)(2,1)} %bitcast.5), calls=%async_computation.1 | async-start | bytes 524288 | tf_op jit(solution)/shard_map/all_to_all | solution.py:325
  70.7 0.1 pad_add_fusion.refs_0_
  70.7 1.3 copy-done.5
  72.0 8.8 %shard_map.105 = (bf16[1024,256]{1,0:T(8,128)(2,1)S(1)}, bf16[8,64,128]{2,1,0:T(8,128)(2,1)}, bf16[272,128]{1,0:T(8,128)(2,1)S(1)}) custom-call(s32[18]{0:T(128)S(1)} %pad_add_fusion.refs_0_, bf16[1152,512]{1,0:T(8,128)(2,1)S(1)} %copy-done.5, bf16[512,256]{1,0:T(8,128)(2,1)S(1)} %all_gather.20.refs_2_), custom_call_target="tpu_custom_call" | custom-call | flops 9200000000 | tf_op jit(solution)/shard_map/pallas_call | solution.py:71
  80.8 0.8 copy-done.17
  81.6 5.4 %all-to-all-done.1 = bf16[16,16,512]{2,1,0:T(8,128)(2,1)S(1)} async-done(((bf16[16,16,512]{2,1,0:T(8,128)(2,1)}), bf16[16,16,512]{2,1,0:T(8,128)(2,1)S(1)}, u32[]{:S(2)}, u32[]{:S(2)}) %all-to-all-start.1) | async-done | bytes 262176 | tf_op jit(solution)/shard_map/all_to_all | solution.py:325
  87.1 15.0 %all-to-all-start.2 = ((bf16[8,64,128]{2,1,0:T(8,128)(2,1)}), bf16[8,64,128]{2,1,0:T(8,128)(2,1)S(1)}, u32[]{:S(2)}, u32[]{:S(2)}) async-start(bf16[8,64,128]{2,1,0:T(8,128)(2,1)} %get-tuple-element.33), calls=%async_computation.2 | async-start | bytes 262144 | tf_op jit(solution)/shard_map/all_to_all | solution.py:325
  102.1 0.9 shard_map.106.refs_4_.refs_3_
  103.0 4.9 %all-to-all-done.2 = bf16[8,64,128]{2,1,0:T(8,128)(2,1)S(1)} async-done(((bf16[8,64,128]{2,1,0:T(8,128)(2,1)}), bf16[8,64,128]{2,1,0:T(8,128)(2,1)S(1)}, u32[]{:S(2)}, u32[]{:S(2)}) %all-to-all-start.2) | async-done | bytes 131104 | tf_op jit(solution)/shard_map/all_to_all | solution.py:325
  107.9 0.0 copy-done.16
  107.9 1.7 copy-done
  109.6 0.5 shard_map.107
  110.1 24.8 %all_to_all.46 = bf16[16,16,512]{2,1,0:T(8,128)(2,1)S(1)} all-to-all(bf16[16,16,512]{2,1,0:T(8,128)(2,1)S(1)} %bitcast.21), channel_id=1, replica_groups=mesh['x'=4,'zh'=4,'zl'=4,'core'=2,'scene'=4] {'x','zh'}, dimensions={0} | all-to-all | bytes 524288 | tf_op jit(solution)/shard_map/all_to_all | solution.py:325
  134.9 1.6 shard_map.108
  136.6 0.8 copy-done.3
  137.4 8.4 %all-to-all-start.4 = ((bf16[8,256,128]{2,1,0:T(8,128)(2,1)}), bf16[8,256,128]{2,1,0:T(8,128)(2,1)S(1)}, u32[]{:S(2)}, u32[]{:S(2)}) async-start(bf16[8,256,128]{2,1,0:T(8,128)(2,1)} %copy-done.3), calls=%async_computation.4 | async-start | bytes 1048576 | tf_op jit(solution)/shard_map/all_to_all | solution.py:325
  145.7 0.0 all-gather.9.cloned.1.call-start
  145.7 0.7 all-gather.9.cloned.1.call-update
  146.5 13.8 %all-to-all-done.4.refs_0_ = bf16[8,256,128]{2,1,0:T(8,128)(2,1)S(1)} async-done(((bf16[8,256,128]{2,1,0:T(8,128)(2,1)}), bf16[8,256,128]{2,1,0:T(8,128)(2,1)S(1)}, u32[]{:S(2)}, u32[]{:S(2)}) %all-to-all-start.4) | async-done | bytes 524320 | tf_op jit(solution)/shard_map/all_to_all | solution.py:325
  160.2 11.9 %shard_map.109 = (bf16[8,192,128]{2,1,0:T(8,128)(2,1)}, bf16[64,1024]{1,0:T(8,128)(2,1)S(1)}) custom-call(bf16[8,256,128]{2,1,0:T(8,128)(2,1)S(1)} %all-to-all-done.4.refs_0_, bf16[272,128]{1,0:T(8,128)(2,1)S(1)} %get-tuple-element.35.refs_1_.refs_4_), custom_call_target="tpu_custom_call" | custom-call | flops 12650000384 | tf_op jit(solution)/shard_map/pallas_call | solution.py:71
  172.1 4.2 %all-to-all-start.5 = ((bf16[8,192,128]{2,1,0:T(8,128)(2,1)}), bf16[8,192,128]{2,1,0:T(8,128)(2,1)S(1)}, u32[]{:S(2)}, u32[]{:S(2)}) async-start(bf16[8,192,128]{2,1,0:T(8,128)(2,1)} %get-tuple-element.40), calls=%async_computation.5 | async-start | bytes 786432 | tf_op jit(solution)/shard_map/all_to_all | solution.py:325
  176.4 5.8 %all-gather.9.cloned.1.call-done.refs_6_ = bf16[1024,512]{1,0:T(8,128)(2,1)} async-done(((bf16[128,512]{1,0:T(8,128)(2,1)}), bf16[1024,512]{1,0:T(8,128)(2,1)}) %all-gather.9.cloned.1.call-update) | async-done | bytes 1048592 | tf_op jit(solution)/shard_map/all_gather | solution.py:392
  182.2 6.9 %all-to-all-done.5.refs_0_ = bf16[8,192,128]{2,1,0:T(8,128)(2,1)S(1)} async-done(((bf16[8,192,128]{2,1,0:T(8,128)(2,1)}), bf16[8,192,128]{2,1,0:T(8,128)(2,1)S(1)}, u32[]{:S(2)}, u32[]{:S(2)}) %all-to-all-start.5) | async-done | bytes 393248 | tf_op jit(solution)/shard_map/all_to_all | solution.py:325
  189.2 1.2 copy-done.2
  190.4 2.0 shard_map.110
  192.4 26.8 %all_to_all.47.refs_0_ = bf16[16,24,512]{2,1,0:T(8,128)(2,1)S(1)} all-to-all(bf16[16,24,512]{2,1,0:T(8,128)(2,1)S(1)} %shard_map.110), channel_id=1, replica_groups=mesh['x'=4,'zh'=4,'zl'=4,'core'=2,'scene'=4] {'x','zh'}, dimensions={0} | all-to-all | bytes 786432 | tf_op jit(solution)/shard_map/all_to_all | solution.py:325
  219.3 1.3 shard_map.111
  220.6 13.6 %all-to-all-start.7 = ((bf16[8,64,128]{2,1,0:T(8,128)(2,1)}), bf16[8,64,128]{2,1,0:T(8,128)(2,1)S(1)}, u32[]{:S(2)}, u32[]{:S(2)}) async-start(bf16[8,64,128]{2,1,0:T(8,128)(2,1)} %bitcast.11), calls=%async_computation.7 | async-start | bytes 262144 | tf_op jit(solution)/shard_map/all_to_all | solution.py:325
  234.2 1.6 slice.9
  235.8 0.0 all-gather.11.cloned.1.call-update
  235.8 2.9 %collective-permute-start = (f32[4,512]{1,0:T(4,128)S(1)}, f32[4,512]{1,0:T(4,128)S(1)}, u32[]{:S(2)}, u32[]{:S(2)}) collective-permute-start(f32[4,512]{1,0:T(4,128)S(1)} %get-tuple-element.44), channel_id=1, source_target_pairs={{0,1},{1,0},{2,3},{3,2},{4,5},{5,4},{6,7},{7,6},{8,9},{9,8},{10,11... | collective-permute-start | bytes 24584 | tf_op jit(solution)/shard_map/ppermute | solution.py:439
  238.7 1.8 collective-permute-done
  240.5 0.0 all-to-all-done.7.refs_1_
  240.5 3.6 %collective-permute-start.1 = (f32[4,512]{1,0:T(4,128)S(1)}, f32[4,512]{1,0:T(4,128)S(1)}, u32[]{:S(2)}, u32[]{:S(2)}) collective-permute-start(f32[4,512]{1,0:T(4,128)S(1)} %add.24), channel_id=1, source_target_pairs={{0,2},{1,3},{2,0},{3,1},{4,6},{5,7},{6,4},{7,5},{8,10},{9,11},{10,... | collective-permute-start | bytes 24584 | tf_op jit(solution)/shard_map/ppermute | solution.py:443
  244.1 0.0 copy-start.9
  244.1 11.0 %shard_map.112 = bf16[8,192,128]{2,1,0:T(8,128)(2,1)} custom-call(s32[18]{0:T(128)S(1)} %pad_add_fusion.refs_0_, bf16[8,64,128]{2,1,0:T(8,128)(2,1)S(1)} %all-to-all-done.7.refs_1_, bf16[1024,256]{1,0:T(8,128)(2,1)S(1)} %copy-done.18), custom_call_target="tpu_custom_call" | custom-call | flops 12650000384 | tf_op jit(solution)/shard_map/pallas_call | solution.py:71
  255.1 0.0 collective-permute-done.1
  255.1 6.2 %all-to-all-start.8 = ((bf16[8,192,128]{2,1,0:T(8,128)(2,1)}), bf16[8,192,128]{2,1,0:T(8,128)(2,1)S(1)}, u32[]{:S(2)}, u32[]{:S(2)}) async-start(bf16[8,192,128]{2,1,0:T(8,128)(2,1)} %shard_map.112), calls=%async_computation.8 | async-start | bytes 786432 | tf_op jit(solution)/shard_map/all_to_all | solution.py:325
  261.3 3.5 %collective-permute-start.2 = (f32[4,512]{1,0:T(4,128)S(1)}, f32[4,512]{1,0:T(4,128)S(1)}, u32[]{:S(2)}, u32[]{:S(2)}) collective-permute-start(f32[4,512]{1,0:T(4,128)S(1)} %add.25), channel_id=1, source_target_pairs={{0,0},{4,64},{8,128},{12,192},{16,256},{20,320},{24,384},{28,448},... | collective-permute-start | bytes 24584 | tf_op jit(solution)/shard_map/ppermute | solution.py:452
  264.9 5.5 %collective-permute-done.2 = f32[4,512]{1,0:T(4,128)S(1)} collective-permute-done((f32[4,512]{1,0:T(4,128)S(1)}, f32[4,512]{1,0:T(4,128)S(1)}, u32[]{:S(2)}, u32[]{:S(2)}) %collective-permute-start.2) | collective-permute-done | bytes 8224 | tf_op jit(solution)/shard_map/ppermute | solution.py:452
  270.4 2.9 %all-to-all-done.8.refs_0_ = bf16[8,192,128]{2,1,0:T(8,128)(2,1)S(1)} async-done(((bf16[8,192,128]{2,1,0:T(8,128)(2,1)}), bf16[8,192,128]{2,1,0:T(8,128)(2,1)S(1)}, u32[]{:S(2)}, u32[]{:S(2)}) %all-to-all-start.8) | async-done | bytes 393248 | tf_op jit(solution)/shard_map/all_to_all | solution.py:325
  273.3 1.4 copy-done.4
  274.7 1.4 shard_map.113
  276.1 0.6 copy.12
  (35 shorter events, 0.1 us)
Async XLA Ops:
  7.2 63.6 %all-gather.5.cloned.1.call-start = ((), (), s32[]{:S(2)}) async-start(), calls=%async_computation.9 | async-start | bytes 1327104 | tf_op jit(solution)/shard_map/all_gather | solution.py:350
  7.2 0.9 copy-start.6
  8.1 0.9 copy-start.7
  9.0 0.7 copy-start.10
  9.7 0.7 copy-start.11
  10.4 0.7 copy-start.12
  11.1 0.7 copy-start.13
  11.8 0.7 copy-start.14
  12.5 0.7 copy-start.15
  14.2 56.4 %copy-start.20 = (s32[1,16]{1,0:T(1,128)S(1)}, s32[1,16]{1,0:T(1,128)}, u32[]{:S(2)}) copy-start(s32[1,16]{1,0:T(1,128)} %param.11) | copy-start | bytes 196
  14.3 93.6 %all-gather.7.cloned.1.call-start = ((), (), s32[]{:S(2)}) async-start(), calls=%async_computation.10 | async-start | bytes 2949120 | tf_op jit(solution)/shard_map/all_gather | solution.py:364
  51.6 1.1 copy-start.19
  63.4 23.6 %all-to-all-start.1 = ((bf16[16,16,512]{2,1,0:T(8,128)(2,1)}), bf16[16,16,512]{2,1,0:T(8,128)(2,1)S(1)}, u32[]{:S(2)}, u32[]{:S(2)}) async-start(bf16[16,16,512]{2,1,0:T(8,128)(2,1)} %bitcast.5), calls=%async_computation.1 | async-start | bytes 524288 | tf_op jit(solution)/shard_map/all_to_all | solution.py:325
  70.7 1.3 copy-start.5
  80.8 0.8 copy-start.17
  87.1 20.8 %all-to-all-start.2 = ((bf16[8,64,128]{2,1,0:T(8,128)(2,1)}), bf16[8,64,128]{2,1,0:T(8,128)(2,1)S(1)}, u32[]{:S(2)}, u32[]{:S(2)}) async-start(bf16[8,64,128]{2,1,0:T(8,128)(2,1)} %get-tuple-element.33), calls=%async_computation.2 | async-start | bytes 262144 | tf_op jit(solution)/shard_map/all_to_all | solution.py:325
  102.1 5.8 %copy-start.8 = (bf16[1,128,512]{2,1,0:T(8,128)(2,1)S(1)}, bf16[1,128,512]{2,1,0:T(8,128)(2,1)}, u32[]{:S(2)}) copy-start(bf16[1,128,512]{2,1,0:T(8,128)(2,1)} %param.9) | copy-start | bytes 393220
  102.1 5.8 %copy-start.16 = (s32[1,128]{1,0:T(1,128)S(1)}, s32[1,128]{1,0:T(1,128)}, u32[]{:S(2)}) copy-start(s32[1,128]{1,0:T(1,128)} %refs_1_.1) | copy-start | bytes 1540
  107.9 1.7 copy-start
  109.6 25.3 %copy-start.1 = (bf16[1024,1280]{1,0:T(8,128)(2,1)S(1)}, bf16[1024,1280]{1,0:T(8,128)(2,1)}, u32[]{:S(2)}) copy-start(bf16[1024,1280]{1,0:T(8,128)(2,1)} %all-gather.7.cloned.1.call-done) | copy-start | bytes 7864324
  136.6 0.8 copy-start.3
  137.4 22.9 %all-to-all-start.4 = ((bf16[8,256,128]{2,1,0:T(8,128)(2,1)}), bf16[8,256,128]{2,1,0:T(8,128)(2,1)S(1)}, u32[]{:S(2)}, u32[]{:S(2)}) async-start(bf16[8,256,128]{2,1,0:T(8,128)(2,1)} %copy-done.3), calls=%async_computation.4 | async-start | bytes 1048576 | tf_op jit(solution)/shard_map/all_to_all | solution.py:325
  145.7 36.5 %all-gather.9.cloned.1.call-start = ((), (), s32[]{:S(2)}) async-start(), calls=%async_computation.11 | async-start | bytes 1179648 | tf_op jit(solution)/shard_map/all_gather | solution.py:392
  172.1 17.0 %all-to-all-start.5 = ((bf16[8,192,128]{2,1,0:T(8,128)(2,1)}), bf16[8,192,128]{2,1,0:T(8,128)(2,1)S(1)}, u32[]{:S(2)}, u32[]{:S(2)}) async-start(bf16[8,192,128]{2,1,0:T(8,128)(2,1)} %get-tuple-element.40), calls=%async_computation.5 | async-start | bytes 786432 | tf_op jit(solution)/shard_map/all_to_all | solution.py:325
  189.2 1.2 copy-start.2
  219.2 24.8 %copy-start.18 = (bf16[1024,256]{1,0:T(8,128)(2,1)S(1)}, bf16[1024,256]{1,0:T(8,128)(2,1)}, u32[]{:S(2)}) copy-start(bf16[1024,256]{1,0:T(8,128)(2,1)} %copy-done.17) | copy-start | bytes 1572868
  220.6 19.9 %all-to-all-start.7 = ((bf16[8,64,128]{2,1,0:T(8,128)(2,1)}), bf16[8,64,128]{2,1,0:T(8,128)(2,1)S(1)}, u32[]{:S(2)}, u32[]{:S(2)}) async-start(bf16[8,64,128]{2,1,0:T(8,128)(2,1)} %bitcast.11), calls=%async_computation.7 | async-start | bytes 262144 | tf_op jit(solution)/shard_map/all_to_all | solution.py:325
  234.2 36.3 %all-gather.11.cloned.1.call-start = ((), (), s32[]{:S(2)}) async-start(), calls=%async_computation.12 | async-start | bytes 1769472 | tf_op jit(solution)/shard_map/all_gather | solution.py:366
  235.8 4.7 %collective-permute-start = (f32[4,512]{1,0:T(4,128)S(1)}, f32[4,512]{1,0:T(4,128)S(1)}, u32[]{:S(2)}, u32[]{:S(2)}) collective-permute-start(f32[4,512]{1,0:T(4,128)S(1)} %get-tuple-element.44), channel_id=1, source_target_pairs={{0,1},{1,0},{2,3},{3,2},{4,5},{5,4},{6,7},{7,6},{8,9},{9,8},{10,11... | collective-permute-start | bytes 24584 | tf_op jit(solution)/shard_map/ppermute | solution.py:439
  240.5 14.6 %collective-permute-start.1 = (f32[4,512]{1,0:T(4,128)S(1)}, f32[4,512]{1,0:T(4,128)S(1)}, u32[]{:S(2)}, u32[]{:S(2)}) collective-permute-start(f32[4,512]{1,0:T(4,128)S(1)} %add.24), channel_id=1, source_target_pairs={{0,2},{1,3},{2,0},{3,1},{4,6},{5,7},{6,4},{7,5},{8,10},{9,11},{10,... | collective-permute-start | bytes 24584 | tf_op jit(solution)/shard_map/ppermute | solution.py:443
  244.1 29.2 %copy-start.9 = (bf16[1,128,512]{2,1,0:T(8,128)(2,1)S(1)}, bf16[1,128,512]{2,1,0:T(8,128)(2,1)}, u32[]{:S(2)}) copy-start(bf16[1,128,512]{2,1,0:T(8,128)(2,1)} %param.9) | copy-start | bytes 393220
  255.1 18.2 %all-to-all-start.8 = ((bf16[8,192,128]{2,1,0:T(8,128)(2,1)}), bf16[8,192,128]{2,1,0:T(8,128)(2,1)S(1)}, u32[]{:S(2)}, u32[]{:S(2)}) async-start(bf16[8,192,128]{2,1,0:T(8,128)(2,1)} %shard_map.112), calls=%async_computation.8 | async-start | bytes 786432 | tf_op jit(solution)/shard_map/all_to_all | solution.py:325
  261.3 9.1 %collective-permute-start.2 = (f32[4,512]{1,0:T(4,128)S(1)}, f32[4,512]{1,0:T(4,128)S(1)}, u32[]{:S(2)}, u32[]{:S(2)}) collective-permute-start(f32[4,512]{1,0:T(4,128)S(1)} %add.25), channel_id=1, source_target_pairs={{0,0},{4,64},{8,128},{12,192},{16,256},{20,320},{24,384},{28,448},... | collective-permute-start | bytes 24584 | tf_op jit(solution)/shard_map/ppermute | solution.py:452
  273.3 1.4 copy-start.4
Sparse Core Ops, SparseCore 0:
  14.4 46.0 all-gather.4
  62.6 35.9 all-gather.6
  148.6 33.5 all-gather.8
  236.8 24.2 all-gather.10

commit v3 on v2

--- a/solution.py
+++ b/solution.py
@@ -26,7 +26,7 @@
 NEGATIVE = -1e30
 SCALE = HEAD ** (-0.5)
 LOG2E = 1.4426950408889634
-QBLOCK = 256
+QBLOCK = 1024
 MICRO = 1_150_000_000
 
 F32 = jnp.float32
@@ -55,13 +55,25 @@
     return lax.broadcasted_iota(jnp.int32, shape, dim)
 
 
-def call(kernel, ins, outs, scratch=(), limit=32, micros=1):
+def call(kernel, ins, outs, scratch=(), limit=32, micros=1, pull=False):
     views = [item[1:] if isinstance(item, tuple) else None for item in ins]
     arrays = [item[0] if isinstance(item, tuple) else item for item in ins]
     scalars = [a.ndim == 1 for a in arrays]
+    held = [pltpu.VMEM(a.shape, a.dtype) for a in arrays] if pull else []
+    held += [pltpu.SemaphoreType.DMA((len(arrays),))] if pull else []
 
     def body(*refs):
         given = list(refs)
+        if pull:
+            given, buffers, sems = given[: -len(held)], given[-len(held) : -1], given[-1]
+            copies = [
+                pltpu.make_async_copy(refs[k], buffer, sems.at[k]) for k, buffer in enumerate(buffers)
+            ]
+            for copy in copies:
+                copy.start()
+            for copy in copies:
+                copy.wait()
+            given[: len(buffers)] = buffers
         for k, view in enumerate(views):
             if view is not None:
                 lead = (slice(None),) * (len(arrays[k].shape) - 1)
@@ -71,9 +83,12 @@
     return pl.pallas_call(
         body,
         out_shape=[jax.ShapeDtypeStruct(shape, dtype) for shape, dtype in outs],
-        in_specs=[pl.BlockSpec(memory_space=pltpu.SMEM if flat else pltpu.VMEM) for flat in scalars],
+        in_specs=[
+            pl.BlockSpec(memory_space=pltpu.SMEM if flat else pl.ANY if pull else pltpu.VMEM)
+            for flat in scalars
+        ],
         out_specs=[pl.BlockSpec(memory_space=pltpu.VMEM) for _ in outs],
-        scratch_shapes=list(scratch),
+        scratch_shapes=list(scratch) + held,
         cost_estimate=pl.CostEstimate(flops=micros * MICRO, bytes_accessed=0, transcendentals=0),
         compiler_params=pltpu.CompilerParams(vmem_limit_bytes=limit * 1024 * 1024),
     )(*arrays)
@@ -346,6 +361,8 @@
             ((2, SHARE, 4 * WIDTH), BF16),
             ((PATCHES * SLOTS, WIDTH), BF16),
         ],
+        limit=60,
+        pull=True,
     )
     gathered = lax.all_gather(mine, GROUP, axis=0, tiled=True)
     weights = exchange(weights, "core").reshape(MEMBERS, 4 * WIDTH)
@@ -436,11 +453,12 @@
         [arrived, targets, (shared, *OUTPUT_Z)],
         [((ROWS, WIDTH), BF16), ((WIDTH, ROWS), BF16), ((SHARE, WIDTH), F32)],
     )
-    beside = lax.ppermute(term, "scene", [(i, i ^ 1) for i in range(SCENES)])
+    term = lax.ppermute(
+        term,
+        PTS,
+        [(r * MEMBERS + j, j * PATCHES + r) for r in range(PATCHES) for j in range(MEMBERS)],
+    )
     arrived = exchange(send.reshape(MEMBERS, PAIR, ROWS), GROUP)
-    arrived, beside = lax.optimization_barrier((arrived, beside))
-    term = term + beside
-    beside = lax.ppermute(term, "scene", [(i, i ^ 2) for i in range(SCENES)])
     (send,) = call(
         backward_z_kernel,
         [scal, arrived, qkv_z],
@@ -448,12 +466,9 @@
         [pltpu.VMEM((PAIR, PATCH), BF16)] + sums,
         micros=11,
     )
-    send, term, beside = lax.optimization_barrier((send, term, beside))
-    term = lax.ppermute(
-        term + beside,
-        PTS,
-        [(r * MEMBERS + j, j * PATCHES + r) for r in range(PATCHES) for j in range(MEMBERS)],
-    )
+    send, term = lax.optimization_barrier((send, term))
+    for k in (1, 2):
+        term = term + lax.ppermute(term, "scene", [(i, i ^ k) for i in range(SCENES)])
 
     arrived = exchange(send, GROUP)
     (out,) = call(finish_kernel, [arrived, project_z, rows, grad_mixed], [((ROWS, WIDTH), BF16)])

time: 285 us -> 271 us (0.951)
  Pallas kernels: 40.6 us -> 34 us
  local copies, waits for them, and re-layouts: 16.4 us -> 9.89 us
  starting transfers between devices: 64.7 us -> 60.3 us
  blocking collectives: 99.7 us -> 104 us
  waiting for transfers between devices: 47.8 us -> 44.9 us
    all_to_all x6, starting transfers between devices: 54.6 us -> 46 us  [exchange(): return lax.all_to_all(value, axes, split_axis=0, concat_axis=0, tiled=True)]
    pallas_call x10, Pallas kernels: 40.6 us -> 34 us  [call(): pl.pallas_call(body, out_shape=[jax.ShapeDtypeStruct(shape, dtype) for sh...]
    unnamed x43 -> x26, local copies, waits for them, and re-layouts: 13.7 us -> 7.27 us
    ppermute x3, waiting for transfers between devices: 7.29 us -> 2.45 us  [the longest x2 2.45 us: per_device(): lax.ppermute(term, 'scene', [(i, i ^ k) for i in range(SCENES)])]
    all_to_all x3, blocking collectives: 61.9 us -> 66.7 us  [exchange(): return lax.all_to_all(value, axes, split_axis=0, concat_axis=0, tiled=True)]
    ppermute x3, starting transfers between devices: 10 us -> 14.2 us  [the longest x2 9.62 us: per_device(): lax.ppermute(term, 'scene', [(i, i ^ k) for i in range(SCENES)])]
    all_gather x1, waiting for transfers between devices: 5.85 us -> 9.65 us  [per_device(): all_grads_h = lax.all_gather(grads_h, GROUP, axis=0, tiled=True)]
  transfers between devices with their start and end apart: 13 -> 13, of which waited for: 8 -> 7; matrix products, arithmetic and copies ran while one was open for 1% -> 1% of each run, Pallas kernels for 12% -> 9%
where the time goes in v3:
time: 271 us; the launch traced here: 267 us
  blocking collectives  104 us (38%)
  starting transfers between devices  60.3 us (22%)
  waiting for transfers between devices  44.9 us (17%)
  Pallas kernels  34 us (13%)
  between operations  13.9 us (5%)
  local copies, waits for them, and re-layouts  9.89 us (4%)
    all_to_all x3, blocking collectives, exchange(): return lax.all_to_all(value, axes, split_axis=0, concat_axis=0, tiled=True)  66.7 us
    all_to_all x6, starting transfers between devices, exchange(): return lax.all_to_all(value, axes, split_axis=0, concat_axis=0, tiled=True)  46 us
    pallas_call x10, Pallas kernels, call(): pl.pallas_call(body, out_shape=[jax.ShapeDtypeStruct(shape, dtype) for sh...  34 us
    all_to_all x6, waiting for transfers between devices, exchange(): return lax.all_to_all(value, axes, split_axis=0, concat_axis=0, tiled=True)  32.1 us
    all_gather x1, blocking collectives, per_device(): weights = lax.all_gather(weights, ('zh', 'zl'), axis=0, tiled=True)  26.6 us
    all_gather x1, blocking collectives, per_device(): own = lax.all_gather(own, 'x', axis=0, tiled=True)  10.4 us
    all_gather x1, waiting for transfers between devices, per_device(): all_grads_h = lax.all_gather(grads_h, GROUP, axis=0, tiled=True)  9.65 us
    ppermute x2, starting transfers between devices, per_device(): lax.ppermute(term, 'scene', [(i, i ^ k) for i in range(SCENES)])  9.62 us
  transfers between devices with their start and end apart: 13, of which 7 were waited for; matrix products, arithmetic and copies ran while one was open for 1% of the time, Pallas kernels for 9%

profile of v3, /device:TPU:1, one launch (start us, length us, event | category | flops | bytes accessed | tf_op | source)
XLA Modules:
  0.0 267.5 jit_solution(2307602043229664682)
XLA Ops:
  7.2 0.0 all-gather.5.cloned.1.call-start
  7.2 2.2 shard_map.104
  9.4 0.0 copy-start.12
  9.4 0.0 all-gather.5.cloned.1.call-update
  9.4 0.0 all-gather.7.cloned.1.call-start
  9.5 11.2 %all_to_all.45 = bf16[2,4,2048]{2,1,0:T(4,128)(2,1)S(1)} all-to-all(bf16[2,4,2048]{2,1,0:T(4,128)(2,1)} %get-tuple-element.26), channel_id=1, replica_groups=mesh['x'=4,'zh'=4,'zl'=4,'core'=2,'scene'=4] {'core'}, dimensions={0} | all-to-all | bytes 65536 | tf_op jit(solution)/shard_map/all_to_all | solution.py:340
  20.7 26.6 %all_gather.19 = bf16[128,2048]{1,0:T(8,128)(2,1)S(1)} all-gather(bf16[8,2048]{1,0:T(8,128)(2,1)S(1)} %reshape.31), channel_id=1, replica_groups=mesh['x'=4,'zh'=4,'zl'=4,'core'=2,'scene'=4] {'zh','zl'}, dimensions={0}, use_global_device_ids=true | all-gather | bytes 557056 | tf_op jit(solution)/shard_map/all_gather | solution.py:369
  47.2 0.8 slice.8
  48.0 0.0 all-gather.7.cloned.1.call-update
  48.1 0.1 pad.2.clone
  48.1 0.1 constant_dynamic-slice_fusion
  48.3 0.0 copy-done.11
  48.3 10.4 %all_gather.20.refs_2_ = bf16[512,256]{1,0:T(8,128)(2,1)S(1)} all-gather(bf16[128,256]{1,0:T(8,128)(2,1)S(1)} %maximum_maximum_fusion), channel_id=1, replica_groups=mesh['x'=4,'zh'=4,'zl'=4,'core'=2,'scene'=4] {'x'}, dimensions={0}, use_global_device_ids=true | all-gather | bytes 327680 | tf_op jit(solution)/shard_map/all_gather | solution.py:380
  58.7 8.4 %all-to-all-start.1 = ((bf16[16,16,512]{2,1,0:T(8,128)(2,1)}), bf16[16,16,512]{2,1,0:T(8,128)(2,1)S(1)}, u32[]{:S(2)}, u32[]{:S(2)}) async-start(bf16[16,16,512]{2,1,0:T(8,128)(2,1)} %bitcast.5), calls=%async_computation.1 | async-start | bytes 524288 | tf_op jit(solution)/shard_map/all_to_all | solution.py:340
  67.1 0.0 copy-done.12
  67.1 0.1 pad_add_fusion.refs_0_
  67.2 1.3 copy-done.5
  68.5 5.5 %shard_map.105 = (bf16[1024,256]{1,0:T(8,128)(2,1)S(1)}, bf16[8,64,128]{2,1,0:T(8,128)(2,1)}, bf16[272,128]{1,0:T(8,128)(2,1)S(1)}) custom-call(s32[18]{0:T(128)S(1)} %pad_add_fusion.refs_0_, bf16[1152,512]{1,0:T(8,128)(2,1)S(1)} %copy-done.5, bf16[512,256]{1,0:T(8,128)(2,1)S(1)} %all_gather.20.refs_2_), custom_call_target="tpu_custom_call" | custom-call | flops 9200000000 | tf_op jit(solution)/shard_map/pallas_call | solution.py:83
  74.0 0.8 copy-done.9
  74.8 9.3 %all-to-all-done.1 = bf16[16,16,512]{2,1,0:T(8,128)(2,1)S(1)} async-done(((bf16[16,16,512]{2,1,0:T(8,128)(2,1)}), bf16[16,16,512]{2,1,0:T(8,128)(2,1)S(1)}, u32[]{:S(2)}, u32[]{:S(2)}) %all-to-all-start.1) | async-done | bytes 262176 | tf_op jit(solution)/shard_map/all_to_all | solution.py:340
  84.1 14.0 %all-to-all-start.2 = ((bf16[8,64,128]{2,1,0:T(8,128)(2,1)}), bf16[8,64,128]{2,1,0:T(8,128)(2,1)S(1)}, u32[]{:S(2)}, u32[]{:S(2)}) async-start(bf16[8,64,128]{2,1,0:T(8,128)(2,1)} %get-tuple-element.30), calls=%async_computation.2 | async-start | bytes 262144 | tf_op jit(solution)/shard_map/all_to_all | solution.py:340
  98.1 0.9 shard_map.106.refs_4_.refs_3_
  99.0 4.9 %all-to-all-done.2 = bf16[8,64,128]{2,1,0:T(8,128)(2,1)S(1)} async-done(((bf16[8,64,128]{2,1,0:T(8,128)(2,1)}), bf16[8,64,128]{2,1,0:T(8,128)(2,1)S(1)}, u32[]{:S(2)}, u32[]{:S(2)}) %all-to-all-start.2) | async-done | bytes 131104 | tf_op jit(solution)/shard_map/all_to_all | solution.py:340
  103.9 0.0 copy-done.6
  103.9 0.0 copy-done.8
  103.9 1.7 copy-done
  105.7 0.5 shard_map.107
  106.2 23.4 %all_to_all.46 = bf16[16,16,512]{2,1,0:T(8,128)(2,1)S(1)} all-to-all(bf16[16,16,512]{2,1,0:T(8,128)(2,1)S(1)} %bitcast.21), channel_id=1, replica_groups=mesh['x'=4,'zh'=4,'zl'=4,'core'=2,'scene'=4] {'x','zh'}, dimensions={0} | all-to-all | bytes 524288 | tf_op jit(solution)/shard_map/all_to_all | solution.py:340
  129.6 0.0 copy-done.1
  129.6 1.6 shard_map.108
  131.2 0.0 copy-start.3
  131.2 0.8 copy-done.3
  132.0 7.5 %all-to-all-start.4 = ((bf16[8,256,128]{2,1,0:T(8,128)(2,1)}), bf16[8,256,128]{2,1,0:T(8,128)(2,1)S(1)}, u32[]{:S(2)}, u32[]{:S(2)}) async-start(bf16[8,256,128]{2,1,0:T(8,128)(2,1)} %copy-done.3), calls=%async_computation.4 | async-start | bytes 1048576 | tf_op jit(solution)/shard_map/all_to_all | solution.py:340
  139.5 0.0 all-gather.9.cloned.1.call-start
  139.5 0.7 all-gather.9.cloned.1.call-update
  140.2 13.8 %all-to-all-done.4.refs_0_ = bf16[8,256,128]{2,1,0:T(8,128)(2,1)S(1)} async-done(((bf16[8,256,128]{2,1,0:T(8,128)(2,1)}), bf16[8,256,128]{2,1,0:T(8,128)(2,1)S(1)}, u32[]{:S(2)}, u32[]{:S(2)}) %all-to-all-start.4) | async-done | bytes 524320 | tf_op jit(solution)/shard_map/all_to_all | solution.py:340
  154.0 9.3 %shard_map.109 = (bf16[8,192,128]{2,1,0:T(8,128)(2,1)}, bf16[64,1024]{1,0:T(8,128)(2,1)S(1)}) custom-call(bf16[8,256,128]{2,1,0:T(8,128)(2,1)S(1)} %all-to-all-done.4.refs_0_, bf16[272,128]{1,0:T(8,128)(2,1)S(1)} %get-tuple-element.32.refs_1_.refs_4_), custom_call_target="tpu_custom_call" | custom-call | flops 12650000384 | tf_op jit(solution)/shard_map/pallas_call | solution.py:83
  163.3 4.2 %all-to-all-start.5 = ((bf16[8,192,128]{2,1,0:T(8,128)(2,1)}), bf16[8,192,128]{2,1,0:T(8,128)(2,1)S(1)}, u32[]{:S(2)}, u32[]{:S(2)}) async-start(bf16[8,192,128]{2,1,0:T(8,128)(2,1)} %get-tuple-element.37), calls=%async_computation.5 | async-start | bytes 786432 | tf_op jit(solution)/shard_map/all_to_all | solution.py:340
  167.5 9.6 %all-gather.9.cloned.1.call-done.refs_6_ = bf16[1024,512]{1,0:T(8,128)(2,1)} async-done(((bf16[128,512]{1,0:T(8,128)(2,1)}), bf16[1024,512]{1,0:T(8,128)(2,1)}) %all-gather.9.cloned.1.call-update) | async-done | bytes 1048592 | tf_op jit(solution)/shard_map/all_gather | solution.py:409
  177.2 4.1 %all-to-all-done.5.refs_0_ = bf16[8,192,128]{2,1,0:T(8,128)(2,1)S(1)} async-done(((bf16[8,192,128]{2,1,0:T(8,128)(2,1)}), bf16[8,192,128]{2,1,0:T(8,128)(2,1)S(1)}, u32[]{:S(2)}, u32[]{:S(2)}) %all-to-all-start.5) | async-done | bytes 393248 | tf_op jit(solution)/shard_map/all_to_all | solution.py:340
  181.3 1.2 copy-done.2
  182.5 2.0 shard_map.110
  184.5 32.1 %all_to_all.47.refs_0_ = bf16[16,24,512]{2,1,0:T(8,128)(2,1)S(1)} all-to-all(bf16[16,24,512]{2,1,0:T(8,128)(2,1)S(1)} %shard_map.110), channel_id=1, replica_groups=mesh['x'=4,'zh'=4,'zl'=4,'core'=2,'scene'=4] {'x','zh'}, dimensions={0} | all-to-all | bytes 786432 | tf_op jit(solution)/shard_map/all_to_all | solution.py:340
  216.7 1.3 shard_map.111
  218.0 8.0 %all-to-all-start.7 = ((bf16[8,64,128]{2,1,0:T(8,128)(2,1)}), bf16[8,64,128]{2,1,0:T(8,128)(2,1)S(1)}, u32[]{:S(2)}, u32[]{:S(2)}) async-start(bf16[8,64,128]{2,1,0:T(8,128)(2,1)} %bitcast.11), calls=%async_computation.7 | async-start | bytes 262144 | tf_op jit(solution)/shard_map/all_to_all | solution.py:340
  226.0 0.0 all-gather.11.cloned.1.call-start
  226.0 1.6 slice.9
  227.7 0.0 all-gather.11.cloned.1.call-update
  227.7 4.6 %collective-permute-start = (f32[4,512]{1,0:T(4,128)S(1)}, f32[4,512]{1,0:T(4,128)S(1)}, u32[]{:S(2)}, u32[]{:S(2)}) collective-permute-start(f32[4,512]{1,0:T(4,128)S(1)} %get-tuple-element.42), channel_id=1, source_target_pairs={{0,0},{4,64},{8,128},{12,192},{16,256},{20,320},{24,384},{28,448},... | collective-permute-start | bytes 24584 | tf_op jit(solution)/shard_map/ppermute | solution.py:456
  232.3 0.0 all-to-all-done.7.refs_1_
  232.3 0.0 copy-done.10
  232.3 0.0 copy-start.7
  232.4 9.2 %shard_map.112 = bf16[8,192,128]{2,1,0:T(8,128)(2,1)} custom-call(s32[18]{0:T(128)S(1)} %pad_add_fusion.refs_0_, bf16[8,64,128]{2,1,0:T(8,128)(2,1)S(1)} %all-to-all-done.7.refs_1_, bf16[1024,256]{1,0:T(8,128)(2,1)S(1)} %copy-done.10), custom_call_target="tpu_custom_call" | custom-call | flops 12650000384 | tf_op jit(solution)/shard_map/pallas_call | solution.py:83
  241.5 0.0 collective-permute-done
  241.5 3.9 %all-to-all-start.8 = ((bf16[8,192,128]{2,1,0:T(8,128)(2,1)}), bf16[8,192,128]{2,1,0:T(8,128)(2,1)S(1)}, u32[]{:S(2)}, u32[]{:S(2)}) async-start(bf16[8,192,128]{2,1,0:T(8,128)(2,1)} %shard_map.112), calls=%async_computation.8 | async-start | bytes 786432 | tf_op jit(solution)/shard_map/all_to_all | solution.py:340
  245.4 4.5 %collective-permute-start.1 = (f32[4,512]{1,0:T(4,128)S(1)}, f32[4,512]{1,0:T(4,128)S(1)}, u32[]{:S(2)}, u32[]{:S(2)}) collective-permute-start(f32[4,512]{1,0:T(4,128)S(1)} %collective-permute-done), channel_id=1, source_target_pairs={{0,1},{1,0},{2,3},{3,2},{4,5},{5,4},{6,7},{7,6},{8,9},{9,8},{10,11... | collective-permute-start | bytes 24584 | tf_op jit(solution)/shard_map/ppermute | solution.py:471
  249.9 1.4 collective-permute-done.1
  251.4 5.1 %collective-permute-start.2 = (f32[4,512]{1,0:T(4,128)S(1)}, f32[4,512]{1,0:T(4,128)S(1)}, u32[]{:S(2)}, u32[]{:S(2)}) collective-permute-start(f32[4,512]{1,0:T(4,128)S(1)} %add.24), channel_id=1, source_target_pairs={{0,2},{1,3},{2,0},{3,1},{4,6},{5,7},{6,4},{7,5},{8,10},{9,11},{10,... | collective-permute-start | bytes 24584 | tf_op jit(solution)/shard_map/ppermute | solution.py:471
  256.5 1.0 collective-permute-done.2
  257.5 0.6 add.25
  258.1 0.0 all-to-all-done.8.refs_0_
  258.1 0.0 copy-done.7
  258.1 1.4 copy-done.4
  259.5 1.4 shard_map.113
  (18 shorter events, 0.1 us)
Async XLA Ops:
  7.2 60.0 %all-gather.5.cloned.1.call-start = ((), (), s32[]{:S(2)}) async-start(), calls=%async_computation.9 | async-start | bytes 1327104 | tf_op jit(solution)/shard_map/all_gather | solution.py:367
  9.4 57.7 %copy-start.12 = (s32[1,16]{1,0:T(1,128)S(1)}, s32[1,16]{1,0:T(1,128)}, u32[]{:S(2)}) copy-start(s32[1,16]{1,0:T(1,128)} %param.11) | copy-start | bytes 196
  9.4 94.5 %all-gather.7.cloned.1.call-start = ((), (), s32[]{:S(2)}) async-start(), calls=%async_computation.10 | async-start | bytes 2949120 | tf_op jit(solution)/shard_map/all_gather | solution.py:381
  47.2 1.0 copy-start.11
  58.7 25.4 %all-to-all-start.1 = ((bf16[16,16,512]{2,1,0:T(8,128)(2,1)}), bf16[16,16,512]{2,1,0:T(8,128)(2,1)S(1)}, u32[]{:S(2)}, u32[]{:S(2)}) async-start(bf16[16,16,512]{2,1,0:T(8,128)(2,1)} %bitcast.5), calls=%async_computation.1 | async-start | bytes 524288 | tf_op jit(solution)/shard_map/all_to_all | solution.py:340
  67.2 1.3 copy-start.5
  74.0 0.8 copy-start.9
  84.1 19.8 %all-to-all-start.2 = ((bf16[8,64,128]{2,1,0:T(8,128)(2,1)}), bf16[8,64,128]{2,1,0:T(8,128)(2,1)S(1)}, u32[]{:S(2)}, u32[]{:S(2)}) async-start(bf16[8,64,128]{2,1,0:T(8,128)(2,1)} %get-tuple-element.30), calls=%async_computation.2 | async-start | bytes 262144 | tf_op jit(solution)/shard_map/all_to_all | solution.py:340
  98.1 5.8 %copy-start.6 = (bf16[1,128,512]{2,1,0:T(8,128)(2,1)S(1)}, bf16[1,128,512]{2,1,0:T(8,128)(2,1)}, u32[]{:S(2)}) copy-start(bf16[1,128,512]{2,1,0:T(8,128)(2,1)} %param.9) | copy-start | bytes 393220
  98.1 5.8 %copy-start.8 = (s32[1,128]{1,0:T(1,128)S(1)}, s32[1,128]{1,0:T(1,128)}, u32[]{:S(2)}) copy-start(s32[1,128]{1,0:T(1,128)} %refs_1_.1) | copy-start | bytes 1540
  103.9 1.7 copy-start
  105.7 23.9 %copy-start.1 = (bf16[1024,1280]{1,0:T(8,128)(2,1)S(1)}, bf16[1024,1280]{1,0:T(8,128)(2,1)}, u32[]{:S(2)}) copy-start(bf16[1024,1280]{1,0:T(8,128)(2,1)} %all-gather.7.cloned.1.call-done) | copy-start | bytes 7864324
  131.2 0.8 copy-start.3
  132.0 22.0 %all-to-all-start.4 = ((bf16[8,256,128]{2,1,0:T(8,128)(2,1)}), bf16[8,256,128]{2,1,0:T(8,128)(2,1)S(1)}, u32[]{:S(2)}, u32[]{:S(2)}) async-start(bf16[8,256,128]{2,1,0:T(8,128)(2,1)} %copy-done.3), calls=%async_computation.4 | async-start | bytes 1048576 | tf_op jit(solution)/shard_map/all_to_all | solution.py:340
  139.5 37.7 %all-gather.9.cloned.1.call-start = ((), (), s32[]{:S(2)}) async-start(), calls=%async_computation.11 | async-start | bytes 1179648 | tf_op jit(solution)/shard_map/all_gather | solution.py:409
  163.3 18.0 %all-to-all-start.5 = ((bf16[8,192,128]{2,1,0:T(8,128)(2,1)}), bf16[8,192,128]{2,1,0:T(8,128)(2,1)S(1)}, u32[]{:S(2)}, u32[]{:S(2)}) async-start(bf16[8,192,128]{2,1,0:T(8,128)(2,1)} %get-tuple-element.37), calls=%async_computation.5 | async-start | bytes 786432 | tf_op jit(solution)/shard_map/all_to_all | solution.py:340
  181.3 1.2 copy-start.2
  216.7 15.7 %copy-start.10 = (bf16[1024,256]{1,0:T(8,128)(2,1)S(1)}, bf16[1024,256]{1,0:T(8,128)(2,1)}, u32[]{:S(2)}) copy-start(bf16[1024,256]{1,0:T(8,128)(2,1)} %copy-done.9) | copy-start | bytes 1572868
  218.0 14.3 %all-to-all-start.7 = ((bf16[8,64,128]{2,1,0:T(8,128)(2,1)}), bf16[8,64,128]{2,1,0:T(8,128)(2,1)S(1)}, u32[]{:S(2)}, u32[]{:S(2)}) async-start(bf16[8,64,128]{2,1,0:T(8,128)(2,1)} %bitcast.11), calls=%async_computation.7 | async-start | bytes 262144 | tf_op jit(solution)/shard_map/all_to_all | solution.py:340
  226.0 32.1 %all-gather.11.cloned.1.call-start = ((), (), s32[]{:S(2)}) async-start(), calls=%async_computation.12 | async-start | bytes 1769472 | tf_op jit(solution)/shard_map/all_gather | solution.py:383
  227.7 13.8 %collective-permute-start = (f32[4,512]{1,0:T(4,128)S(1)}, f32[4,512]{1,0:T(4,128)S(1)}, u32[]{:S(2)}, u32[]{:S(2)}) collective-permute-start(f32[4,512]{1,0:T(4,128)S(1)} %get-tuple-element.42), channel_id=1, source_target_pairs={{0,0},{4,64},{8,128},{12,192},{16,256},{20,320},{24,384},{28,448},... | collective-permute-start | bytes 24584 | tf_op jit(solution)/shard_map/ppermute | solution.py:456
  232.3 25.8 %copy-start.7 = (bf16[1,128,512]{2,1,0:T(8,128)(2,1)S(1)}, bf16[1,128,512]{2,1,0:T(8,128)(2,1)}, u32[]{:S(2)}) copy-start(bf16[1,128,512]{2,1,0:T(8,128)(2,1)} %param.9) | copy-start | bytes 393220
  241.5 16.6 %all-to-all-start.8 = ((bf16[8,192,128]{2,1,0:T(8,128)(2,1)}), bf16[8,192,128]{2,1,0:T(8,128)(2,1)S(1)}, u32[]{:S(2)}, u32[]{:S(2)}) async-start(bf16[8,192,128]{2,1,0:T(8,128)(2,1)} %shard_map.112), calls=%async_computation.8 | async-start | bytes 786432 | tf_op jit(solution)/shard_map/all_to_all | solution.py:340
  245.4 6.0 %collective-permute-start.1 = (f32[4,512]{1,0:T(4,128)S(1)}, f32[4,512]{1,0:T(4,128)S(1)}, u32[]{:S(2)}, u32[]{:S(2)}) collective-permute-start(f32[4,512]{1,0:T(4,128)S(1)} %collective-permute-done), channel_id=1, source_target_pairs={{0,1},{1,0},{2,3},{3,2},{4,5},{5,4},{6,7},{7,6},{8,9},{9,8},{10,11... | collective-permute-start | bytes 24584 | tf_op jit(solution)/shard_map/ppermute | solution.py:471
  251.4 6.1 %collective-permute-start.2 = (f32[4,512]{1,0:T(4,128)S(1)}, f32[4,512]{1,0:T(4,128)S(1)}, u32[]{:S(2)}, u32[]{:S(2)}) collective-permute-start(f32[4,512]{1,0:T(4,128)S(1)} %add.24), channel_id=1, source_target_pairs={{0,2},{1,3},{2,0},{3,1},{4,6},{5,7},{6,4},{7,5},{8,10},{9,11},{10,... | collective-permute-start | bytes 24584 | tf_op jit(solution)/shard_map/ppermute | solution.py:471
  258.1 1.4 copy-start.4
Sparse Core Ops, SparseCore 0:
  10.1 46.0 all-gather.4
  58.3 36.5 all-gather.6
  142.4 34.7 all-gather.8
  228.7 26.5 all-gather.10

commit v4 on v3

--- a/solution.py
+++ b/solution.py
@@ -309,27 +309,34 @@
 def return_kernel(arrived, project, rows, grads, plan, attended, all_grads, send):
     grad = input_grad(arrived, halves(project, 0, 3 * WIDTH // 2), rows, grads)
     spaced = dot(plan[: PATCHES * SLOTS, :], grad).astype(BF16)
-    term = dot(attended[...], all_grads[...])
-    upper = term.astype(BF16)
-    lower = (term - upper.astype(F32)).astype(BF16)
+    term = dot(attended[...], all_grads[...]).astype(BF16)
+    tiles = [slice(t * ROWS, (t + 1) * ROWS) for t in range(4)]
     for k in range(PATCHES):
-        send[k, :SLOTS, :] = spaced[k * SLOTS : (k + 1) * SLOTS, :]
-        share = slice(k * SHARE, (k + 1) * SHARE)
-        send[k, SLOTS:, :] = jnp.concatenate([upper[share, :], lower[share, :]], axis=0)
+        rows = spaced[k * SLOTS : (k + 1) * SLOTS, :]
+        for t, tile in enumerate(tiles):
+            send[k, t * SLOTS : (t + 1) * SLOTS, :] = rows[:, tile]
+        share = term[k * SHARE : (k + 1) * SHARE, :]
+        send[k, 4 * SLOTS :, :] = jnp.concatenate([share[:, tile] for tile in tiles], axis=0)
 
 
 def regain_kernel(arrived, targets, output, grad_mixed, send, term):
-    spaced = jnp.concatenate([arrived[k, :SLOTS, :] for k in range(PATCHES)], axis=0)
+    spaced = jnp.concatenate(
+        [
+            jnp.concatenate([arrived[k, t * SLOTS : (t + 1) * SLOTS, :] for k in range(PATCHES)], axis=0)
+            for t in range(4)
+        ],
+        axis=1,
+    )
     grad = dot(place_rows(targets), spaced, 0, 0).astype(BF16)
     grad_mixed[...] = grad
     low, high = halves(output, 0, WIDTH // 2)
     grad_attended = dot(low, grad[:, : WIDTH // 2], 1, 1) + dot(high, grad[:, WIDTH // 2 :], 1, 1)
     send[...] = grad_attended.astype(BF16)
-    total = jnp.zeros((2 * SHARE, WIDTH), F32)
+    total = jnp.zeros((4 * SHARE, ROWS), F32)
     for k in range(PATCHES):
-        total += arrived[k, SLOTS:, :].astype(F32)
-    factor = (SCENES * PATCHES * PATCH) ** (-0.5)
-    term[...] = (total[:SHARE, :] + total[SHARE:, :]) * factor
+        total += arrived[k, 4 * SLOTS :, :].astype(F32)
+    total = jnp.concatenate([total[t * SHARE : (t + 1) * SHARE, :] for t in range(4)], axis=1)
+    term[...] = total * (SCENES * PATCHES * PATCH) ** (-0.5)
 
 
 def finish_kernel(arrived, project, rows, grads, out):
@@ -380,10 +387,9 @@
     own = lax.all_gather(own, "x", axis=0, tiled=True)
     shared = lax.all_gather(weights[:, third:], ("x", "core"), axis=0, tiled=True)
     shared = shared.reshape(MEMBERS, ROWS, third + WIDTH)
-    project_z = lax.all_gather(weights[:, :third], ("x", "core"), axis=0, tiled=True)
-    project_z = project_z.reshape(MEMBERS, ROWS, third)
-
-    send_grads, own = lax.optimization_barrier((send_grads, own))
+    project_z = weights[:, :third]
+
+    send_grads, own, gathered = lax.optimization_barrier((send_grads, own, gathered))
     arrived_grads = exchange(send_grads.reshape(PATCHES, SLOTS, WIDTH), ACROSS)
 
     qkv_z, attended, plan = call(
@@ -398,7 +404,9 @@
         micros=8,
     )
 
-    attended, arrived_grads = lax.optimization_barrier((attended, arrived_grads))
+    attended, arrived_grads, project_z = lax.optimization_barrier((attended, arrived_grads, project_z))
+    project_z = lax.all_gather(project_z, ("x", "core"), axis=0, tiled=True)
+    project_z = project_z.reshape(MEMBERS, ROWS, third)
     (grads_h,) = call(
         collect_kernel,
         [arrived_grads.reshape(PATCHES * SLOTS, WIDTH), plan],
@@ -444,7 +452,7 @@
     (send,) = call(
         return_kernel,
         [arrived, (shared, *PROJECT_H), rows_h, grads_h, plan, attended_h, all_grads_h],
-        [((PATCHES, SLOTS + 2 * SHARE, WIDTH), BF16)],
+        [((PATCHES, 4 * SLOTS + 4 * SHARE, ROWS), BF16)],
     )
 
     arrived = exchange(send, ACROSS)

time: 271 us -> 268 us (0.989)
  blocking collectives: 104 us -> 99.8 us
    all_to_all x6, starting transfers between devices: 46 us -> 50.1 us  [exchange(): return lax.all_to_all(value, axes, split_axis=0, concat_axis=0, tiled=True)]
    all_to_all x3, blocking collectives: 66.7 us -> 62.8 us  [exchange(): return lax.all_to_all(value, axes, split_axis=0, concat_axis=0, tiled=True)]
    unnamed x26 -> x24, local copies, waits for them, and re-layouts: 7.27 us -> 7.27 us
  transfers between devices with their start and end apart: 13 -> 13, of which waited for: 7 -> 9; matrix products, arithmetic and copies ran while one was open for 1% -> 1% of each run, Pallas kernels for 9% -> 9%
where the time goes in v4:
time: 268 us; the launch traced here: 265 us
  blocking collectives  99.8 us (37%)
  starting transfers between devices  60.8 us (23%)
  waiting for transfers between devices  47.3 us (18%)
  Pallas kernels  34 us (13%)
  between operations  13.9 us (5%)
  local copies, waits for them, and re-layouts  8.93 us (3%)
    all_to_all x3, blocking collectives, exchange(): return lax.all_to_all(value, axes, split_axis=0, concat_axis=0, tiled=True)  62.8 us
    all_to_all x6, starting transfers between devices, exchange(): return lax.all_to_all(value, axes, split_axis=0, concat_axis=0, tiled=True)  50.1 us
    pallas_call x10, Pallas kernels, call(): pl.pallas_call(body, out_shape=[jax.ShapeDtypeStruct(shape, dtype) for sh...  34 us
    all_to_all x6, waiting for transfers between devices, exchange(): return lax.all_to_all(value, axes, split_axis=0, concat_axis=0, tiled=True)  33.3 us
    all_gather x1, blocking collectives, per_device(): weights = lax.all_gather(weights, ('zh', 'zl'), axis=0, tiled=True)  26.6 us
    all_gather x1, blocking collectives, per_device(): own = lax.all_gather(own, 'x', axis=0, tiled=True)  10.4 us
    all_gather x1, waiting for transfers between devices, per_device(): all_grads_h = lax.all_gather(grads_h, GROUP, axis=0, tiled=True)  9.75 us
    ppermute x2, starting transfers between devices, per_device(): lax.ppermute(term, 'scene', [(i, i ^ k) for i in range(SCENES)])  7.66 us
  transfers between devices with their start and end apart: 13, of which 9 were waited for; matrix products, arithmetic and copies ran while one was open for 1% of the time, Pallas kernels for 9%

profile of v4, /device:TPU:1, one launch (start us, length us, event | category | flops | bytes accessed | tf_op | source)
XLA Modules:
  0.0 265.3 jit_solution(9355958639841134195)
XLA Ops:
  7.2 0.0 all-gather.5.cloned.1.call-start
  7.2 2.2 shard_map.104
  9.4 0.0 all-gather.5.cloned.1.call-update
  9.4 0.0 all-gather.7.cloned.1.call-start
  9.4 11.2 %all_to_all.45 = bf16[2,4,2048]{2,1,0:T(4,128)(2,1)S(1)} all-to-all(bf16[2,4,2048]{2,1,0:T(4,128)(2,1)} %get-tuple-element.27), channel_id=1, replica_groups=mesh['x'=4,'zh'=4,'zl'=4,'core'=2,'scene'=4] {'core'}, dimensions={0} | all-to-all | bytes 65536 | tf_op jit(solution)/shard_map/all_to_all | solution.py:347
  20.6 0.0 copy-start.11
  20.7 26.6 %all_gather.18 = bf16[128,2048]{1,0:T(8,128)(2,1)S(1)} all-gather(bf16[8,2048]{1,0:T(8,128)(2,1)S(1)} %reshape.31), channel_id=1, replica_groups=mesh['x'=4,'zh'=4,'zl'=4,'core'=2,'scene'=4] {'zh','zl'}, dimensions={0}, use_global_device_ids=true | all-gather | bytes 557056 | tf_op jit(solution)/shard_map/all_gather | solution.py:376
  47.2 0.8 slice.9
  48.0 0.0 all-gather.7.cloned.1.call-update
  48.0 0.1 pad.2.clone
  48.1 0.1 constant_dynamic-slice_fusion
  48.2 10.4 %all_gather.19.refs_2_ = bf16[512,256]{1,0:T(8,128)(2,1)S(1)} all-gather(bf16[128,256]{1,0:T(8,128)(2,1)S(1)} %maximum_maximum_fusion), channel_id=1, replica_groups=mesh['x'=4,'zh'=4,'zl'=4,'core'=2,'scene'=4] {'x'}, dimensions={0}, use_global_device_ids=true | all-gather | bytes 327680 | tf_op jit(solution)/shard_map/all_gather | solution.py:387
  58.6 0.0 all-gather.5.cloned.1.call-done.refs_1_
  58.6 10.7 %all-to-all-start.1 = ((bf16[16,16,512]{2,1,0:T(8,128)(2,1)}), bf16[16,16,512]{2,1,0:T(8,128)(2,1)S(1)}, u32[]{:S(2)}, u32[]{:S(2)}) async-start(bf16[16,16,512]{2,1,0:T(8,128)(2,1)} %bitcast.5), calls=%async_computation.1 | async-start | bytes 524288 | tf_op jit(solution)/shard_map/all_to_all | solution.py:347
  69.4 0.7 slice.8
  70.1 0.0 copy-done.11
  70.1 0.1 pad_add_fusion.refs_0_
  70.1 0.0 copy-start.5
  70.1 1.3 copy-done.5
  71.4 5.5 %shard_map.105 = (bf16[1024,256]{1,0:T(8,128)(2,1)S(1)}, bf16[8,64,128]{2,1,0:T(8,128)(2,1)}, bf16[272,128]{1,0:T(8,128)(2,1)S(1)}) custom-call(s32[18]{0:T(128)S(1)} %pad_add_fusion.refs_0_, bf16[1152,512]{1,0:T(8,128)(2,1)S(1)} %copy-done.5, bf16[512,256]{1,0:T(8,128)(2,1)S(1)} %all_gather.19.refs_2_), custom_call_target="tpu_custom_call" | custom-call | flops 9200000000 | tf_op jit(solution)/shard_map/pallas_call | solution.py:83
  76.9 0.8 copy-done.9
  77.7 7.8 %all-to-all-done.1 = bf16[16,16,512]{2,1,0:T(8,128)(2,1)S(1)} async-done(((bf16[16,16,512]{2,1,0:T(8,128)(2,1)}), bf16[16,16,512]{2,1,0:T(8,128)(2,1)S(1)}, u32[]{:S(2)}, u32[]{:S(2)}) %all-to-all-start.1) | async-done | bytes 262176 | tf_op jit(solution)/shard_map/all_to_all | solution.py:347
  85.5 12.6 %all-to-all-start.2 = ((bf16[8,64,128]{2,1,0:T(8,128)(2,1)}), bf16[8,64,128]{2,1,0:T(8,128)(2,1)S(1)}, u32[]{:S(2)}, u32[]{:S(2)}) async-start(bf16[8,64,128]{2,1,0:T(8,128)(2,1)} %get-tuple-element.33), calls=%async_computation.2 | async-start | bytes 262144 | tf_op jit(solution)/shard_map/all_to_all | solution.py:347
  98.1 0.9 shard_map.106.refs_4_.refs_3_
  98.9 4.9 %all-to-all-done.2 = bf16[8,64,128]{2,1,0:T(8,128)(2,1)S(1)} async-done(((bf16[8,64,128]{2,1,0:T(8,128)(2,1)}), bf16[8,64,128]{2,1,0:T(8,128)(2,1)S(1)}, u32[]{:S(2)}, u32[]{:S(2)}) %all-to-all-start.2) | async-done | bytes 131104 | tf_op jit(solution)/shard_map/all_to_all | solution.py:347
  103.9 0.0 copy-done.6
  103.9 0.0 copy-done.8
  103.9 1.7 copy-done
  105.6 0.5 shard_map.107
  106.1 22.4 %all_to_all.46 = bf16[16,16,512]{2,1,0:T(8,128)(2,1)S(1)} all-to-all(bf16[16,16,512]{2,1,0:T(8,128)(2,1)S(1)} %bitcast.21), channel_id=1, replica_groups=mesh['x'=4,'zh'=4,'zl'=4,'core'=2,'scene'=4] {'x','zh'}, dimensions={0} | all-to-all | bytes 524288 | tf_op jit(solution)/shard_map/all_to_all | solution.py:347
  128.5 0.0 copy-done.1
  128.5 1.6 shard_map.108
  130.1 0.0 copy-start.3
  130.1 0.8 copy-done.3
  130.9 8.5 %all-to-all-start.4 = ((bf16[8,256,128]{2,1,0:T(8,128)(2,1)}), bf16[8,256,128]{2,1,0:T(8,128)(2,1)S(1)}, u32[]{:S(2)}, u32[]{:S(2)}) async-start(bf16[8,256,128]{2,1,0:T(8,128)(2,1)} %copy-done.3), calls=%async_computation.4 | async-start | bytes 1048576 | tf_op jit(solution)/shard_map/all_to_all | solution.py:347
  139.4 0.0 all-gather.9.cloned.1.call-start
  139.4 0.7 all-gather.9.cloned.1.call-update
  140.1 13.8 %all-to-all-done.4.refs_0_ = bf16[8,256,128]{2,1,0:T(8,128)(2,1)S(1)} async-done(((bf16[8,256,128]{2,1,0:T(8,128)(2,1)}), bf16[8,256,128]{2,1,0:T(8,128)(2,1)S(1)}, u32[]{:S(2)}, u32[]{:S(2)}) %all-to-all-start.4) | async-done | bytes 524320 | tf_op jit(solution)/shard_map/all_to_all | solution.py:347
  153.9 9.3 %shard_map.109 = (bf16[8,192,128]{2,1,0:T(8,128)(2,1)}, bf16[64,1024]{1,0:T(8,128)(2,1)S(1)}) custom-call(bf16[8,256,128]{2,1,0:T(8,128)(2,1)S(1)} %all-to-all-done.4.refs_0_, bf16[272,128]{1,0:T(8,128)(2,1)S(1)} %get-tuple-element.35.refs_1_.refs_4_), custom_call_target="tpu_custom_call" | custom-call | flops 12650000384 | tf_op jit(solution)/shard_map/pallas_call | solution.py:83
  163.2 4.2 %all-to-all-start.5 = ((bf16[8,192,128]{2,1,0:T(8,128)(2,1)}), bf16[8,192,128]{2,1,0:T(8,128)(2,1)S(1)}, u32[]{:S(2)}, u32[]{:S(2)}) async-start(bf16[8,192,128]{2,1,0:T(8,128)(2,1)} %get-tuple-element.40), calls=%async_computation.5 | async-start | bytes 786432 | tf_op jit(solution)/shard_map/all_to_all | solution.py:347
  167.5 9.7 %all-gather.9.cloned.1.call-done.refs_6_ = bf16[1024,512]{1,0:T(8,128)(2,1)} async-done(((bf16[128,512]{1,0:T(8,128)(2,1)}), bf16[1024,512]{1,0:T(8,128)(2,1)}) %all-gather.9.cloned.1.call-update) | async-done | bytes 1048592 | tf_op jit(solution)/shard_map/all_gather | solution.py:417
  177.2 4.1 %all-to-all-done.5.refs_0_ = bf16[8,192,128]{2,1,0:T(8,128)(2,1)S(1)} async-done(((bf16[8,192,128]{2,1,0:T(8,128)(2,1)}), bf16[8,192,128]{2,1,0:T(8,128)(2,1)S(1)}, u32[]{:S(2)}, u32[]{:S(2)}) %all-to-all-start.5) | async-done | bytes 393248 | tf_op jit(solution)/shard_map/all_to_all | solution.py:347
  181.3 1.2 copy-done.2
  182.5 2.0 shard_map.110
  184.5 29.3 %all_to_all.47.refs_0_ = bf16[16,80,128]{2,1,0:T(8,128)(2,1)S(1)} all-to-all(bf16[16,80,128]{2,1,0:T(8,128)(2,1)S(1)} %shard_map.110), channel_id=1, replica_groups=mesh['x'=4,'zh'=4,'zl'=4,'core'=2,'scene'=4] {'x','zh'}, dimensions={0} | all-to-all | bytes 655360 | tf_op jit(solution)/shard_map/all_to_all | solution.py:347
  213.8 1.3 shard_map.111
  215.1 9.8 %all-to-all-start.7 = ((bf16[8,64,128]{2,1,0:T(8,128)(2,1)}), bf16[8,64,128]{2,1,0:T(8,128)(2,1)S(1)}, u32[]{:S(2)}, u32[]{:S(2)}) async-start(bf16[8,64,128]{2,1,0:T(8,128)(2,1)} %bitcast.11), calls=%async_computation.7 | async-start | bytes 262144 | tf_op jit(solution)/shard_map/all_to_all | solution.py:347
  224.8 0.0 all-gather.11.cloned.1.call-start
  224.8 0.6 all-gather.11.cloned.1.call-update
  225.4 2.9 %collective-permute-start = (f32[4,512]{1,0:T(4,128)S(1)}, f32[4,512]{1,0:T(4,128)S(1)}, u32[]{:S(2)}, u32[]{:S(2)}) collective-permute-start(f32[4,512]{1,0:T(4,128)S(1)} %get-tuple-element.45), channel_id=1, source_target_pairs={{0,0},{4,64},{8,128},{12,192},{16,256},{20,320},{24,384},{28,448},... | collective-permute-start | bytes 24584 | tf_op jit(solution)/shard_map/ppermute | solution.py:464
  228.4 2.3 all-to-all-done.7.refs_1_
  230.7 0.0 copy-done.10
  230.7 9.3 %shard_map.112 = bf16[8,192,128]{2,1,0:T(8,128)(2,1)} custom-call(s32[18]{0:T(128)S(1)} %pad_add_fusion.refs_0_, bf16[8,64,128]{2,1,0:T(8,128)(2,1)S(1)} %all-to-all-done.7.refs_1_, bf16[1024,256]{1,0:T(8,128)(2,1)S(1)} %copy-done.10), custom_call_target="tpu_custom_call" | custom-call | flops 12650000384 | tf_op jit(solution)/shard_map/pallas_call | solution.py:83
  239.9 0.0 collective-permute-done
  239.9 4.3 %all-to-all-start.8 = ((bf16[8,192,128]{2,1,0:T(8,128)(2,1)}), bf16[8,192,128]{2,1,0:T(8,128)(2,1)S(1)}, u32[]{:S(2)}, u32[]{:S(2)}) async-start(bf16[8,192,128]{2,1,0:T(8,128)(2,1)} %shard_map.112), calls=%async_computation.8 | async-start | bytes 786432 | tf_op jit(solution)/shard_map/all_to_all | solution.py:347
  244.3 3.0 %collective-permute-start.1 = (f32[4,512]{1,0:T(4,128)S(1)}, f32[4,512]{1,0:T(4,128)S(1)}, u32[]{:S(2)}, u32[]{:S(2)}) collective-permute-start(f32[4,512]{1,0:T(4,128)S(1)} %collective-permute-done), channel_id=1, source_target_pairs={{0,1},{1,0},{2,3},{3,2},{4,5},{5,4},{6,7},{7,6},{8,9},{9,8},{10,11... | collective-permute-start | bytes 24584 | tf_op jit(solution)/shard_map/ppermute | solution.py:479
  247.3 1.8 collective-permute-done.1
  249.1 4.6 %collective-permute-start.2 = (f32[4,512]{1,0:T(4,128)S(1)}, f32[4,512]{1,0:T(4,128)S(1)}, u32[]{:S(2)}, u32[]{:S(2)}) collective-permute-start(f32[4,512]{1,0:T(4,128)S(1)} %add.24), channel_id=1, source_target_pairs={{0,2},{1,3},{2,0},{3,1},{4,6},{5,7},{6,4},{7,5},{8,10},{9,11},{10,... | collective-permute-start | bytes 24584 | tf_op jit(solution)/shard_map/ppermute | solution.py:479
  253.7 1.2 collective-permute-done.2
  254.9 0.6 add.25
  255.5 0.4 all-to-all-done.8.refs_0_
  256.0 0.0 copy-done.7
  256.0 1.4 copy-done.4
  257.4 1.4 shard_map.113
  (16 shorter events, 0.1 us)
Async XLA Ops:
  7.2 51.5 %all-gather.5.cloned.1.call-start = ((), (), s32[]{:S(2)}) async-start(), calls=%async_computation.9 | async-start | bytes 1327104 | tf_op jit(solution)/shard_map/all_gather | solution.py:374
  9.4 94.5 %all-gather.7.cloned.1.call-start = ((), (), s32[]{:S(2)}) async-start(), calls=%async_computation.10 | async-start | bytes 2949120 | tf_op jit(solution)/shard_map/all_gather | solution.py:388
  20.6 49.4 %copy-start.11 = (s32[1,16]{1,0:T(1,128)S(1)}, s32[1,16]{1,0:T(1,128)}, u32[]{:S(2)}) copy-start(s32[1,16]{1,0:T(1,128)} %param.11) | copy-start | bytes 196
  58.6 26.9 %all-to-all-start.1 = ((bf16[16,16,512]{2,1,0:T(8,128)(2,1)}), bf16[16,16,512]{2,1,0:T(8,128)(2,1)S(1)}, u32[]{:S(2)}, u32[]{:S(2)}) async-start(bf16[16,16,512]{2,1,0:T(8,128)(2,1)} %bitcast.5), calls=%async_computation.1 | async-start | bytes 524288 | tf_op jit(solution)/shard_map/all_to_all | solution.py:347
  70.1 1.3 copy-start.5
  76.9 0.8 copy-start.9
  85.5 18.4 %all-to-all-start.2 = ((bf16[8,64,128]{2,1,0:T(8,128)(2,1)}), bf16[8,64,128]{2,1,0:T(8,128)(2,1)S(1)}, u32[]{:S(2)}, u32[]{:S(2)}) async-start(bf16[8,64,128]{2,1,0:T(8,128)(2,1)} %get-tuple-element.33), calls=%async_computation.2 | async-start | bytes 262144 | tf_op jit(solution)/shard_map/all_to_all | solution.py:347
  98.1 5.8 %copy-start.6 = (bf16[1,128,512]{2,1,0:T(8,128)(2,1)S(1)}, bf16[1,128,512]{2,1,0:T(8,128)(2,1)}, u32[]{:S(2)}) copy-start(bf16[1,128,512]{2,1,0:T(8,128)(2,1)} %param.9) | copy-start | bytes 393220
  98.1 5.8 %copy-start.8 = (s32[1,128]{1,0:T(1,128)S(1)}, s32[1,128]{1,0:T(1,128)}, u32[]{:S(2)}) copy-start(s32[1,128]{1,0:T(1,128)} %refs_1_.1) | copy-start | bytes 1540
  103.9 1.7 copy-start
  105.6 22.9 %copy-start.1 = (bf16[1024,1280]{1,0:T(8,128)(2,1)S(1)}, bf16[1024,1280]{1,0:T(8,128)(2,1)}, u32[]{:S(2)}) copy-start(bf16[1024,1280]{1,0:T(8,128)(2,1)} %all-gather.7.cloned.1.call-done) | copy-start | bytes 7864324
  130.1 0.8 copy-start.3
  130.9 23.0 %all-to-all-start.4 = ((bf16[8,256,128]{2,1,0:T(8,128)(2,1)}), bf16[8,256,128]{2,1,0:T(8,128)(2,1)S(1)}, u32[]{:S(2)}, u32[]{:S(2)}) async-start(bf16[8,256,128]{2,1,0:T(8,128)(2,1)} %copy-done.3), calls=%async_computation.4 | async-start | bytes 1048576 | tf_op jit(solution)/shard_map/all_to_all | solution.py:347
  139.4 37.8 %all-gather.9.cloned.1.call-start = ((), (), s32[]{:S(2)}) async-start(), calls=%async_computation.11 | async-start | bytes 1179648 | tf_op jit(solution)/shard_map/all_gather | solution.py:417
  163.2 18.0 %all-to-all-start.5 = ((bf16[8,192,128]{2,1,0:T(8,128)(2,1)}), bf16[8,192,128]{2,1,0:T(8,128)(2,1)S(1)}, u32[]{:S(2)}, u32[]{:S(2)}) async-start(bf16[8,192,128]{2,1,0:T(8,128)(2,1)} %get-tuple-element.40), calls=%async_computation.5 | async-start | bytes 786432 | tf_op jit(solution)/shard_map/all_to_all | solution.py:347
  181.3 1.2 copy-start.2
  213.8 16.9 %copy-start.10 = (bf16[1024,256]{1,0:T(8,128)(2,1)S(1)}, bf16[1024,256]{1,0:T(8,128)(2,1)}, u32[]{:S(2)}) copy-start(bf16[1024,256]{1,0:T(8,128)(2,1)} %copy-done.9) | copy-start | bytes 1572868
  215.1 15.6 %all-to-all-start.7 = ((bf16[8,64,128]{2,1,0:T(8,128)(2,1)}), bf16[8,64,128]{2,1,0:T(8,128)(2,1)S(1)}, u32[]{:S(2)}, u32[]{:S(2)}) async-start(bf16[8,64,128]{2,1,0:T(8,128)(2,1)} %bitcast.11), calls=%async_computation.7 | async-start | bytes 262144 | tf_op jit(solution)/shard_map/all_to_all | solution.py:347
  224.8 30.7 %all-gather.11.cloned.1.call-start = ((), (), s32[]{:S(2)}) async-start(), calls=%async_computation.12 | async-start | bytes 1769472 | tf_op jit(solution)/shard_map/all_gather | solution.py:408
  225.4 14.5 %collective-permute-start = (f32[4,512]{1,0:T(4,128)S(1)}, f32[4,512]{1,0:T(4,128)S(1)}, u32[]{:S(2)}, u32[]{:S(2)}) collective-permute-start(f32[4,512]{1,0:T(4,128)S(1)} %get-tuple-element.45), channel_id=1, source_target_pairs={{0,0},{4,64},{8,128},{12,192},{16,256},{20,320},{24,384},{28,448},... | collective-permute-start | bytes 24584 | tf_op jit(solution)/shard_map/ppermute | solution.py:464
  230.7 25.3 %copy-start.7 = (bf16[1,128,512]{2,1,0:T(8,128)(2,1)S(1)}, bf16[1,128,512]{2,1,0:T(8,128)(2,1)}, u32[]{:S(2)}) copy-start(bf16[1,128,512]{2,1,0:T(8,128)(2,1)} %param.9) | copy-start | bytes 393220
  239.9 16.0 %all-to-all-start.8 = ((bf16[8,192,128]{2,1,0:T(8,128)(2,1)}), bf16[8,192,128]{2,1,0:T(8,128)(2,1)S(1)}, u32[]{:S(2)}, u32[]{:S(2)}) async-start(bf16[8,192,128]{2,1,0:T(8,128)(2,1)} %shard_map.112), calls=%async_computation.8 | async-start | bytes 786432 | tf_op jit(solution)/shard_map/all_to_all | solution.py:347
  244.3 4.8 %collective-permute-start.1 = (f32[4,512]{1,0:T(4,128)S(1)}, f32[4,512]{1,0:T(4,128)S(1)}, u32[]{:S(2)}, u32[]{:S(2)}) collective-permute-start(f32[4,512]{1,0:T(4,128)S(1)} %collective-permute-done), channel_id=1, source_target_pairs={{0,1},{1,0},{2,3},{3,2},{4,5},{5,4},{6,7},{7,6},{8,9},{9,8},{10,11... | collective-permute-start | bytes 24584 | tf_op jit(solution)/shard_map/ppermute | solution.py:479
  249.1 5.9 %collective-permute-start.2 = (f32[4,512]{1,0:T(4,128)S(1)}, f32[4,512]{1,0:T(4,128)S(1)}, u32[]{:S(2)}, u32[]{:S(2)}) collective-permute-start(f32[4,512]{1,0:T(4,128)S(1)} %add.24), channel_id=1, source_target_pairs={{0,2},{1,3},{2,0},{3,1},{4,6},{5,7},{6,4},{7,5},{8,10},{9,11},{10,... | collective-permute-start | bytes 24584 | tf_op jit(solution)/shard_map/ppermute | solution.py:479
  256.0 1.4 copy-start.4
Sparse Core Ops, SparseCore 0:
  10.1 46.1 all-gather.4
  58.4 36.3 all-gather.6
  142.3 34.8 all-gather.8
  227.5 24.3 all-gather.10

commit v5 on v4

--- a/solution.py
+++ b/solution.py
@@ -26,7 +26,7 @@
 NEGATIVE = -1e30
 SCALE = HEAD ** (-0.5)
 LOG2E = 1.4426950408889634
-QBLOCK = 1024
+QBLOCK = PATCH
 MICRO = 1_150_000_000
 
 F32 = jnp.float32
@@ -94,11 +94,25 @@
     )(*arrays)
 
 
+def masked_scores(keys, query, mask):
+    return jnp.where(mask, dot(keys, query, 1, 1) * (SCALE * LOG2E), NEGATIVE)
+
+
 def softmax_keys(keys, query, mask):
-    scores = dot(keys, query, 1, 1) * (SCALE * LOG2E)
-    scores = jnp.where(mask, scores, NEGATIVE)
-    weights = jnp.exp2(scores - jnp.max(scores, axis=0, keepdims=True))
-    return weights * (1.0 / jnp.sum(weights, axis=0, keepdims=True))
+    scores = masked_scores(keys, query, mask)
+    highest = jnp.max(scores, axis=0, keepdims=True)
+    weights = jnp.exp2(scores - highest)
+    inverse = 1.0 / jnp.sum(weights, axis=0, keepdims=True)
+    return weights * inverse, highest, inverse
+
+
+def split_exact(values):
+    parts = []
+    for _ in range(3):
+        part = values.astype(BF16).astype(F32)
+        parts.append(part)
+        values = values - part
+    return parts
 
 
 def key_mask(flags):
@@ -145,9 +159,12 @@
         weights[c] = jnp.concatenate(pieces, axis=1).astype(BF16)
 
 
-def forward_kernel(scal, gathered, weights, qkv, attended, plan, att):
+def forward_kernel(scal, gathered, own, one, two, three, qkv, attended, plan, att, weights):
     member = scal[0]
     limit = scal[2 + scal[1]]
+    for k, part in enumerate((own, one, two, three)):
+        place = jnp.bitwise_xor(scal[1] // 4, k)
+        weights[pl.ds(pl.multiple_of(place * ROWS, ROWS), ROWS), :] = part[...]
     w = weights[...]
     stride = ROWS + META
     source = gathered
@@ -191,14 +208,18 @@
         offset += here
     plan[PATCHES * SLOTS :, :] = jnp.concatenate([flags, flags], axis=0).astype(BF16)
     mask = iota((PATCH, QBLOCK), 0) < limit
+    norms = []
     for h in range(2):
         keys = qkv[:, h * HEAD : (h + 1) * HEAD]
         values_t = qkv[:, PAIR + h * HEAD : PAIR + (h + 1) * HEAD].astype(F32).T.astype(BF16)
         for n in range(PATCH // QBLOCK):
             span = slice(n * QBLOCK, (n + 1) * QBLOCK)
             query = qkv[span, 2 * PAIR + h * HEAD : 2 * PAIR + (h + 1) * HEAD]
-            probs = softmax_keys(keys, query, mask)
+            probs, highest, inverse = softmax_keys(keys, query, mask)
+            norms += split_exact(highest) + split_exact(inverse)
             att[h * HEAD : (h + 1) * HEAD, span] = dot(values_t, probs.astype(BF16))
+    norms.append(jnp.zeros((PAIR - 12, PATCH), F32))
+    qkv[:, 3 * PAIR :] = jnp.concatenate(norms, axis=0).T.astype(BF16)
     for b in range(MEMBERS):
         attended[b] = att[:, b * ROWS : (b + 1) * ROWS].astype(BF16)
 
@@ -240,7 +261,7 @@
         ).astype(BF16)
 
 
-def backward_body(qkv, grad_t, mask, send, attended, dq, dk, dv):
+def backward_body(qkv, grad_t, mask, norms, send, attended, dq, dk, dv):
     for h in range(2):
         low, high = h * HEAD, (h + 1) * HEAD
         keys = qkv[:, low:high]
@@ -251,7 +272,11 @@
             span = slice(n * QBLOCK, (n + 1) * QBLOCK)
             query = qkv[span, 2 * PAIR + low : 2 * PAIR + high]
             grad = grad_t[low:high, span]
-            probs = softmax_keys(keys, query, mask)
+            if norms is None:
+                probs, _, _ = softmax_keys(keys, query, mask)
+            else:
+                weights = jnp.exp2(masked_scores(keys, query, mask) - norms[2 * h][:, span])
+                probs = weights * norms[2 * h + 1][:, span]
             probs_low = probs.astype(BF16)
             grad_probs = dot(values, grad)
             row_dot = jnp.sum(probs * grad_probs, axis=0, keepdims=True)
@@ -281,14 +306,16 @@
         qkv[rows, ROWS:] = both
         grad_t[:, rows] = both.astype(F32).T[PAIR:, :].astype(BF16)
     mask = key_mask(plan[PATCHES * SLOTS : PATCHES * SLOTS + MEMBERS, :])
-    backward_body(qkv, grad_t, mask, send, attended, dq, dk, dv)
+    backward_body(qkv, grad_t, mask, None, send, attended, dq, dk, dv)
 
 
 def backward_z_kernel(scal, arrived, qkv, send, grad_t, dq, dk, dv):
     for b in range(MEMBERS):
         grad_t[:, b * ROWS : (b + 1) * ROWS] = arrived[b]
     mask = iota((PATCH, QBLOCK), 0) < scal[2 + scal[1]]
-    backward_body(qkv, grad_t, mask, send, None, dq, dk, dv)
+    kept = qkv[:, 3 * PAIR :].astype(F32).T
+    norms = [kept[k : k + 1, :] + kept[k + 1 : k + 2, :] + kept[k + 2 : k + 3, :] for k in (0, 3, 6, 9)]
+    backward_body(qkv, grad_t, mask, norms, send, None, dq, dk, dv)
 
 
 def input_grad(arrived, weights, rows, grads):
@@ -384,23 +411,23 @@
         ],
         axis=1,
     )
-    own = lax.all_gather(own, "x", axis=0, tiled=True)
     shared = lax.all_gather(weights[:, third:], ("x", "core"), axis=0, tiled=True)
     shared = shared.reshape(MEMBERS, ROWS, third + WIDTH)
     project_z = weights[:, :third]
 
     send_grads, own, gathered = lax.optimization_barrier((send_grads, own, gathered))
+    others = [lax.ppermute(own, "x", [(i, i ^ k) for i in range(4)]) for k in (1, 2, 3)]
     arrived_grads = exchange(send_grads.reshape(PATCHES, SLOTS, WIDTH), ACROSS)
 
     qkv_z, attended, plan = call(
         forward_kernel,
-        [scal, gathered, own],
+        [scal, gathered, own] + others,
         [
             ((PATCH, 4 * PAIR), BF16),
             ((MEMBERS, PAIR, ROWS), BF16),
             ((PATCHES * SLOTS + 2 * MEMBERS, ROWS), BF16),
         ],
-        [pltpu.VMEM((PAIR, PATCH), F32)],
+        [pltpu.VMEM((PAIR, PATCH), F32), pltpu.VMEM((WIDTH, 4 * PAIR), BF16)],
         micros=8,
     )
 

time: 268 us -> 276 us (1.030)
  starting transfers between devices: 60.8 us -> 67 us
  waiting for transfers between devices: 47.3 us -> 53.1 us
  blocking collectives: 99.8 us -> 95.7 us
    all_gather x1 -> x0, blocking collectives: 10.4 us -> none  [per_device(): own = lax.all_gather(own, 'x', axis=0, tiled=True)]
    ppermute x0 -> x3, starting transfers between devices: none -> 9.57 us  [per_device(): lax.ppermute(own, 'x', [(i, i ^ k) for i in range(4)])]
    all_to_all x6, waiting for transfers between devices: 33.3 us -> 24.7 us  [exchange(): return lax.all_to_all(value, axes, split_axis=0, concat_axis=0, tiled=True)]
    all_gather x1, waiting for transfers between devices: 0.01 us -> 7.71 us  [per_device(): gathered = lax.all_gather(mine, GROUP, axis=0, tiled=True)]
    ppermute x0 -> x3, waiting for transfers between devices: none -> 6.77 us  [per_device(): lax.ppermute(own, 'x', [(i, i ^ k) for i in range(4)])]
    all_to_all x3, blocking collectives: 62.8 us -> 69.1 us  [exchange(): return lax.all_to_all(value, axes, split_axis=0, concat_axis=0, tiled=True)]
    all_to_all x6, starting transfers between devices: 50.1 us -> 45.8 us  [exchange(): return lax.all_to_all(value, axes, split_axis=0, concat_axis=0, tiled=True)]
  transfers between devices with their start and end apart: 13 -> 16, of which waited for: 9 -> 11; matrix products, arithmetic and copies ran while one was open for 1% -> 1% of each run, Pallas kernels for 9% -> 9%
where the time goes in v5:
time: 276 us; the launch traced here: 273 us
  blocking collectives  95.7 us (35%)
  starting transfers between devices  67 us (24%)
  waiting for transfers between devices  53.1 us (19%)
  Pallas kernels  33.4 us (12%)
  between operations  13.9 us (5%)
  local copies, waits for them, and re-layouts  8.92 us (3%)
    all_to_all x3, blocking collectives, exchange(): return lax.all_to_all(value, axes, split_axis=0, concat_axis=0, tiled=True)  69.1 us
    all_to_all x6, starting transfers between devices, exchange(): return lax.all_to_all(value, axes, split_axis=0, concat_axis=0, tiled=True)  45.8 us
    pallas_call x10, Pallas kernels, call(): pl.pallas_call(body, out_shape=[jax.ShapeDtypeStruct(shape, dtype) for sh...  33.4 us
    all_gather x1, blocking collectives, per_device(): weights = lax.all_gather(weights, ('zh', 'zl'), axis=0, tiled=True)  26.6 us
    all_to_all x6, waiting for transfers between devices, exchange(): return lax.all_to_all(value, axes, split_axis=0, concat_axis=0, tiled=True)  24.7 us
    all_gather x1, waiting for transfers between devices, per_device(): all_grads_h = lax.all_gather(grads_h, GROUP, axis=0, tiled=True)  9.66 us
    ppermute x3, starting transfers between devices, per_device(): lax.ppermute(own, 'x', [(i, i ^ k) for i in range(4)])  9.57 us
    ppermute x2, starting transfers between devices, per_device(): lax.ppermute(term, 'scene', [(i, i ^ k) for i in range(SCENES)])  7.71 us
  transfers between devices with their start and end apart: 16, of which 11 were waited for; matrix products, arithmetic and copies ran while one was open for 1% of the time, Pallas kernels for 9%

profile of v5, /device:TPU:1, one launch (start us, length us, event | category | flops | bytes accessed | tf_op | source)
XLA Modules:
  0.0 272.8 jit_solution(5197264385224014924)
XLA Ops:
  7.2 0.0 all-gather.5.cloned.1.call-start
  7.2 2.1 shard_map.104
  9.4 0.0 copy-start.11
  9.4 0.0 all-gather.5.cloned.1.call-update
  9.4 0.0 all-gather.7.cloned.1.call-start
  9.4 11.2 %all_to_all.45 = bf16[2,4,2048]{2,1,0:T(4,128)(2,1)S(1)} all-to-all(bf16[2,4,2048]{2,1,0:T(4,128)(2,1)} %get-tuple-element.27), channel_id=1, replica_groups=mesh['x'=4,'zh'=4,'zl'=4,'core'=2,'scene'=4] {'core'}, dimensions={0} | all-to-all | bytes 65536 | tf_op jit(solution)/shard_map/all_to_all | solution.py:374
  20.6 26.6 %all_gather.15 = bf16[128,2048]{1,0:T(8,128)(2,1)S(1)} all-gather(bf16[8,2048]{1,0:T(8,128)(2,1)S(1)} %reshape.31), channel_id=1, replica_groups=mesh['x'=4,'zh'=4,'zl'=4,'core'=2,'scene'=4] {'zh','zl'}, dimensions={0}, use_global_device_ids=true | all-gather | bytes 557056 | tf_op jit(solution)/shard_map/all_gather | solution.py:403
  47.2 0.8 slice.9
  48.0 0.0 all-gather.7.cloned.1.call-update
  48.0 0.1 pad.2.clone
  48.1 0.1 constant_dynamic-slice_fusion
  48.2 7.7 %all-gather.5.cloned.1.call-done.refs_1_ = bf16[1152,512]{1,0:T(8,128)(2,1)} async-done(((bf16[144,512]{1,0:T(8,128)(2,1)}), bf16[1152,512]{1,0:T(8,128)(2,1)}) %all-gather.5.cloned.1.call-update) | async-done | bytes 1179664 | tf_op jit(solution)/shard_map/all_gather | solution.py:401
  55.9 13.5 %all-to-all-start.1 = ((bf16[16,16,512]{2,1,0:T(8,128)(2,1)}), bf16[16,16,512]{2,1,0:T(8,128)(2,1)S(1)}, u32[]{:S(2)}, u32[]{:S(2)}) async-start(bf16[16,16,512]{2,1,0:T(8,128)(2,1)} %bitcast.5), calls=%async_computation.1 | async-start | bytes 524288 | tf_op jit(solution)/shard_map/all_to_all | solution.py:374
  69.4 0.7 slice.8
  70.1 3.3 %collective-permute-start = (bf16[128,256]{1,0:T(8,128)(2,1)S(1)}, bf16[128,256]{1,0:T(8,128)(2,1)S(1)}, u32[]{:S(2)}, u32[]{:S(2)}) collective-permute-start(bf16[128,256]{1,0:T(8,128)(2,1)S(1)} %maximum_maximum_fusion.refs_2_), channel_id=1, source_target_pairs={{0,128},{128,0},{256,384},{384,256},{1,129},{129,1},{257,385},{385... | collective-permute-start | bytes 196616 | tf_op jit(solution)/shard_map/ppermute | solution.py:419
  73.4 4.3 %collective-permute-start.1 = (bf16[128,256]{1,0:T(8,128)(2,1)S(1)}, bf16[128,256]{1,0:T(8,128)(2,1)S(1)}, u32[]{:S(2)}, u32[]{:S(2)}) collective-permute-start(bf16[128,256]{1,0:T(8,128)(2,1)S(1)} %maximum_maximum_fusion.refs_2_), channel_id=1, source_target_pairs={{0,256},{128,384},{256,0},{384,128},{1,257},{129,385},{257,1},{385... | collective-permute-start | bytes 196616 | tf_op jit(solution)/shard_map/ppermute | solution.py:419
  77.7 2.0 collective-permute-start.2
  79.7 0.1 pad_add_fusion.refs_0_
  79.8 0.0 collective-permute-done.refs_3_
  79.8 1.3 collective-permute-done.1.refs_4_
  81.1 5.5 %collective-permute-done.2.refs_5_ = bf16[128,256]{1,0:T(8,128)(2,1)S(1)} collective-permute-done((bf16[128,256]{1,0:T(8,128)(2,1)S(1)}, bf16[128,256]{1,0:T(8,128)(2,1)S(1)}, u32[]{:S(2)}, u32[]{:S(2)}) %collective-permute-start.2) | collective-permute-done | bytes 65568 | tf_op jit(solution)/shard_map/ppermute | solution.py:419
  86.6 1.3 copy-done.5
  87.8 5.7 %shard_map.105 = (bf16[1024,256]{1,0:T(8,128)(2,1)S(1)}, bf16[8,64,128]{2,1,0:T(8,128)(2,1)}, bf16[272,128]{1,0:T(8,128)(2,1)S(1)}) custom-call(s32[18]{0:T(128)S(1)} %pad_add_fusion.refs_0_, bf16[1152,512]{1,0:T(8,128)(2,1)S(1)} %copy-done.5, bf16[128,256]{1,0:T(8,128)(2,1)S(1)} %maximum_maximum_fusion.refs_2_, ...), custom_call_target="tpu_custom_call" | custom-call | flops 9200000000 | tf_op jit(solution)/shard_map/pallas_call | solution.py:83
  93.6 0.8 copy-done.9
  94.4 0.0 all-to-all-done.1
  94.4 6.4 %all-to-all-start.2 = ((bf16[8,64,128]{2,1,0:T(8,128)(2,1)}), bf16[8,64,128]{2,1,0:T(8,128)(2,1)S(1)}, u32[]{:S(2)}, u32[]{:S(2)}) async-start(bf16[8,64,128]{2,1,0:T(8,128)(2,1)} %get-tuple-element.33), calls=%async_computation.2 | async-start | bytes 262144 | tf_op jit(solution)/shard_map/all_to_all | solution.py:374
  100.8 0.9 shard_map.106.refs_4_.refs_3_
  101.7 5.0 %all-to-all-done.2 = bf16[8,64,128]{2,1,0:T(8,128)(2,1)S(1)} async-done(((bf16[8,64,128]{2,1,0:T(8,128)(2,1)}), bf16[8,64,128]{2,1,0:T(8,128)(2,1)S(1)}, u32[]{:S(2)}, u32[]{:S(2)}) %all-to-all-start.2) | async-done | bytes 131104 | tf_op jit(solution)/shard_map/all_to_all | solution.py:374
  106.7 0.0 copy-done.6
  106.7 1.7 copy-done
  108.4 0.5 shard_map.107
  108.9 29.0 %all_to_all.46 = bf16[16,16,512]{2,1,0:T(8,128)(2,1)S(1)} all-to-all(bf16[16,16,512]{2,1,0:T(8,128)(2,1)S(1)} %bitcast.21), channel_id=1, replica_groups=mesh['x'=4,'zh'=4,'zl'=4,'core'=2,'scene'=4] {'x','zh'}, dimensions={0} | all-to-all | bytes 524288 | tf_op jit(solution)/shard_map/all_to_all | solution.py:374
  137.9 1.6 shard_map.108
  139.5 0.0 copy-start.3
  139.6 0.8 copy-done.3
  140.3 8.4 %all-to-all-start.4 = ((bf16[8,256,128]{2,1,0:T(8,128)(2,1)}), bf16[8,256,128]{2,1,0:T(8,128)(2,1)S(1)}, u32[]{:S(2)}, u32[]{:S(2)}) async-start(bf16[8,256,128]{2,1,0:T(8,128)(2,1)} %copy-done.3), calls=%async_computation.4 | async-start | bytes 1048576 | tf_op jit(solution)/shard_map/all_to_all | solution.py:374
  148.7 0.0 all-gather.9.cloned.1.call-start
  148.7 0.7 all-gather.9.cloned.1.call-update
  149.4 13.8 %all-to-all-done.4.refs_0_ = bf16[8,256,128]{2,1,0:T(8,128)(2,1)S(1)} async-done(((bf16[8,256,128]{2,1,0:T(8,128)(2,1)}), bf16[8,256,128]{2,1,0:T(8,128)(2,1)S(1)}, u32[]{:S(2)}, u32[]{:S(2)}) %all-to-all-start.4) | async-done | bytes 524320 | tf_op jit(solution)/shard_map/all_to_all | solution.py:374
  163.2 9.3 %shard_map.109 = (bf16[8,192,128]{2,1,0:T(8,128)(2,1)}, bf16[64,1024]{1,0:T(8,128)(2,1)S(1)}) custom-call(bf16[8,256,128]{2,1,0:T(8,128)(2,1)S(1)} %all-to-all-done.4.refs_0_, bf16[272,128]{1,0:T(8,128)(2,1)S(1)} %get-tuple-element.35.refs_1_.refs_4_), custom_call_target="tpu_custom_call" | custom-call | flops 12650000384 | tf_op jit(solution)/shard_map/pallas_call | solution.py:83
  172.5 4.2 %all-to-all-start.5 = ((bf16[8,192,128]{2,1,0:T(8,128)(2,1)}), bf16[8,192,128]{2,1,0:T(8,128)(2,1)S(1)}, u32[]{:S(2)}, u32[]{:S(2)}) async-start(bf16[8,192,128]{2,1,0:T(8,128)(2,1)} %get-tuple-element.40), calls=%async_computation.5 | async-start | bytes 786432 | tf_op jit(solution)/shard_map/all_to_all | solution.py:374
  176.8 9.7 %all-gather.9.cloned.1.call-done.refs_6_ = bf16[1024,512]{1,0:T(8,128)(2,1)} async-done(((bf16[128,512]{1,0:T(8,128)(2,1)}), bf16[1024,512]{1,0:T(8,128)(2,1)}) %all-gather.9.cloned.1.call-update) | async-done | bytes 1048592 | tf_op jit(solution)/shard_map/all_gather | solution.py:444
  186.4 4.2 %all-to-all-done.5.refs_0_ = bf16[8,192,128]{2,1,0:T(8,128)(2,1)S(1)} async-done(((bf16[8,192,128]{2,1,0:T(8,128)(2,1)}), bf16[8,192,128]{2,1,0:T(8,128)(2,1)S(1)}, u32[]{:S(2)}, u32[]{:S(2)}) %all-to-all-start.5) | async-done | bytes 393248 | tf_op jit(solution)/shard_map/all_to_all | solution.py:374
  190.6 1.2 copy-done.2
  191.9 2.0 shard_map.110
  193.9 28.9 %all_to_all.47.refs_0_ = bf16[16,80,128]{2,1,0:T(8,128)(2,1)S(1)} all-to-all(bf16[16,80,128]{2,1,0:T(8,128)(2,1)S(1)} %shard_map.110), channel_id=1, replica_groups=mesh['x'=4,'zh'=4,'zl'=4,'core'=2,'scene'=4] {'x','zh'}, dimensions={0} | all-to-all | bytes 655360 | tf_op jit(solution)/shard_map/all_to_all | solution.py:374
  222.8 1.3 shard_map.111
  224.1 9.0 %all-to-all-start.7 = ((bf16[8,64,128]{2,1,0:T(8,128)(2,1)}), bf16[8,64,128]{2,1,0:T(8,128)(2,1)S(1)}, u32[]{:S(2)}, u32[]{:S(2)}) async-start(bf16[8,64,128]{2,1,0:T(8,128)(2,1)} %bitcast.11), calls=%async_computation.7 | async-start | bytes 262144 | tf_op jit(solution)/shard_map/all_to_all | solution.py:374
  233.1 0.0 all-gather.11.cloned.1.call-start
  233.1 0.6 all-gather.11.cloned.1.call-update
  233.6 3.9 %collective-permute-start.3 = (f32[4,512]{1,0:T(4,128)S(1)}, f32[4,512]{1,0:T(4,128)S(1)}, u32[]{:S(2)}, u32[]{:S(2)}) collective-permute-start(f32[4,512]{1,0:T(4,128)S(1)} %get-tuple-element.45), channel_id=1, source_target_pairs={{0,0},{4,64},{8,128},{12,192},{16,256},{20,320},{24,384},{28,448},... | collective-permute-start | bytes 24584 | tf_op jit(solution)/shard_map/ppermute | solution.py:491
  237.5 1.3 all-to-all-done.7.refs_1_
  238.9 0.0 copy-done.10
  238.9 8.5 %shard_map.112 = bf16[8,192,128]{2,1,0:T(8,128)(2,1)} custom-call(s32[18]{0:T(128)S(1)} %pad_add_fusion.refs_0_, bf16[8,64,128]{2,1,0:T(8,128)(2,1)S(1)} %all-to-all-done.7.refs_1_, bf16[1024,256]{1,0:T(8,128)(2,1)S(1)} %copy-done.10), custom_call_target="tpu_custom_call" | custom-call | flops 12650000384 | tf_op jit(solution)/shard_map/pallas_call | solution.py:83
  247.4 0.0 collective-permute-done.3
  247.4 4.3 %all-to-all-start.8 = ((bf16[8,192,128]{2,1,0:T(8,128)(2,1)}), bf16[8,192,128]{2,1,0:T(8,128)(2,1)S(1)}, u32[]{:S(2)}, u32[]{:S(2)}) async-start(bf16[8,192,128]{2,1,0:T(8,128)(2,1)} %shard_map.112), calls=%async_computation.8 | async-start | bytes 786432 | tf_op jit(solution)/shard_map/all_to_all | solution.py:374
  251.7 3.1 %collective-permute-start.4 = (f32[4,512]{1,0:T(4,128)S(1)}, f32[4,512]{1,0:T(4,128)S(1)}, u32[]{:S(2)}, u32[]{:S(2)}) collective-permute-start(f32[4,512]{1,0:T(4,128)S(1)} %collective-permute-done.3), channel_id=1, source_target_pairs={{0,1},{1,0},{2,3},{3,2},{4,5},{5,4},{6,7},{7,6},{8,9},{9,8},{10,11... | collective-permute-start | bytes 24584 | tf_op jit(solution)/shard_map/ppermute | solution.py:506
  254.8 1.7 collective-permute-done.4
  256.5 4.6 %collective-permute-start.5 = (f32[4,512]{1,0:T(4,128)S(1)}, f32[4,512]{1,0:T(4,128)S(1)}, u32[]{:S(2)}, u32[]{:S(2)}) collective-permute-start(f32[4,512]{1,0:T(4,128)S(1)} %add.24), channel_id=1, source_target_pairs={{0,2},{1,3},{2,0},{3,1},{4,6},{5,7},{6,4},{7,5},{8,10},{9,11},{10,... | collective-permute-start | bytes 24584 | tf_op jit(solution)/shard_map/ppermute | solution.py:506
  261.1 1.3 collective-permute-done.5
  262.4 0.6 add.25
  263.0 0.4 all-to-all-done.8.refs_0_
  263.4 1.4 copy-done.4
  264.8 1.4 shard_map.113
  (21 shorter events, 0.1 us)
Async XLA Ops:
  7.2 48.8 %all-gather.5.cloned.1.call-start = ((), (), s32[]{:S(2)}) async-start(), calls=%async_computation.9 | async-start | bytes 1327104 | tf_op jit(solution)/shard_map/all_gather | solution.py:401
  9.4 70.4 %copy-start.11 = (s32[1,16]{1,0:T(1,128)S(1)}, s32[1,16]{1,0:T(1,128)}, u32[]{:S(2)}) copy-start(s32[1,16]{1,0:T(1,128)} %param.11) | copy-start | bytes 196
  9.4 97.3 %all-gather.7.cloned.1.call-start = ((), (), s32[]{:S(2)}) async-start(), calls=%async_computation.10 | async-start | bytes 2949120 | tf_op jit(solution)/shard_map/all_gather | solution.py:414
  55.9 38.4 %all-to-all-start.1 = ((bf16[16,16,512]{2,1,0:T(8,128)(2,1)}), bf16[16,16,512]{2,1,0:T(8,128)(2,1)S(1)}, u32[]{:S(2)}, u32[]{:S(2)}) async-start(bf16[16,16,512]{2,1,0:T(8,128)(2,1)} %bitcast.5), calls=%async_computation.1 | async-start | bytes 524288 | tf_op jit(solution)/shard_map/all_to_all | solution.py:374
  70.1 9.7 %collective-permute-start = (bf16[128,256]{1,0:T(8,128)(2,1)S(1)}, bf16[128,256]{1,0:T(8,128)(2,1)S(1)}, u32[]{:S(2)}, u32[]{:S(2)}) collective-permute-start(bf16[128,256]{1,0:T(8,128)(2,1)S(1)} %maximum_maximum_fusion.refs_2_), channel_id=1, source_target_pairs={{0,128},{128,0},{256,384},{384,256},{1,129},{129,1},{257,385},{385... | collective-permute-start | bytes 196616 | tf_op jit(solution)/shard_map/ppermute | solution.py:419
  73.4 7.7 %collective-permute-start.1 = (bf16[128,256]{1,0:T(8,128)(2,1)S(1)}, bf16[128,256]{1,0:T(8,128)(2,1)S(1)}, u32[]{:S(2)}, u32[]{:S(2)}) collective-permute-start(bf16[128,256]{1,0:T(8,128)(2,1)S(1)} %maximum_maximum_fusion.refs_2_), channel_id=1, source_target_pairs={{0,256},{128,384},{256,0},{384,128},{1,257},{129,385},{257,1},{385... | collective-permute-start | bytes 196616 | tf_op jit(solution)/shard_map/ppermute | solution.py:419
  77.7 8.9 %collective-permute-start.2 = (bf16[128,256]{1,0:T(8,128)(2,1)S(1)}, bf16[128,256]{1,0:T(8,128)(2,1)S(1)}, u32[]{:S(2)}, u32[]{:S(2)}) collective-permute-start(bf16[128,256]{1,0:T(8,128)(2,1)S(1)} %maximum_maximum_fusion.refs_2_), channel_id=1, source_target_pairs={{0,384},{128,256},{256,128},{384,0},{1,385},{129,257},{257,129},{3... | collective-permute-start | bytes 196616 | tf_op jit(solution)/shard_map/ppermute | solution.py:419
  86.6 1.3 copy-start.5
  93.6 0.8 copy-start.9
  94.4 12.3 %all-to-all-start.2 = ((bf16[8,64,128]{2,1,0:T(8,128)(2,1)}), bf16[8,64,128]{2,1,0:T(8,128)(2,1)S(1)}, u32[]{:S(2)}, u32[]{:S(2)}) async-start(bf16[8,64,128]{2,1,0:T(8,128)(2,1)} %get-tuple-element.33), calls=%async_computation.2 | async-start | bytes 262144 | tf_op jit(solution)/shard_map/all_to_all | solution.py:374
  100.8 5.8 %copy-start.6 = (bf16[1,128,512]{2,1,0:T(8,128)(2,1)S(1)}, bf16[1,128,512]{2,1,0:T(8,128)(2,1)}, u32[]{:S(2)}) copy-start(bf16[1,128,512]{2,1,0:T(8,128)(2,1)} %param.9) | copy-start | bytes 393220
  100.8 5.8 %copy-start.8 = (s32[1,128]{1,0:T(1,128)S(1)}, s32[1,128]{1,0:T(1,128)}, u32[]{:S(2)}) copy-start(s32[1,128]{1,0:T(1,128)} %refs_1_.1) | copy-start | bytes 1540
  106.7 1.7 copy-start
  108.4 29.5 %copy-start.1 = (bf16[1024,1280]{1,0:T(8,128)(2,1)S(1)}, bf16[1024,1280]{1,0:T(8,128)(2,1)}, u32[]{:S(2)}) copy-start(bf16[1024,1280]{1,0:T(8,128)(2,1)} %all-gather.7.cloned.1.call-done) | copy-start | bytes 7864324
  139.5 0.8 copy-start.3
  140.3 22.8 %all-to-all-start.4 = ((bf16[8,256,128]{2,1,0:T(8,128)(2,1)}), bf16[8,256,128]{2,1,0:T(8,128)(2,1)S(1)}, u32[]{:S(2)}, u32[]{:S(2)}) async-start(bf16[8,256,128]{2,1,0:T(8,128)(2,1)} %copy-done.3), calls=%async_computation.4 | async-start | bytes 1048576 | tf_op jit(solution)/shard_map/all_to_all | solution.py:374
  148.7 37.7 %all-gather.9.cloned.1.call-start = ((), (), s32[]{:S(2)}) async-start(), calls=%async_computation.11 | async-start | bytes 1179648 | tf_op jit(solution)/shard_map/all_gather | solution.py:444
  172.5 18.1 %all-to-all-start.5 = ((bf16[8,192,128]{2,1,0:T(8,128)(2,1)}), bf16[8,192,128]{2,1,0:T(8,128)(2,1)S(1)}, u32[]{:S(2)}, u32[]{:S(2)}) async-start(bf16[8,192,128]{2,1,0:T(8,128)(2,1)} %get-tuple-element.40), calls=%async_computation.5 | async-start | bytes 786432 | tf_op jit(solution)/shard_map/all_to_all | solution.py:374
  190.6 1.2 copy-start.2
  222.8 16.1 %copy-start.10 = (bf16[1024,256]{1,0:T(8,128)(2,1)S(1)}, bf16[1024,256]{1,0:T(8,128)(2,1)}, u32[]{:S(2)}) copy-start(bf16[1024,256]{1,0:T(8,128)(2,1)} %copy-done.9) | copy-start | bytes 1572868
  224.1 14.8 %all-to-all-start.7 = ((bf16[8,64,128]{2,1,0:T(8,128)(2,1)}), bf16[8,64,128]{2,1,0:T(8,128)(2,1)S(1)}, u32[]{:S(2)}, u32[]{:S(2)}) async-start(bf16[8,64,128]{2,1,0:T(8,128)(2,1)} %bitcast.11), calls=%async_computation.7 | async-start | bytes 262144 | tf_op jit(solution)/shard_map/all_to_all | solution.py:374
  233.1 29.9 %all-gather.11.cloned.1.call-start = ((), (), s32[]{:S(2)}) async-start(), calls=%async_computation.12 | async-start | bytes 1769472 | tf_op jit(solution)/shard_map/all_gather | solution.py:435
  233.6 13.8 %collective-permute-start.3 = (f32[4,512]{1,0:T(4,128)S(1)}, f32[4,512]{1,0:T(4,128)S(1)}, u32[]{:S(2)}, u32[]{:S(2)}) collective-permute-start(f32[4,512]{1,0:T(4,128)S(1)} %get-tuple-element.45), channel_id=1, source_target_pairs={{0,0},{4,64},{8,128},{12,192},{16,256},{20,320},{24,384},{28,448},... | collective-permute-start | bytes 24584 | tf_op jit(solution)/shard_map/ppermute | solution.py:491
  238.9 24.5 %copy-start.7 = (bf16[1,128,512]{2,1,0:T(8,128)(2,1)S(1)}, bf16[1,128,512]{2,1,0:T(8,128)(2,1)}, u32[]{:S(2)}) copy-start(bf16[1,128,512]{2,1,0:T(8,128)(2,1)} %param.9) | copy-start | bytes 393220
  247.4 16.0 %all-to-all-start.8 = ((bf16[8,192,128]{2,1,0:T(8,128)(2,1)}), bf16[8,192,128]{2,1,0:T(8,128)(2,1)S(1)}, u32[]{:S(2)}, u32[]{:S(2)}) async-start(bf16[8,192,128]{2,1,0:T(8,128)(2,1)} %shard_map.112), calls=%async_computation.8 | async-start | bytes 786432 | tf_op jit(solution)/shard_map/all_to_all | solution.py:374
  251.7 4.8 %collective-permute-start.4 = (f32[4,512]{1,0:T(4,128)S(1)}, f32[4,512]{1,0:T(4,128)S(1)}, u32[]{:S(2)}, u32[]{:S(2)}) collective-permute-start(f32[4,512]{1,0:T(4,128)S(1)} %collective-permute-done.3), channel_id=1, source_target_pairs={{0,1},{1,0},{2,3},{3,2},{4,5},{5,4},{6,7},{7,6},{8,9},{9,8},{10,11... | collective-permute-start | bytes 24584 | tf_op jit(solution)/shard_map/ppermute | solution.py:506
  256.5 5.9 %collective-permute-start.5 = (f32[4,512]{1,0:T(4,128)S(1)}, f32[4,512]{1,0:T(4,128)S(1)}, u32[]{:S(2)}, u32[]{:S(2)}) collective-permute-start(f32[4,512]{1,0:T(4,128)S(1)} %add.24), channel_id=1, source_target_pairs={{0,2},{1,3},{2,0},{3,1},{4,6},{5,7},{6,4},{7,5},{8,10},{9,11},{10,... | collective-permute-start | bytes 24584 | tf_op jit(solution)/shard_map/ppermute | solution.py:506
  263.4 1.4 copy-start.4
Sparse Core Ops, SparseCore 0:
  10.1 45.8 all-gather.4
  58.1 38.7 all-gather.6
  151.6 34.7 all-gather.8
  235.7 25.2 all-gather.10
